TPU v7x, 256 devices: a whole 4x4x8 slice. The times are simulated.
256 devices in a mesh: ctx: 32 (over z, x), head: 8 (over y, core).
Axes of the slice: x: 4, y: 4, z: 8, core: 2. Of those that a mesh axis runs over, the one named last changes fastest.
Arguments:
- queries: bfloat16 [2048, 16, 128], P('ctx', 'head'), may hold values from -9 to 9
- cache_keys: bfloat16 [65536, 128], P('ctx'), may hold values from -15 to 15
- cache_values: bfloat16 [65536, 128], P('ctx'), may hold values from -6 to 6
- page_table: int32 [32, 4], P('ctx'), may hold values from 0 to 3, each once within a row
- page_count: int32 [32], P('ctx'), may hold values from 1 to 4, as said below
- new_kv: bfloat16 [2048, 2, 128], P(('ctx', 'head')), may hold values from -15 to 15
- new_owner: int32 [2048], replicated, may hold values from 0 to 31, as said below
- new_offset: int32 [2048], replicated, may hold values from 0 to 127
Outputs:
- attended: bfloat16 [2048, 16, 128], P('ctx', 'head')
- appended: bfloat16 [4096, 2, 128], P('ctx')
Inputs may be any that keep to these rules, and one draw needn't show every extreme that they name: `page_count`: some store has all 4 pages live. `page_table`: each row names every page once. `new_owner`: no two new tokens share a pair of owner and offset; some store's 128 rows are all taken.
All inputs are finite; a program needn't handle non-finite values.
Results may differ from a plain program's by a relative error of at most 0.0028.
Values may be sent and summed in bfloat16 or wider, within the bound.
No kernel may reach another device: no remote copies, remote signals or barrier semaphores. Data moves between devices by JAX's collectives and lax.ppermute only.
A program may use at most 64 MiB of HBM per device.

v0:
```python
import math

import jax
import jax.numpy as jnp
from jax import lax
from jax.sharding import PartitionSpec as P


def passed_along(value, axis, steps):
    count = lax.axis_size(axis)
    pairs = [(source, (source + steps) % count) for source in range(count)]
    return lax.ppermute(value, axis, pairs)


def cache_part(query_rows, cache_keys, cache_values, table_row, live_count, scaling):
    page_rows = cache_keys.shape[0] // table_row.shape[0]
    count_rows = query_rows.shape[0]

    def take_page(number, carry):
        maxima, totals, summed = carry
        page_index = lax.dynamic_index_in_dim(table_row, number, 0, keepdims=False)
        key_block = lax.dynamic_slice_in_dim(cache_keys, page_index * page_rows, page_rows, 0)
        value_block = lax.dynamic_slice_in_dim(cache_values, page_index * page_rows, page_rows, 0)
        scores = (
            lax.dot_general(
                query_rows, key_block, (((1,), (1,)), ((), ())), preferred_element_type=jnp.float32
            )
            * scaling
        )
        updated = jnp.maximum(maxima, jnp.max(scores, axis=1))
        factor = jnp.exp(maxima - updated)
        weights = jnp.exp(scores - updated[:, None])
        totals = totals * factor + jnp.sum(weights, axis=1)
        summed = summed * factor[:, None] + jnp.dot(
            weights.astype(jnp.bfloat16), value_block, preferred_element_type=jnp.float32
        )
        return (updated, totals, summed)

    initial = (
        jnp.full((count_rows,), -1e30, jnp.float32),
        jnp.zeros((count_rows,), jnp.float32),
        jnp.zeros((count_rows, query_rows.shape[1]), jnp.float32),
    )
    return lax.fori_loop(0, live_count, take_page, initial)


def join_partials(first, second):
    combined = jnp.maximum(first[0], second[0])
    factor_one = jnp.exp(first[0] - combined)
    factor_two = jnp.exp(second[0] - combined)
    totals = first[1] * factor_one + second[1] * factor_two
    summed = first[2] * factor_one[..., None] + second[2] * factor_two[..., None]
    return (combined, totals, summed)


def shards(
    queries, cache_keys, cache_values, page_table, page_count, new_kv, new_owner, new_offset
):
    tok_dev, head_dev, head_size = queries.shape
    stores = lax.axis_size("ctx")
    own_store = lax.axis_index("ctx")
    scaling = 1.0 / math.sqrt(head_size)
    table_row = page_table[0]
    live_count = page_count[0]

    def local_part(query_rows):
        return cache_part(query_rows, cache_keys, cache_values, table_row, live_count, scaling)

    def travel_step(number, carry):
        visiting, maxima, totals, summed = carry
        found = local_part(visiting.reshape(tok_dev * head_dev, head_size))
        found = (
            found[0].reshape(tok_dev, head_dev),
            found[1].reshape(tok_dev, head_dev),
            found[2].reshape(tok_dev, head_dev, head_size),
        )
        maxima, totals, summed = join_partials((maxima, totals, summed), found)
        visiting = passed_along(visiting, "ctx", 1)
        summed, maxima, totals = passed_along((summed, maxima, totals), "ctx", 1)
        return (visiting, maxima, totals, summed)

    initial = (
        queries,
        jnp.full((tok_dev, head_dev), -1e30, jnp.float32),
        jnp.zeros((tok_dev, head_dev), jnp.float32),
        jnp.zeros((tok_dev, head_dev, head_size), jnp.float32),
    )
    visited, cache_max, cache_total, cache_sum = lax.fori_loop(0, stores, travel_step, initial)
    new_rows = lax.all_gather(new_kv, ("ctx", "head"), axis=0, tiled=True)
    query_rows = queries.reshape(tok_dev * head_dev, head_size)
    scores = (
        lax.dot_general(
            query_rows, new_rows[:, 0], (((1,), (1,)), ((), ())), preferred_element_type=jnp.float32
        )
        * scaling
    )
    positions = own_store * tok_dev + jnp.arange(tok_dev * head_dev, dtype=jnp.int32) // head_dev
    visible = jnp.arange(new_rows.shape[0], dtype=jnp.int32)[None, :] <= positions[:, None]
    scores = jnp.where(visible, scores, jnp.float32(-1e30))
    self_max = jnp.max(scores, axis=1)
    weights = jnp.exp(scores - self_max[:, None])
    self_total = jnp.sum(weights, axis=1)
    self_sum = jnp.dot(
        weights.astype(jnp.bfloat16), new_rows[:, 1], preferred_element_type=jnp.float32
    )
    self_part = (
        self_max.reshape(tok_dev, head_dev),
        self_total.reshape(tok_dev, head_dev),
        self_sum.reshape(tok_dev, head_dev, head_size),
    )
    maxima, totals, summed = join_partials((cache_max, cache_total, cache_sum), self_part)
    attended = (summed / totals[..., None]).astype(jnp.bfloat16)
    append_rows = 2 * tok_dev
    target = jnp.where(new_owner == own_store, new_offset, append_rows)
    appended = (
        jnp.zeros((append_rows, 2, head_size), jnp.bfloat16).at[target].set(new_rows, mode="drop")
    )
    return (attended, appended)


def solution(mesh):
    in_specs = (
        P("ctx", "head", None),
        P("ctx", None),
        P("ctx", None),
        P("ctx", None),
        P("ctx"),
        P(("ctx", "head"), None, None),
        P(),
        P(),
    )
    out_specs = (P("ctx", "head", None), P("ctx", None, None))
    return jax.shard_map(shards, mesh=mesh, in_specs=in_specs, out_specs=out_specs, check_vma=False)
```

profile of v0, /device:TPU:8, one launch (start us, length us, event | category | flops | bytes accessed | tf_op | source)
XLA Modules:
  0.0 972.5 jit_solution(9819336521950343187)
XLA Ops:
  9.3 100.0 %all-gather.2.cloned.1.call-done = bf16[2048,2,128]{2,0,1:T(8,128)(2,1)} async-done(((bf16[8,2,128]{2,0,1:T(8,128)(2,1)}), bf16[2048,2,128]{2,0,1:T(8,128)(2,1)}) %all-gather.2.cloned.1.call-update) | async-done | bytes 1048592 | tf_op jit(solution)/shard_map/all_gather | solution.py:89
  112.1 782.5 %while.31 = (s32[]{:T(128)}, bf16[64,2,128]{2,1,0:T(2,128)(2,1)S(1)}, f32[64,2]{1,0:T(8,128)S(1)}, f32[64,2]{1,0:T(8,128)S(1)}, f32[64,2,128]{2,1,0:T(2,128)S(1)...) while((s32[]{:T(128)}, ...), condition=%wide.region_5.6_spmd, body=%wide.region_0.5_spmd.sunk | while | flops 34030600 | bytes 1954490 | solution.py:88
  117.7 14.6 %collective-permute-start.3 = (f32[64,2,128]{2,1,0:T(2,128)S(1)}, f32[64,2,128]{2,1,0:T(2,128)S(1)}, u32[]{:S(2)}, u32[]{:S(2)}) collective-permute-start(f32[64,2,128]{2,1,0:T(2,128)S(1)} %multiply_add_fusion.8), channel_id=1, source_target_pairs={{0,8},{8,16},{16,24},{24,32},{32,40},{40,48},{48,56},{56,64},{64,7... | collective-permute-start | bytes 196616 | tf_op jit(solution)/shard_map/while/body/eval_jaxpr/ppermute | solution.py:12
  132.6 7.4 collective-permute-done.1
  145.9 11.6 %collective-permute-start.3 = (f32[64,2,128]{2,1,0:T(2,128)S(1)}, f32[64,2,128]{2,1,0:T(2,128)S(1)}, u32[]{:S(2)}, u32[]{:S(2)}) collective-permute-start(f32[64,2,128]{2,1,0:T(2,128)S(1)} %multiply_add_fusion.8), channel_id=1, source_target_pairs={{0,8},{8,16},{16,24},{24,32},{32,40},{40,48},{48,56},{56,64},{64,7... | collective-permute-start | bytes 196616 | tf_op jit(solution)/shard_map/while/body/eval_jaxpr/ppermute | solution.py:12
  171.1 10.8 %collective-permute-start.3 = (f32[64,2,128]{2,1,0:T(2,128)S(1)}, f32[64,2,128]{2,1,0:T(2,128)S(1)}, u32[]{:S(2)}, u32[]{:S(2)}) collective-permute-start(f32[64,2,128]{2,1,0:T(2,128)S(1)} %multiply_add_fusion.8), channel_id=1, source_target_pairs={{0,8},{8,16},{16,24},{24,32},{32,40},{40,48},{48,56},{56,64},{64,7... | collective-permute-start | bytes 196616 | tf_op jit(solution)/shard_map/while/body/eval_jaxpr/ppermute | solution.py:12
  182.2 7.3 collective-permute-done.1
  195.5 10.6 %collective-permute-start.3 = (f32[64,2,128]{2,1,0:T(2,128)S(1)}, f32[64,2,128]{2,1,0:T(2,128)S(1)}, u32[]{:S(2)}, u32[]{:S(2)}) collective-permute-start(f32[64,2,128]{2,1,0:T(2,128)S(1)} %multiply_add_fusion.8), channel_id=1, source_target_pairs={{0,8},{8,16},{16,24},{24,32},{32,40},{40,48},{48,56},{56,64},{64,7... | collective-permute-start | bytes 196616 | tf_op jit(solution)/shard_map/while/body/eval_jaxpr/ppermute | solution.py:12
  219.7 10.6 %collective-permute-start.3 = (f32[64,2,128]{2,1,0:T(2,128)S(1)}, f32[64,2,128]{2,1,0:T(2,128)S(1)}, u32[]{:S(2)}, u32[]{:S(2)}) collective-permute-start(f32[64,2,128]{2,1,0:T(2,128)S(1)} %multiply_add_fusion.8), channel_id=1, source_target_pairs={{0,8},{8,16},{16,24},{24,32},{32,40},{40,48},{48,56},{56,64},{64,7... | collective-permute-start | bytes 196616 | tf_op jit(solution)/shard_map/while/body/eval_jaxpr/ppermute | solution.py:12
  230.6 7.3 collective-permute-done.1
  243.9 10.6 %collective-permute-start.3 = (f32[64,2,128]{2,1,0:T(2,128)S(1)}, f32[64,2,128]{2,1,0:T(2,128)S(1)}, u32[]{:S(2)}, u32[]{:S(2)}) collective-permute-start(f32[64,2,128]{2,1,0:T(2,128)S(1)} %multiply_add_fusion.8), channel_id=1, source_target_pairs={{0,8},{8,16},{16,24},{24,32},{32,40},{40,48},{48,56},{56,64},{64,7... | collective-permute-start | bytes 196616 | tf_op jit(solution)/shard_map/while/body/eval_jaxpr/ppermute | solution.py:12
  268.1 10.6 %collective-permute-start.3 = (f32[64,2,128]{2,1,0:T(2,128)S(1)}, f32[64,2,128]{2,1,0:T(2,128)S(1)}, u32[]{:S(2)}, u32[]{:S(2)}) collective-permute-start(f32[64,2,128]{2,1,0:T(2,128)S(1)} %multiply_add_fusion.8), channel_id=1, source_target_pairs={{0,8},{8,16},{16,24},{24,32},{32,40},{40,48},{48,56},{56,64},{64,7... | collective-permute-start | bytes 196616 | tf_op jit(solution)/shard_map/while/body/eval_jaxpr/ppermute | solution.py:12
  279.0 7.3 collective-permute-done.1
  292.3 10.6 %collective-permute-start.3 = (f32[64,2,128]{2,1,0:T(2,128)S(1)}, f32[64,2,128]{2,1,0:T(2,128)S(1)}, u32[]{:S(2)}, u32[]{:S(2)}) collective-permute-start(f32[64,2,128]{2,1,0:T(2,128)S(1)} %multiply_add_fusion.8), channel_id=1, source_target_pairs={{0,8},{8,16},{16,24},{24,32},{32,40},{40,48},{48,56},{56,64},{64,7... | collective-permute-start | bytes 196616 | tf_op jit(solution)/shard_map/while/body/eval_jaxpr/ppermute | solution.py:12
  316.4 10.6 %collective-permute-start.3 = (f32[64,2,128]{2,1,0:T(2,128)S(1)}, f32[64,2,128]{2,1,0:T(2,128)S(1)}, u32[]{:S(2)}, u32[]{:S(2)}) collective-permute-start(f32[64,2,128]{2,1,0:T(2,128)S(1)} %multiply_add_fusion.8), channel_id=1, source_target_pairs={{0,8},{8,16},{16,24},{24,32},{32,40},{40,48},{48,56},{56,64},{64,7... | collective-permute-start | bytes 196616 | tf_op jit(solution)/shard_map/while/body/eval_jaxpr/ppermute | solution.py:12
  327.3 7.3 collective-permute-done.1
  340.6 10.6 %collective-permute-start.3 = (f32[64,2,128]{2,1,0:T(2,128)S(1)}, f32[64,2,128]{2,1,0:T(2,128)S(1)}, u32[]{:S(2)}, u32[]{:S(2)}) collective-permute-start(f32[64,2,128]{2,1,0:T(2,128)S(1)} %multiply_add_fusion.8), channel_id=1, source_target_pairs={{0,8},{8,16},{16,24},{24,32},{32,40},{40,48},{48,56},{56,64},{64,7... | collective-permute-start | bytes 196616 | tf_op jit(solution)/shard_map/while/body/eval_jaxpr/ppermute | solution.py:12
  364.8 10.6 %collective-permute-start.3 = (f32[64,2,128]{2,1,0:T(2,128)S(1)}, f32[64,2,128]{2,1,0:T(2,128)S(1)}, u32[]{:S(2)}, u32[]{:S(2)}) collective-permute-start(f32[64,2,128]{2,1,0:T(2,128)S(1)} %multiply_add_fusion.8), channel_id=1, source_target_pairs={{0,8},{8,16},{16,24},{24,32},{32,40},{40,48},{48,56},{56,64},{64,7... | collective-permute-start | bytes 196616 | tf_op jit(solution)/shard_map/while/body/eval_jaxpr/ppermute | solution.py:12
  375.7 7.5 collective-permute-done.1
  389.5 10.1 %collective-permute-start.3 = (f32[64,2,128]{2,1,0:T(2,128)S(1)}, f32[64,2,128]{2,1,0:T(2,128)S(1)}, u32[]{:S(2)}, u32[]{:S(2)}) collective-permute-start(f32[64,2,128]{2,1,0:T(2,128)S(1)} %multiply_add_fusion.8), channel_id=1, source_target_pairs={{0,8},{8,16},{16,24},{24,32},{32,40},{40,48},{48,56},{56,64},{64,7... | collective-permute-start | bytes 196616 | tf_op jit(solution)/shard_map/while/body/eval_jaxpr/ppermute | solution.py:12
  399.9 7.5 collective-permute-done.1
  413.4 10.5 %collective-permute-start.3 = (f32[64,2,128]{2,1,0:T(2,128)S(1)}, f32[64,2,128]{2,1,0:T(2,128)S(1)}, u32[]{:S(2)}, u32[]{:S(2)}) collective-permute-start(f32[64,2,128]{2,1,0:T(2,128)S(1)} %multiply_add_fusion.8), channel_id=1, source_target_pairs={{0,8},{8,16},{16,24},{24,32},{32,40},{40,48},{48,56},{56,64},{64,7... | collective-permute-start | bytes 196616 | tf_op jit(solution)/shard_map/while/body/eval_jaxpr/ppermute | solution.py:12
  424.1 7.3 collective-permute-done.1
  437.4 10.6 %collective-permute-start.3 = (f32[64,2,128]{2,1,0:T(2,128)S(1)}, f32[64,2,128]{2,1,0:T(2,128)S(1)}, u32[]{:S(2)}, u32[]{:S(2)}) collective-permute-start(f32[64,2,128]{2,1,0:T(2,128)S(1)} %multiply_add_fusion.8), channel_id=1, source_target_pairs={{0,8},{8,16},{16,24},{24,32},{32,40},{40,48},{48,56},{56,64},{64,7... | collective-permute-start | bytes 196616 | tf_op jit(solution)/shard_map/while/body/eval_jaxpr/ppermute | solution.py:12
  461.6 10.6 %collective-permute-start.3 = (f32[64,2,128]{2,1,0:T(2,128)S(1)}, f32[64,2,128]{2,1,0:T(2,128)S(1)}, u32[]{:S(2)}, u32[]{:S(2)}) collective-permute-start(f32[64,2,128]{2,1,0:T(2,128)S(1)} %multiply_add_fusion.8), channel_id=1, source_target_pairs={{0,8},{8,16},{16,24},{24,32},{32,40},{40,48},{48,56},{56,64},{64,7... | collective-permute-start | bytes 196616 | tf_op jit(solution)/shard_map/while/body/eval_jaxpr/ppermute | solution.py:12
  472.5 7.3 collective-permute-done.1
  485.8 10.6 %collective-permute-start.3 = (f32[64,2,128]{2,1,0:T(2,128)S(1)}, f32[64,2,128]{2,1,0:T(2,128)S(1)}, u32[]{:S(2)}, u32[]{:S(2)}) collective-permute-start(f32[64,2,128]{2,1,0:T(2,128)S(1)} %multiply_add_fusion.8), channel_id=1, source_target_pairs={{0,8},{8,16},{16,24},{24,32},{32,40},{40,48},{48,56},{56,64},{64,7... | collective-permute-start | bytes 196616 | tf_op jit(solution)/shard_map/while/body/eval_jaxpr/ppermute | solution.py:12
  510.0 10.6 %collective-permute-start.3 = (f32[64,2,128]{2,1,0:T(2,128)S(1)}, f32[64,2,128]{2,1,0:T(2,128)S(1)}, u32[]{:S(2)}, u32[]{:S(2)}) collective-permute-start(f32[64,2,128]{2,1,0:T(2,128)S(1)} %multiply_add_fusion.8), channel_id=1, source_target_pairs={{0,8},{8,16},{16,24},{24,32},{32,40},{40,48},{48,56},{56,64},{64,7... | collective-permute-start | bytes 196616 | tf_op jit(solution)/shard_map/while/body/eval_jaxpr/ppermute | solution.py:12
  520.8 7.3 collective-permute-done.1
  534.1 10.6 %collective-permute-start.3 = (f32[64,2,128]{2,1,0:T(2,128)S(1)}, f32[64,2,128]{2,1,0:T(2,128)S(1)}, u32[]{:S(2)}, u32[]{:S(2)}) collective-permute-start(f32[64,2,128]{2,1,0:T(2,128)S(1)} %multiply_add_fusion.8), channel_id=1, source_target_pairs={{0,8},{8,16},{16,24},{24,32},{32,40},{40,48},{48,56},{56,64},{64,7... | collective-permute-start | bytes 196616 | tf_op jit(solution)/shard_map/while/body/eval_jaxpr/ppermute | solution.py:12
  558.3 10.6 %collective-permute-start.3 = (f32[64,2,128]{2,1,0:T(2,128)S(1)}, f32[64,2,128]{2,1,0:T(2,128)S(1)}, u32[]{:S(2)}, u32[]{:S(2)}) collective-permute-start(f32[64,2,128]{2,1,0:T(2,128)S(1)} %multiply_add_fusion.8), channel_id=1, source_target_pairs={{0,8},{8,16},{16,24},{24,32},{32,40},{40,48},{48,56},{56,64},{64,7... | collective-permute-start | bytes 196616 | tf_op jit(solution)/shard_map/while/body/eval_jaxpr/ppermute | solution.py:12
  569.2 7.3 collective-permute-done.1
  582.5 10.6 %collective-permute-start.3 = (f32[64,2,128]{2,1,0:T(2,128)S(1)}, f32[64,2,128]{2,1,0:T(2,128)S(1)}, u32[]{:S(2)}, u32[]{:S(2)}) collective-permute-start(f32[64,2,128]{2,1,0:T(2,128)S(1)} %multiply_add_fusion.8), channel_id=1, source_target_pairs={{0,8},{8,16},{16,24},{24,32},{32,40},{40,48},{48,56},{56,64},{64,7... | collective-permute-start | bytes 196616 | tf_op jit(solution)/shard_map/while/body/eval_jaxpr/ppermute | solution.py:12
  607.0 11.0 %collective-permute-start.3 = (f32[64,2,128]{2,1,0:T(2,128)S(1)}, f32[64,2,128]{2,1,0:T(2,128)S(1)}, u32[]{:S(2)}, u32[]{:S(2)}) collective-permute-start(f32[64,2,128]{2,1,0:T(2,128)S(1)} %multiply_add_fusion.8), channel_id=1, source_target_pairs={{0,8},{8,16},{16,24},{24,32},{32,40},{40,48},{48,56},{56,64},{64,7... | collective-permute-start | bytes 196616 | tf_op jit(solution)/shard_map/while/body/eval_jaxpr/ppermute | solution.py:12
  618.3 8.0 collective-permute-done.1
  632.3 11.6 %collective-permute-start.3 = (f32[64,2,128]{2,1,0:T(2,128)S(1)}, f32[64,2,128]{2,1,0:T(2,128)S(1)}, u32[]{:S(2)}, u32[]{:S(2)}) collective-permute-start(f32[64,2,128]{2,1,0:T(2,128)S(1)} %multiply_add_fusion.8), channel_id=1, source_target_pairs={{0,8},{8,16},{16,24},{24,32},{32,40},{40,48},{48,56},{56,64},{64,7... | collective-permute-start | bytes 196616 | tf_op jit(solution)/shard_map/while/body/eval_jaxpr/ppermute | solution.py:12
  657.4 11.5 %collective-permute-start.3 = (f32[64,2,128]{2,1,0:T(2,128)S(1)}, f32[64,2,128]{2,1,0:T(2,128)S(1)}, u32[]{:S(2)}, u32[]{:S(2)}) collective-permute-start(f32[64,2,128]{2,1,0:T(2,128)S(1)} %multiply_add_fusion.8), channel_id=1, source_target_pairs={{0,8},{8,16},{16,24},{24,32},{32,40},{40,48},{48,56},{56,64},{64,7... | collective-permute-start | bytes 196616 | tf_op jit(solution)/shard_map/while/body/eval_jaxpr/ppermute | solution.py:12
  682.5 10.6 %collective-permute-start.3 = (f32[64,2,128]{2,1,0:T(2,128)S(1)}, f32[64,2,128]{2,1,0:T(2,128)S(1)}, u32[]{:S(2)}, u32[]{:S(2)}) collective-permute-start(f32[64,2,128]{2,1,0:T(2,128)S(1)} %multiply_add_fusion.8), channel_id=1, source_target_pairs={{0,8},{8,16},{16,24},{24,32},{32,40},{40,48},{48,56},{56,64},{64,7... | collective-permute-start | bytes 196616 | tf_op jit(solution)/shard_map/while/body/eval_jaxpr/ppermute | solution.py:12
  706.6 10.6 %collective-permute-start.3 = (f32[64,2,128]{2,1,0:T(2,128)S(1)}, f32[64,2,128]{2,1,0:T(2,128)S(1)}, u32[]{:S(2)}, u32[]{:S(2)}) collective-permute-start(f32[64,2,128]{2,1,0:T(2,128)S(1)} %multiply_add_fusion.8), channel_id=1, source_target_pairs={{0,8},{8,16},{16,24},{24,32},{32,40},{40,48},{48,56},{56,64},{64,7... | collective-permute-start | bytes 196616 | tf_op jit(solution)/shard_map/while/body/eval_jaxpr/ppermute | solution.py:12
  730.8 10.6 %collective-permute-start.3 = (f32[64,2,128]{2,1,0:T(2,128)S(1)}, f32[64,2,128]{2,1,0:T(2,128)S(1)}, u32[]{:S(2)}, u32[]{:S(2)}) collective-permute-start(f32[64,2,128]{2,1,0:T(2,128)S(1)} %multiply_add_fusion.8), channel_id=1, source_target_pairs={{0,8},{8,16},{16,24},{24,32},{32,40},{40,48},{48,56},{56,64},{64,7... | collective-permute-start | bytes 196616 | tf_op jit(solution)/shard_map/while/body/eval_jaxpr/ppermute | solution.py:12
  755.0 10.6 %collective-permute-start.3 = (f32[64,2,128]{2,1,0:T(2,128)S(1)}, f32[64,2,128]{2,1,0:T(2,128)S(1)}, u32[]{:S(2)}, u32[]{:S(2)}) collective-permute-start(f32[64,2,128]{2,1,0:T(2,128)S(1)} %multiply_add_fusion.8), channel_id=1, source_target_pairs={{0,8},{8,16},{16,24},{24,32},{32,40},{40,48},{48,56},{56,64},{64,7... | collective-permute-start | bytes 196616 | tf_op jit(solution)/shard_map/while/body/eval_jaxpr/ppermute | solution.py:12
  779.2 10.6 %collective-permute-start.3 = (f32[64,2,128]{2,1,0:T(2,128)S(1)}, f32[64,2,128]{2,1,0:T(2,128)S(1)}, u32[]{:S(2)}, u32[]{:S(2)}) collective-permute-start(f32[64,2,128]{2,1,0:T(2,128)S(1)} %multiply_add_fusion.8), channel_id=1, source_target_pairs={{0,8},{8,16},{16,24},{24,32},{32,40},{40,48},{48,56},{56,64},{64,7... | collective-permute-start | bytes 196616 | tf_op jit(solution)/shard_map/while/body/eval_jaxpr/ppermute | solution.py:12
  803.4 10.6 %collective-permute-start.3 = (f32[64,2,128]{2,1,0:T(2,128)S(1)}, f32[64,2,128]{2,1,0:T(2,128)S(1)}, u32[]{:S(2)}, u32[]{:S(2)}) collective-permute-start(f32[64,2,128]{2,1,0:T(2,128)S(1)} %multiply_add_fusion.8), channel_id=1, source_target_pairs={{0,8},{8,16},{16,24},{24,32},{32,40},{40,48},{48,56},{56,64},{64,7... | collective-permute-start | bytes 196616 | tf_op jit(solution)/shard_map/while/body/eval_jaxpr/ppermute | solution.py:12
  827.6 10.6 %collective-permute-start.3 = (f32[64,2,128]{2,1,0:T(2,128)S(1)}, f32[64,2,128]{2,1,0:T(2,128)S(1)}, u32[]{:S(2)}, u32[]{:S(2)}) collective-permute-start(f32[64,2,128]{2,1,0:T(2,128)S(1)} %multiply_add_fusion.8), channel_id=1, source_target_pairs={{0,8},{8,16},{16,24},{24,32},{32,40},{40,48},{48,56},{56,64},{64,7... | collective-permute-start | bytes 196616 | tf_op jit(solution)/shard_map/while/body/eval_jaxpr/ppermute | solution.py:12
  851.8 10.6 %collective-permute-start.3 = (f32[64,2,128]{2,1,0:T(2,128)S(1)}, f32[64,2,128]{2,1,0:T(2,128)S(1)}, u32[]{:S(2)}, u32[]{:S(2)}) collective-permute-start(f32[64,2,128]{2,1,0:T(2,128)S(1)} %multiply_add_fusion.8), channel_id=1, source_target_pairs={{0,8},{8,16},{16,24},{24,32},{32,40},{40,48},{48,56},{56,64},{64,7... | collective-permute-start | bytes 196616 | tf_op jit(solution)/shard_map/while/body/eval_jaxpr/ppermute | solution.py:12
  876.0 10.6 %collective-permute-start.3 = (f32[64,2,128]{2,1,0:T(2,128)S(1)}, f32[64,2,128]{2,1,0:T(2,128)S(1)}, u32[]{:S(2)}, u32[]{:S(2)}) collective-permute-start(f32[64,2,128]{2,1,0:T(2,128)S(1)} %multiply_add_fusion.8), channel_id=1, source_target_pairs={{0,8},{8,16},{16,24},{24,32},{32,40},{40,48},{48,56},{56,64},{64,7... | collective-permute-start | bytes 196616 | tf_op jit(solution)/shard_map/while/body/eval_jaxpr/ppermute | solution.py:12
  896.8 8.6 copy.23
  905.5 59.5 %scatter_fusion = bf16[128,2,128]{2,1,0:T(2,128)(2,1)S(1)} fusion(bf16[128,2,128]{2,1,0:T(2,128)(2,1)S(1)} %broadcast_in_dim.37, s32[2048]{0:T(1024)S(1)} %compare_select_fusion, bf16[2048,2,128]{2,1,0:T(2,128)(2,1)S(1)} %copy.23), kind=kCustom, calls=%fused_computation | custom fusion | bytes 3153920 | tf_op jit(solution)/shard_map/scatter | solution.py:116
  (757 shorter events, 450.8 us)
Async XLA Ops:
  7.2 102.2 %all-gather.2.cloned.1.call-start = ((), (), s32[]{:S(2)}) async-start(), calls=%async_computation | async-start | bytes 1052672 | tf_op jit(solution)/shard_map/all_gather | solution.py:89
  117.7 22.6 %collective-permute-start.3 = (f32[64,2,128]{2,1,0:T(2,128)S(1)}, f32[64,2,128]{2,1,0:T(2,128)S(1)}, u32[]{:S(2)}, u32[]{:S(2)}) collective-permute-start(f32[64,2,128]{2,1,0:T(2,128)S(1)} %multiply_add_fusion.8), channel_id=1, source_target_pairs={{0,8},{8,16},{16,24},{24,32},{32,40},{40,48},{48,56},{56,64},{64,7... | collective-permute-start | bytes 196616 | tf_op jit(solution)/shard_map/while/body/eval_jaxpr/ppermute | solution.py:12
  132.3 8.0 collective-permute-start
  145.9 19.5 %collective-permute-start.3 = (f32[64,2,128]{2,1,0:T(2,128)S(1)}, f32[64,2,128]{2,1,0:T(2,128)S(1)}, u32[]{:S(2)}, u32[]{:S(2)}) collective-permute-start(f32[64,2,128]{2,1,0:T(2,128)S(1)} %multiply_add_fusion.8), channel_id=1, source_target_pairs={{0,8},{8,16},{16,24},{24,32},{32,40},{40,48},{48,56},{56,64},{64,7... | collective-permute-start | bytes 196616 | tf_op jit(solution)/shard_map/while/body/eval_jaxpr/ppermute | solution.py:12
  157.5 7.9 collective-permute-start
  171.1 18.8 %collective-permute-start.3 = (f32[64,2,128]{2,1,0:T(2,128)S(1)}, f32[64,2,128]{2,1,0:T(2,128)S(1)}, u32[]{:S(2)}, u32[]{:S(2)}) collective-permute-start(f32[64,2,128]{2,1,0:T(2,128)S(1)} %multiply_add_fusion.8), channel_id=1, source_target_pairs={{0,8},{8,16},{16,24},{24,32},{32,40},{40,48},{48,56},{56,64},{64,7... | collective-permute-start | bytes 196616 | tf_op jit(solution)/shard_map/while/body/eval_jaxpr/ppermute | solution.py:12
  181.9 7.9 collective-permute-start
  195.5 18.6 %collective-permute-start.3 = (f32[64,2,128]{2,1,0:T(2,128)S(1)}, f32[64,2,128]{2,1,0:T(2,128)S(1)}, u32[]{:S(2)}, u32[]{:S(2)}) collective-permute-start(f32[64,2,128]{2,1,0:T(2,128)S(1)} %multiply_add_fusion.8), channel_id=1, source_target_pairs={{0,8},{8,16},{16,24},{24,32},{32,40},{40,48},{48,56},{56,64},{64,7... | collective-permute-start | bytes 196616 | tf_op jit(solution)/shard_map/while/body/eval_jaxpr/ppermute | solution.py:12
  206.1 7.9 collective-permute-start
  219.7 18.6 %collective-permute-start.3 = (f32[64,2,128]{2,1,0:T(2,128)S(1)}, f32[64,2,128]{2,1,0:T(2,128)S(1)}, u32[]{:S(2)}, u32[]{:S(2)}) collective-permute-start(f32[64,2,128]{2,1,0:T(2,128)S(1)} %multiply_add_fusion.8), channel_id=1, source_target_pairs={{0,8},{8,16},{16,24},{24,32},{32,40},{40,48},{48,56},{56,64},{64,7... | collective-permute-start | bytes 196616 | tf_op jit(solution)/shard_map/while/body/eval_jaxpr/ppermute | solution.py:12
  230.3 7.9 collective-permute-start
  243.9 18.6 %collective-permute-start.3 = (f32[64,2,128]{2,1,0:T(2,128)S(1)}, f32[64,2,128]{2,1,0:T(2,128)S(1)}, u32[]{:S(2)}, u32[]{:S(2)}) collective-permute-start(f32[64,2,128]{2,1,0:T(2,128)S(1)} %multiply_add_fusion.8), channel_id=1, source_target_pairs={{0,8},{8,16},{16,24},{24,32},{32,40},{40,48},{48,56},{56,64},{64,7... | collective-permute-start | bytes 196616 | tf_op jit(solution)/shard_map/while/body/eval_jaxpr/ppermute | solution.py:12
  254.5 7.9 collective-permute-start
  268.1 18.6 %collective-permute-start.3 = (f32[64,2,128]{2,1,0:T(2,128)S(1)}, f32[64,2,128]{2,1,0:T(2,128)S(1)}, u32[]{:S(2)}, u32[]{:S(2)}) collective-permute-start(f32[64,2,128]{2,1,0:T(2,128)S(1)} %multiply_add_fusion.8), channel_id=1, source_target_pairs={{0,8},{8,16},{16,24},{24,32},{32,40},{40,48},{48,56},{56,64},{64,7... | collective-permute-start | bytes 196616 | tf_op jit(solution)/shard_map/while/body/eval_jaxpr/ppermute | solution.py:12
  278.7 7.9 collective-permute-start
  292.3 18.6 %collective-permute-start.3 = (f32[64,2,128]{2,1,0:T(2,128)S(1)}, f32[64,2,128]{2,1,0:T(2,128)S(1)}, u32[]{:S(2)}, u32[]{:S(2)}) collective-permute-start(f32[64,2,128]{2,1,0:T(2,128)S(1)} %multiply_add_fusion.8), channel_id=1, source_target_pairs={{0,8},{8,16},{16,24},{24,32},{32,40},{40,48},{48,56},{56,64},{64,7... | collective-permute-start | bytes 196616 | tf_op jit(solution)/shard_map/while/body/eval_jaxpr/ppermute | solution.py:12
  316.4 18.6 %collective-permute-start.3 = (f32[64,2,128]{2,1,0:T(2,128)S(1)}, f32[64,2,128]{2,1,0:T(2,128)S(1)}, u32[]{:S(2)}, u32[]{:S(2)}) collective-permute-start(f32[64,2,128]{2,1,0:T(2,128)S(1)} %multiply_add_fusion.8), channel_id=1, source_target_pairs={{0,8},{8,16},{16,24},{24,32},{32,40},{40,48},{48,56},{56,64},{64,7... | collective-permute-start | bytes 196616 | tf_op jit(solution)/shard_map/while/body/eval_jaxpr/ppermute | solution.py:12
  340.6 18.6 %collective-permute-start.3 = (f32[64,2,128]{2,1,0:T(2,128)S(1)}, f32[64,2,128]{2,1,0:T(2,128)S(1)}, u32[]{:S(2)}, u32[]{:S(2)}) collective-permute-start(f32[64,2,128]{2,1,0:T(2,128)S(1)} %multiply_add_fusion.8), channel_id=1, source_target_pairs={{0,8},{8,16},{16,24},{24,32},{32,40},{40,48},{48,56},{56,64},{64,7... | collective-permute-start | bytes 196616 | tf_op jit(solution)/shard_map/while/body/eval_jaxpr/ppermute | solution.py:12
  364.8 19.1 %collective-permute-start.3 = (f32[64,2,128]{2,1,0:T(2,128)S(1)}, f32[64,2,128]{2,1,0:T(2,128)S(1)}, u32[]{:S(2)}, u32[]{:S(2)}) collective-permute-start(f32[64,2,128]{2,1,0:T(2,128)S(1)} %multiply_add_fusion.8), channel_id=1, source_target_pairs={{0,8},{8,16},{16,24},{24,32},{32,40},{40,48},{48,56},{56,64},{64,7... | collective-permute-start | bytes 196616 | tf_op jit(solution)/shard_map/while/body/eval_jaxpr/ppermute | solution.py:12
  375.4 8.5 collective-permute-start
  375.6 8.3 collective-permute-start.2
  389.5 18.2 %collective-permute-start.3 = (f32[64,2,128]{2,1,0:T(2,128)S(1)}, f32[64,2,128]{2,1,0:T(2,128)S(1)}, u32[]{:S(2)}, u32[]{:S(2)}) collective-permute-start(f32[64,2,128]{2,1,0:T(2,128)S(1)} %multiply_add_fusion.8), channel_id=1, source_target_pairs={{0,8},{8,16},{16,24},{24,32},{32,40},{40,48},{48,56},{56,64},{64,7... | collective-permute-start | bytes 196616 | tf_op jit(solution)/shard_map/while/body/eval_jaxpr/ppermute | solution.py:12
  399.6 8.1 collective-permute-start
  413.4 18.4 %collective-permute-start.3 = (f32[64,2,128]{2,1,0:T(2,128)S(1)}, f32[64,2,128]{2,1,0:T(2,128)S(1)}, u32[]{:S(2)}, u32[]{:S(2)}) collective-permute-start(f32[64,2,128]{2,1,0:T(2,128)S(1)} %multiply_add_fusion.8), channel_id=1, source_target_pairs={{0,8},{8,16},{16,24},{24,32},{32,40},{40,48},{48,56},{56,64},{64,7... | collective-permute-start | bytes 196616 | tf_op jit(solution)/shard_map/while/body/eval_jaxpr/ppermute | solution.py:12
  437.4 18.6 %collective-permute-start.3 = (f32[64,2,128]{2,1,0:T(2,128)S(1)}, f32[64,2,128]{2,1,0:T(2,128)S(1)}, u32[]{:S(2)}, u32[]{:S(2)}) collective-permute-start(f32[64,2,128]{2,1,0:T(2,128)S(1)} %multiply_add_fusion.8), channel_id=1, source_target_pairs={{0,8},{8,16},{16,24},{24,32},{32,40},{40,48},{48,56},{56,64},{64,7... | collective-permute-start | bytes 196616 | tf_op jit(solution)/shard_map/while/body/eval_jaxpr/ppermute | solution.py:12
  461.6 18.6 %collective-permute-start.3 = (f32[64,2,128]{2,1,0:T(2,128)S(1)}, f32[64,2,128]{2,1,0:T(2,128)S(1)}, u32[]{:S(2)}, u32[]{:S(2)}) collective-permute-start(f32[64,2,128]{2,1,0:T(2,128)S(1)} %multiply_add_fusion.8), channel_id=1, source_target_pairs={{0,8},{8,16},{16,24},{24,32},{32,40},{40,48},{48,56},{56,64},{64,7... | collective-permute-start | bytes 196616 | tf_op jit(solution)/shard_map/while/body/eval_jaxpr/ppermute | solution.py:12
  485.8 18.6 %collective-permute-start.3 = (f32[64,2,128]{2,1,0:T(2,128)S(1)}, f32[64,2,128]{2,1,0:T(2,128)S(1)}, u32[]{:S(2)}, u32[]{:S(2)}) collective-permute-start(f32[64,2,128]{2,1,0:T(2,128)S(1)} %multiply_add_fusion.8), channel_id=1, source_target_pairs={{0,8},{8,16},{16,24},{24,32},{32,40},{40,48},{48,56},{56,64},{64,7... | collective-permute-start | bytes 196616 | tf_op jit(solution)/shard_map/while/body/eval_jaxpr/ppermute | solution.py:12
  510.0 18.6 %collective-permute-start.3 = (f32[64,2,128]{2,1,0:T(2,128)S(1)}, f32[64,2,128]{2,1,0:T(2,128)S(1)}, u32[]{:S(2)}, u32[]{:S(2)}) collective-permute-start(f32[64,2,128]{2,1,0:T(2,128)S(1)} %multiply_add_fusion.8), channel_id=1, source_target_pairs={{0,8},{8,16},{16,24},{24,32},{32,40},{40,48},{48,56},{56,64},{64,7... | collective-permute-start | bytes 196616 | tf_op jit(solution)/shard_map/while/body/eval_jaxpr/ppermute | solution.py:12
  534.1 18.6 %collective-permute-start.3 = (f32[64,2,128]{2,1,0:T(2,128)S(1)}, f32[64,2,128]{2,1,0:T(2,128)S(1)}, u32[]{:S(2)}, u32[]{:S(2)}) collective-permute-start(f32[64,2,128]{2,1,0:T(2,128)S(1)} %multiply_add_fusion.8), channel_id=1, source_target_pairs={{0,8},{8,16},{16,24},{24,32},{32,40},{40,48},{48,56},{56,64},{64,7... | collective-permute-start | bytes 196616 | tf_op jit(solution)/shard_map/while/body/eval_jaxpr/ppermute | solution.py:12
  558.3 18.6 %collective-permute-start.3 = (f32[64,2,128]{2,1,0:T(2,128)S(1)}, f32[64,2,128]{2,1,0:T(2,128)S(1)}, u32[]{:S(2)}, u32[]{:S(2)}) collective-permute-start(f32[64,2,128]{2,1,0:T(2,128)S(1)} %multiply_add_fusion.8), channel_id=1, source_target_pairs={{0,8},{8,16},{16,24},{24,32},{32,40},{40,48},{48,56},{56,64},{64,7... | collective-permute-start | bytes 196616 | tf_op jit(solution)/shard_map/while/body/eval_jaxpr/ppermute | solution.py:12
  582.5 18.8 %collective-permute-start.3 = (f32[64,2,128]{2,1,0:T(2,128)S(1)}, f32[64,2,128]{2,1,0:T(2,128)S(1)}, u32[]{:S(2)}, u32[]{:S(2)}) collective-permute-start(f32[64,2,128]{2,1,0:T(2,128)S(1)} %multiply_add_fusion.8), channel_id=1, source_target_pairs={{0,8},{8,16},{16,24},{24,32},{32,40},{40,48},{48,56},{56,64},{64,7... | collective-permute-start | bytes 196616 | tf_op jit(solution)/shard_map/while/body/eval_jaxpr/ppermute | solution.py:12
  593.1 8.2 collective-permute-start
  593.3 8.0 collective-permute-start.2
  607.0 19.7 %collective-permute-start.3 = (f32[64,2,128]{2,1,0:T(2,128)S(1)}, f32[64,2,128]{2,1,0:T(2,128)S(1)}, u32[]{:S(2)}, u32[]{:S(2)}) collective-permute-start(f32[64,2,128]{2,1,0:T(2,128)S(1)} %multiply_add_fusion.8), channel_id=1, source_target_pairs={{0,8},{8,16},{16,24},{24,32},{32,40},{40,48},{48,56},{56,64},{64,7... | collective-permute-start | bytes 196616 | tf_op jit(solution)/shard_map/while/body/eval_jaxpr/ppermute | solution.py:12
  618.0 8.7 collective-permute-start
  618.1 8.2 collective-permute-start.1
  618.2 8.5 collective-permute-start.2
  632.3 19.5 %collective-permute-start.3 = (f32[64,2,128]{2,1,0:T(2,128)S(1)}, f32[64,2,128]{2,1,0:T(2,128)S(1)}, u32[]{:S(2)}, u32[]{:S(2)}) collective-permute-start(f32[64,2,128]{2,1,0:T(2,128)S(1)} %multiply_add_fusion.8), channel_id=1, source_target_pairs={{0,8},{8,16},{16,24},{24,32},{32,40},{40,48},{48,56},{56,64},{64,7... | collective-permute-start | bytes 196616 | tf_op jit(solution)/shard_map/while/body/eval_jaxpr/ppermute | solution.py:12
  657.4 19.4 %collective-permute-start.3 = (f32[64,2,128]{2,1,0:T(2,128)S(1)}, f32[64,2,128]{2,1,0:T(2,128)S(1)}, u32[]{:S(2)}, u32[]{:S(2)}) collective-permute-start(f32[64,2,128]{2,1,0:T(2,128)S(1)} %multiply_add_fusion.8), channel_id=1, source_target_pairs={{0,8},{8,16},{16,24},{24,32},{32,40},{40,48},{48,56},{56,64},{64,7... | collective-permute-start | bytes 196616 | tf_op jit(solution)/shard_map/while/body/eval_jaxpr/ppermute | solution.py:12
  682.5 18.6 %collective-permute-start.3 = (f32[64,2,128]{2,1,0:T(2,128)S(1)}, f32[64,2,128]{2,1,0:T(2,128)S(1)}, u32[]{:S(2)}, u32[]{:S(2)}) collective-permute-start(f32[64,2,128]{2,1,0:T(2,128)S(1)} %multiply_add_fusion.8), channel_id=1, source_target_pairs={{0,8},{8,16},{16,24},{24,32},{32,40},{40,48},{48,56},{56,64},{64,7... | collective-permute-start | bytes 196616 | tf_op jit(solution)/shard_map/while/body/eval_jaxpr/ppermute | solution.py:12
  706.6 18.6 %collective-permute-start.3 = (f32[64,2,128]{2,1,0:T(2,128)S(1)}, f32[64,2,128]{2,1,0:T(2,128)S(1)}, u32[]{:S(2)}, u32[]{:S(2)}) collective-permute-start(f32[64,2,128]{2,1,0:T(2,128)S(1)} %multiply_add_fusion.8), channel_id=1, source_target_pairs={{0,8},{8,16},{16,24},{24,32},{32,40},{40,48},{48,56},{56,64},{64,7... | collective-permute-start | bytes 196616 | tf_op jit(solution)/shard_map/while/body/eval_jaxpr/ppermute | solution.py:12
  730.8 18.6 %collective-permute-start.3 = (f32[64,2,128]{2,1,0:T(2,128)S(1)}, f32[64,2,128]{2,1,0:T(2,128)S(1)}, u32[]{:S(2)}, u32[]{:S(2)}) collective-permute-start(f32[64,2,128]{2,1,0:T(2,128)S(1)} %multiply_add_fusion.8), channel_id=1, source_target_pairs={{0,8},{8,16},{16,24},{24,32},{32,40},{40,48},{48,56},{56,64},{64,7... | collective-permute-start | bytes 196616 | tf_op jit(solution)/shard_map/while/body/eval_jaxpr/ppermute | solution.py:12
  755.0 18.6 %collective-permute-start.3 = (f32[64,2,128]{2,1,0:T(2,128)S(1)}, f32[64,2,128]{2,1,0:T(2,128)S(1)}, u32[]{:S(2)}, u32[]{:S(2)}) collective-permute-start(f32[64,2,128]{2,1,0:T(2,128)S(1)} %multiply_add_fusion.8), channel_id=1, source_target_pairs={{0,8},{8,16},{16,24},{24,32},{32,40},{40,48},{48,56},{56,64},{64,7... | collective-permute-start | bytes 196616 | tf_op jit(solution)/shard_map/while/body/eval_jaxpr/ppermute | solution.py:12
  779.2 18.6 %collective-permute-start.3 = (f32[64,2,128]{2,1,0:T(2,128)S(1)}, f32[64,2,128]{2,1,0:T(2,128)S(1)}, u32[]{:S(2)}, u32[]{:S(2)}) collective-permute-start(f32[64,2,128]{2,1,0:T(2,128)S(1)} %multiply_add_fusion.8), channel_id=1, source_target_pairs={{0,8},{8,16},{16,24},{24,32},{32,40},{40,48},{48,56},{56,64},{64,7... | collective-permute-start | bytes 196616 | tf_op jit(solution)/shard_map/while/body/eval_jaxpr/ppermute | solution.py:12
  803.4 18.6 %collective-permute-start.3 = (f32[64,2,128]{2,1,0:T(2,128)S(1)}, f32[64,2,128]{2,1,0:T(2,128)S(1)}, u32[]{:S(2)}, u32[]{:S(2)}) collective-permute-start(f32[64,2,128]{2,1,0:T(2,128)S(1)} %multiply_add_fusion.8), channel_id=1, source_target_pairs={{0,8},{8,16},{16,24},{24,32},{32,40},{40,48},{48,56},{56,64},{64,7... | collective-permute-start | bytes 196616 | tf_op jit(solution)/shard_map/while/body/eval_jaxpr/ppermute | solution.py:12
  827.6 18.6 %collective-permute-start.3 = (f32[64,2,128]{2,1,0:T(2,128)S(1)}, f32[64,2,128]{2,1,0:T(2,128)S(1)}, u32[]{:S(2)}, u32[]{:S(2)}) collective-permute-start(f32[64,2,128]{2,1,0:T(2,128)S(1)} %multiply_add_fusion.8), channel_id=1, source_target_pairs={{0,8},{8,16},{16,24},{24,32},{32,40},{40,48},{48,56},{56,64},{64,7... | collective-permute-start | bytes 196616 | tf_op jit(solution)/shard_map/while/body/eval_jaxpr/ppermute | solution.py:12
  851.8 18.6 %collective-permute-start.3 = (f32[64,2,128]{2,1,0:T(2,128)S(1)}, f32[64,2,128]{2,1,0:T(2,128)S(1)}, u32[]{:S(2)}, u32[]{:S(2)}) collective-permute-start(f32[64,2,128]{2,1,0:T(2,128)S(1)} %multiply_add_fusion.8), channel_id=1, source_target_pairs={{0,8},{8,16},{16,24},{24,32},{32,40},{40,48},{48,56},{56,64},{64,7... | collective-permute-start | bytes 196616 | tf_op jit(solution)/shard_map/while/body/eval_jaxpr/ppermute | solution.py:12
  876.0 18.6 %collective-permute-start.3 = (f32[64,2,128]{2,1,0:T(2,128)S(1)}, f32[64,2,128]{2,1,0:T(2,128)S(1)}, u32[]{:S(2)}, u32[]{:S(2)}) collective-permute-start(f32[64,2,128]{2,1,0:T(2,128)S(1)} %multiply_add_fusion.8), channel_id=1, source_target_pairs={{0,8},{8,16},{16,24},{24,32},{32,40},{40,48},{48,56},{56,64},{64,7... | collective-permute-start | bytes 196616 | tf_op jit(solution)/shard_map/while/body/eval_jaxpr/ppermute | solution.py:12
  (87 other events, 629.3 us)
Sparse Core Ops, SparseCore 0:
  12.3 96.9 all-gather.1
where the time goes:
time: 980 us; the launch traced here: 972 us
  starting transfers between devices  355 us (36%)
  waiting for transfers between devices  347 us (35%)
  local copies, waits for them, and re-layouts  104 us (11%)
  matrix products  75.6 us (8%)
  loops' own time  64.9 us (7%)
  between operations  14.2 us (1%)
  other arithmetic  11.3 us (1%)
    ppermute x128, starting transfers between devices, passed_along(): return lax.ppermute(value, axis, pairs)  355 us
    ppermute x128, waiting for transfers between devices, passed_along(): return lax.ppermute(value, axis, pairs)  247 us
    all_gather x1, waiting for transfers between devices, shards(): new_rows = lax.all_gather(new_kv, ('ctx', 'head'), axis=0, tiled=True)  100 us
    another operation x32, loops' own time, cache_part(): return lax.fori_loop(0, live_count, take_page, initial)  62.8 us
    scatter x1, local copies, waits for them, and re-layouts, shards(): jnp.zeros((append_rows, 2, head_size), jnp.bfloat16).at[target]  59.5 us
    dot_general x32, matrix products, take_page(): jnp.dot(weights.astype(jnp.bfloat16), value_block, preferred_element_type...  37.3 us
    dot_general x32, matrix products, take_page(): lax.dot_general(query_rows, key_block, (((1,), (1,)), ((), ())), preferre...  36.6 us
    dynamic_slice x32, local copies, waits for them, and re-layouts, take_page(): page_index = lax.dynamic_index_in_dim(table_row, number, 0, keepdims=False)  20.7 us
  transfers between devices with their start and end apart: 129, of which 65 were waited for; matrix products, arithmetic and copies ran while one was open for 0% of the time, Pallas kernels for 0%

commit v1 on v0

v1 whole, which is shorter than its diff:
```python
import functools
import math

import jax
import jax.numpy as jnp
from jax import lax
from jax.experimental import pallas as pl
from jax.experimental.pallas import tpu as pltpu
from jax.sharding import Mesh, PartitionSpec as P

F32 = jnp.float32
BF16 = jnp.bfloat16
I32 = jnp.int32
HD = 128
PAGES = 4
HALF = 256
KEYS = 2 * HALF
SIDE = PAGES * HALF
QROWS = 1024
TILE = 256
BLOCK = 128
NEG = -1e30
SCALE = 1.4426950408889634 / math.sqrt(HD)
FIXED = float(1 << 18)
PAYLOAD = 144
SENT = 160


def shifted(value, axis, steps):
    count = lax.axis_size(axis)
    return lax.ppermute(value, axis, [(i, (i + steps) % count) for i in range(count)])


def swapped(value, axis, bit):
    count = lax.axis_size(axis)
    return lax.ppermute(value, axis, [(i, i ^ bit) for i in range(count)])


def across(row):
    return jnp.transpose(jnp.broadcast_to(row, (BLOCK, BLOCK)), (1, 0))


def split_fixed(value):
    fixed = jnp.round(value * FIXED).astype(I32)
    return [fixed >> 16, (fixed & 0xFFFF) - 32768]


def join_fixed(high, low):
    return (high * 65536 + (low + 32768)).astype(F32) * (1.0 / FIXED)


def page_parts(ref, p, start=0, stride=HALF):
    return ref[pl.ds(pl.multiple_of(start + p * stride, HALF), HALF), :]


def score_pages(q, scores, top, slot, mask, keys_at):
    def page(p, carry):
        @pl.when(((mask >> p) & 1) != 0)
        def _():
            for i, keys in enumerate(keys_at(p)):
                for t in range(QROWS // TILE):
                    rows = pl.ds(t * TILE, TILE)
                    s = lax.dot_general(
                        q[rows, :], keys, (((1,), (1,)), ((), ())), preferred_element_type=F32
                    )
                    scores[slot + p, rows, i * HALF : (i + 1) * HALF] = s
                    top[rows, :] = jnp.maximum(
                        top[rows, :], jnp.maximum(s[:, :HD], s[:, HD:])
                    )

        return carry

    lax.fori_loop(0, PAGES, page, 0)


def weigh(scores_at, values, level, total, acc, width):
    for t in range(QROWS // TILE):
        rows = pl.ds(t * TILE, TILE)
        now = level[rows, :]
        s = scores_at(rows)
        parts = [
            jnp.exp2((s[:, j * HD : (j + 1) * HD] - now) * SCALE) for j in range(width // HD)
        ]
        total[rows, :] = total[rows, :] + functools.reduce(jnp.add, parts)
        weight = jnp.concatenate([e.astype(BF16) for e in parts], axis=1)
        acc[rows, :] = acc[rows, :] + jnp.dot(weight, values, preferred_element_type=F32)


def weigh_pages(scores, level, total, acc, slot, mask, values_at):
    def page(p, carry):
        @pl.when(((mask >> p) & 1) != 0)
        def _():
            values = jnp.concatenate(values_at(p), axis=0)
            weigh(lambda rows: scores[slot + p, rows, :], values, level, total, acc, KEYS)

        return carry

    lax.fori_loop(0, PAGES, page, 0)


def settle(top, level):
    found = []
    for b in range(QROWS // BLOCK):
        rows = pl.ds(b * BLOCK, BLOCK)
        row = jnp.max(jnp.transpose(top[rows, :], (1, 0)), axis=0, keepdims=True)
        level[rows, :] = across(row)
        found.append(row)
    return found


def mask_of(ref, start=2 * SIDE):
    return jnp.sum(ref[start : start + 16, :].astype(F32)).astype(I32)


def here():
    return [lax.axis_index(a) for a in ("z", "x", "y", "core")]


def load_queries(q, q3):
    for b in range(8):
        q[pl.ds(b * BLOCK, BLOCK), :] = q3[b, 0:BLOCK, :]


def gather_kernel(queries, near, far, out):
    for b in range(8):
        out[b, 0:BLOCK, :] = queries[...]
        out[b, BLOCK : BLOCK + 16, :] = near[...]
        out[b, BLOCK + 16 : SENT, :] = far[...]


def first_kernel(
    table, live, q3, ok, ov, an, af, bn, bf, level, total, acc, q, scores, top
):
    load_queries(q, q3)
    top[...] = jnp.full(top.shape, NEG, F32)
    total[...] = jnp.zeros(total.shape, F32)
    acc[...] = jnp.zeros(acc.shape, F32)
    own = 0
    for k in range(PAGES):
        own = own + jnp.where(k < live[0], jnp.left_shift(1, table[0, k]), 0)
    stores = [
        (
            own,
            lambda p: [page_parts(ok, p, 0, KEYS), page_parts(ok, p, HALF, KEYS)],
            lambda p: [page_parts(ov, p, 0, KEYS), page_parts(ov, p, HALF, KEYS)],
        )
    ]
    for near, far in ((an, af), (bn, bf)):
        stores.append(
            (
                mask_of(near),
                lambda p, near=near, far=far: [page_parts(near, p), page_parts(far, p)],
                lambda p, near=near, far=far: [page_parts(near, p, SIDE), page_parts(far, p, SIDE)],
            )
        )
    for i, (mask, keys_at, _) in enumerate(stores):
        score_pages(q, scores, top, i * PAGES, mask, keys_at)
    settle(top, level)
    for i, (mask, _, values_at) in enumerate(stores):
        weigh_pages(scores, level, total, acc, i * PAGES, mask, values_at)


def second_kernel(
    q3, ckn, cvn, ckf, cvf, new, level_in, total_in, acc_in, out,
    q, scores, fresh, top, level, total, acc,
):
    z, x, y, core = here()
    load_queries(q, q3)
    top[...] = level_in[...]
    mask = mask_of(cvn, SIDE)
    score_pages(q, scores, top, 0, mask, lambda p: [page_parts(ckn, p), page_parts(ckf, p)])

    at = lax.broadcasted_iota(I32, (BLOCK, BLOCK), 0)
    place = lax.broadcasted_iota(I32, (BLOCK, BLOCK), 1) == (at % 64) * 2 + at // 64
    place = jnp.where(place, 1.0, 0.0).astype(BF16)
    apart = [
        jnp.dot(place, new[g * BLOCK : (g + 1) * BLOCK, :], preferred_element_type=F32).astype(BF16)
        for g in range(4)
    ]
    keys = jnp.concatenate([n[0:64, :] for n in apart], axis=0)
    values = jnp.concatenate([n[64:BLOCK, :] for n in apart], axis=0)
    slot = lax.broadcasted_iota(I32, (TILE, 256), 1)
    side = jnp.where(slot < 128, jnp.where(z < 4, 0, 3), jnp.where(z < 4, 2, 1))
    head = ((y + side) & 3) * 2 + (core ^ ((slot // 8) & 1))
    token = ((slot // 16) % 8 * 4 + ((x + z) & 3)) * 64 + head * 8 + slot % 8
    row = lax.broadcasted_iota(I32, (TILE, 256), 0)
    for t in range(QROWS // TILE):
        rows = pl.ds(t * TILE, TILE)
        s = lax.dot_general(q[rows, :], keys, (((1,), (1,)), ((), ())), preferred_element_type=F32)
        position = ((2 * t + row // BLOCK) * 4 + x) * 64 + (row % BLOCK) // 2
        s = jnp.where(token <= position, s, NEG)
        fresh[rows, :] = s
        top[rows, :] = jnp.maximum(top[rows, :], jnp.maximum(s[:, :HD], s[:, HD:]))
    peaks = settle(top, level)
    for t in range(QROWS // TILE):
        rows = pl.ds(t * TILE, TILE)
        factor = jnp.exp2((level_in[rows, :] - level[rows, :]) * SCALE)
        total[rows, :] = total_in[rows, :] * factor
        acc[rows, :] = acc_in[rows, :] * factor
    weigh_pages(
        scores, level, total, acc, 0, mask, lambda p: [page_parts(cvn, p), page_parts(cvf, p)]
    )
    weigh(lambda rows: fresh[rows, :], values, level, total, acc, 256)

    for j in range(8):
        rows = pl.ds(j * BLOCK, BLOCK)
        full = acc[rows, :]
        size = jnp.max(jnp.transpose(jnp.abs(full), (1, 0)), axis=0, keepdims=True)
        size = jnp.maximum(size, 1e-30)
        number = jnp.round(full * across(32767.0 / size)).astype(I32).astype(jnp.int16)
        weight = jnp.sum(jnp.transpose(total[rows, :], (1, 0)), axis=0, keepdims=True)
        stats = (
            split_fixed(peaks[j] * SCALE)
            + split_fixed(jnp.log2(weight))
            + split_fixed(jnp.log2(size))
        )
        stats = jnp.concatenate(stats + [jnp.zeros((10, BLOCK), I32)], axis=0)
        out[j] = jnp.concatenate([number, stats.astype(jnp.int16)], axis=0)


def merge_kernel(parts, out):
    stats = [parts[s, BLOCK:PAYLOAD, :].astype(I32) for s in range(8)]

    def rows(at):
        return jnp.concatenate(
            [join_fixed(s[at : at + 1, :], s[at + 1 : at + 2, :]) for s in stats], axis=0
        )

    peak, weight, size = rows(0), rows(2), rows(4)
    peak = peak - jnp.max(peak, axis=0, keepdims=True)
    whole = jnp.sum(jnp.exp2(peak + weight), axis=0, keepdims=True)
    factor = jnp.exp2(peak + size) / (whole * 32767.0)
    columns = jnp.transpose(factor, (1, 0))
    total = jnp.zeros((BLOCK, HD), F32)
    for s in range(8):
        total = total + parts[s, 0:BLOCK, :].astype(F32) * columns[:, s : s + 1]
    out[...] = total.astype(BF16)


def route_kernel(r0, r1, r2, r3, code, o0, o1, o2, o3):
    z, x, y, core = here()
    target = lax.broadcasted_iota(I32, (4 * 256, 256), 0)
    lane = lax.broadcasted_iota(I32, (4 * 256, 256), 1)
    store = z * 4 + ((x + target // 256) & 3)
    want = jnp.where((target & 1) == (lane & 1), store * 128 + (target % 256) // 2, -1)
    total = jnp.zeros((4 * 256, HD), F32)
    for j, r in enumerate((r0, r1, r2, r3)):
        have = code[pl.ds((y + (0, 3, 1, 2)[j]) & 3, 1), :]
        chosen = jnp.where(want == have, 1.0, 0.0).astype(BF16)
        total = total + jnp.dot(chosen, r[...], preferred_element_type=F32)
    total = total.astype(BF16)
    for d, o in enumerate((o0, o1, o2, o3)):
        o[...] = total[d * 256 : (d + 1) * 256, :]


def place_kernel(n0, n1, n2, n3, out):
    total = n0[...].astype(F32) + n1[...].astype(F32)
    total = total + n2[...].astype(F32) + n3[...].astype(F32)
    out[...] = total.astype(BF16)


def after(value, *others):
    def kernel(*refs):
        pass

    return pl.pallas_call(
        kernel,
        out_shape=jax.ShapeDtypeStruct(value.shape, value.dtype),
        in_specs=[pl.BlockSpec(memory_space=pl.ANY)] * (1 + len(others)),
        out_specs=pl.BlockSpec(memory_space=pl.ANY),
        input_output_aliases={0: 0},
        name="after",
    )(value, *others)


def smem():
    return pl.BlockSpec(memory_space=pltpu.SMEM)


def vmem():
    return pl.BlockSpec(memory_space=pltpu.VMEM)


def cost(pages):
    return pl.CostEstimate(
        flops=4 * QROWS * KEYS * HD * pages,
        bytes_accessed=1 << 20,
        transcendentals=QROWS * KEYS * pages,
    )


def shards(
    queries, cache_keys, cache_values, page_table, page_count, new_kv, new_owner, new_offset
):
    z, x = lax.axis_index("z"), lax.axis_index("x")
    y, core = lax.axis_index("y"), lax.axis_index("core")

    bits = jnp.where(jnp.arange(PAGES) < page_count[0], 1 << page_table[0], 0)
    bits_row = jnp.pad(bits.astype(BF16)[None, :], ((0, 15), (0, HD - PAGES)))
    halves = [
        lax.dynamic_index_in_dim(a.reshape(PAGES, 2, HALF, HD), core, 1, keepdims=False).reshape(
            SIDE, HD
        )
        for a in (cache_keys, cache_values)
    ]
    halves = jnp.concatenate(halves + [bits_row], axis=0)
    an, bn = shifted(halves, "x", 1), shifted(halves, "x", -1)
    ckn, cvn = shifted(an[:SIDE], "x", 1), shifted(bn[SIDE:], "x", -1)
    af, bf, ckf, cvf = [swapped(a, "core", 1) for a in (an, bn, ckn, cvn)]

    near = new_kv.reshape(16, HD)
    far = swapped(near, "core", 1)
    sent = pl.pallas_call(
        gather_kernel,
        out_shape=jax.ShapeDtypeStruct((8, SENT, HD), BF16),
        in_specs=[vmem()] * 3,
        out_specs=vmem(),
        name="gather",
    )(queries.reshape(BLOCK, HD), near, far)
    q3 = lax.all_to_all(sent, "z", 0, 0)
    rows = q3[:, BLOCK:, :].reshape(256, HD)
    rows = [rows, shifted(rows, "y", 1), shifted(rows, "y", -1), shifted(rows, "y", 2)]
    lower = z < 4
    new = jnp.concatenate(
        [jnp.where(lower, rows[0], rows[1]), jnp.where(lower, rows[3], rows[2])], axis=0
    )
    new = lax.ppermute(
        new, ("z", "x"), [(p * 4 + (i + p) % 4, p * 4 + i) for p in range(8) for i in range(4)]
    )

    state = jax.ShapeDtypeStruct((QROWS, HD), F32)
    params = pltpu.CompilerParams(vmem_limit_bytes=48 * 1024 * 1024)
    level, total, acc = pl.pallas_call(
        first_kernel,
        out_shape=(state,) * 3,
        in_specs=[smem()] * 2 + [vmem()] * 7,
        out_specs=(vmem(),) * 3,
        scratch_shapes=[
            pltpu.VMEM((QROWS, HD), BF16),
            pltpu.VMEM((3 * PAGES, QROWS, KEYS), F32),
            pltpu.VMEM((QROWS, HD), F32),
        ],
        compiler_params=params,
        cost_estimate=cost(6),
        name="first",
    )(page_table, page_count, q3, cache_keys, cache_values, an, af, bn, bf)
    payload = pl.pallas_call(
        second_kernel,
        out_shape=jax.ShapeDtypeStruct((8, PAYLOAD, HD), jnp.int16),
        in_specs=[vmem()] * 9,
        out_specs=vmem(),
        scratch_shapes=[
            pltpu.VMEM((QROWS, HD), BF16),
            pltpu.VMEM((PAGES, QROWS, KEYS), F32),
            pltpu.VMEM((QROWS, 256), F32),
        ]
        + [pltpu.VMEM((QROWS, HD), F32)] * 4,
        compiler_params=params,
        cost_estimate=cost(2),
        name="second",
    )(q3, ckn, cvn, ckf, cvf, new, level, total, acc)

    code = (new_owner * 128 + new_offset).reshape(8, 4, 4, 2, 8)
    code = lax.dynamic_index_in_dim(code, x, 1, keepdims=False)
    code = jnp.where(core == 1, jnp.flip(code, 2), code)
    code = jnp.repeat(jnp.transpose(code, (1, 0, 2, 3)).reshape(4, 128), 2, axis=1)
    code = after(code, payload)
    piece = jax.ShapeDtypeStruct((256, HD), BF16)
    t0, to_after, to_opposite, to_before = pl.pallas_call(
        route_kernel,
        out_shape=(piece,) * 4,
        in_specs=[vmem()] * 5,
        out_specs=(vmem(),) * 4,
        name="route",
    )(*rows, code)
    t1 = shifted(to_after, "x", 1)
    t2 = shifted(to_before, "x", -1)
    t3 = shifted(to_opposite, "x", 2)
    parts = lax.all_to_all(payload, "z", 0, 0)
    attended = pl.pallas_call(
        merge_kernel,
        out_shape=jax.ShapeDtypeStruct((BLOCK, HD), BF16),
        in_specs=[vmem()],
        out_specs=vmem(),
        name="merge",
    )(parts)
    appended = pl.pallas_call(
        place_kernel,
        out_shape=jax.ShapeDtypeStruct((256, HD), BF16),
        in_specs=[vmem()] * 4,
        out_specs=vmem(),
        name="place",
    )(t0, t1, t2, t3)
    return attended.reshape(queries.shape), appended.reshape(BLOCK, 2, HD)


def solution(mesh):
    grid = Mesh(mesh.devices.reshape(8, 4, 4, 2), ("z", "x", "y", "core"))
    ctx, head = ("z", "x"), ("y", "core")
    in_specs = (
        P(ctx, head, None),
        P(ctx, None),
        P(ctx, None),
        P(ctx, None),
        P(ctx),
        P(ctx + head, None, None),
        P(),
        P(),
    )
    out_specs = (P(ctx, head, None), P(ctx, None, None))
    return jax.shard_map(shards, mesh=grid, in_specs=in_specs, out_specs=out_specs, check_vma=False)
```

time: 980 us -> 78.6 us (0.08)
  waiting for transfers between devices: 347 us -> 21.2 us
  starting transfers between devices: 355 us -> 30.9 us
  local copies, waits for them, and re-layouts: 104 us -> 4.22 us
  matrix products: 75.6 us -> 0 us
  loops' own time: 64.9 us -> 0 us
  Pallas kernels: 0 us -> 18.9 us
  between operations: 14.2 us -> 1.56 us
  other arithmetic: 11.3 us -> 0.75 us
    ppermute x128 -> x16, starting transfers between devices: 355 us -> 17.5 us  [the longest x10 15.8 us: shifted(): lax.ppermute(value, axis, [(i, (i + steps) % count) for i in range(count)])]
    ppermute x128 -> x16, waiting for transfers between devices: 247 us -> 10.2 us  [the longest x10 10.1 us: shifted(): lax.ppermute(value, axis, [(i, (i + steps) % count) for i in range(count)])]
    all_gather x1 -> x0, waiting for transfers between devices: 100 us -> none  [shards(): new_rows = lax.all_gather(new_kv, ('ctx', 'head'), axis=0, tiled=True)]
    dot_general x66 -> x0, matrix products: 75.6 us -> none  [the longest x32 37.3 us: take_page(): jnp.dot(weights.astype(jnp.bfloat16), value_block, preferred_element_type...]
    another operation x33 -> x0, loops' own time: 64.9 us -> none  [the longest x32 62.8 us: cache_part(): return lax.fori_loop(0, live_count, take_page, initial)]
    scatter x1 -> x0, local copies, waits for them, and re-layouts: 59.5 us -> none  [shards(): jnp.zeros((append_rows, 2, head_size), jnp.bfloat16).at[target]]
    dynamic_slice x32 -> x3, local copies, waits for them, and re-layouts: 20.7 us -> 1.09 us  [the longest x1 1.06 us: shards(): lax.dynamic_index_in_dim(a.reshape(PAGES, 2, HALF, HD), core, 1, keepdims...]
    pallas_call x0 -> x7, Pallas kernels: none -> 18.9 us  [the longest x1 7.27 us: shards(): pl.pallas_call(first_kernel, out_shape=(state,) * 3, in_specs=[smem()] *...]
  transfers between devices with their start and end apart: 129 -> 18, of which waited for: 65 -> 8; matrix products, arithmetic and copies ran while one was open for 0% -> 4% of each run, Pallas kernels for 0% -> 14%
where the time goes in v1:
time: 78.6 us; the launch traced here: 77.6 us
  starting transfers between devices  30.9 us (39%)
  waiting for transfers between devices  21.2 us (27%)
  Pallas kernels  18.9 us (24%)
  local copies, waits for them, and re-layouts  4.22 us (5%)
  between operations  1.56 us (2%)
    ppermute x10, starting transfers between devices, shifted(): lax.ppermute(value, axis, [(i, (i + steps) % count) for i in range(count)])  15.8 us
    all_to_all x1, waiting for transfers between devices, shards(): q3 = lax.all_to_all(sent, 'z', 0, 0)  11.1 us
    ppermute x10, waiting for transfers between devices, shifted(): lax.ppermute(value, axis, [(i, (i + steps) % count) for i in range(count)])  10.1 us
    all_to_all x1, starting transfers between devices, shards(): q3 = lax.all_to_all(sent, 'z', 0, 0)  8.47 us
    pallas_call x1, Pallas kernels, shards(): pl.pallas_call(first_kernel, out_shape=(state,) * 3, in_specs=[smem()] *...  7.27 us
    all_to_all x1, starting transfers between devices, shards(): parts = lax.all_to_all(payload, 'z', 0, 0)  4.95 us
    pallas_call x1, Pallas kernels, shards(): pl.pallas_call(second_kernel, out_shape=jax.ShapeDtypeStruct((8, PAYLOAD,...  4.18 us
    pallas_call x1, Pallas kernels, shards(): pl.pallas_call(route_kernel, out_shape=(piece,) * 4, in_specs=[vmem()] *...  2.33 us
  transfers between devices with their start and end apart: 18, of which 8 were waited for; matrix products, arithmetic and copies ran while one was open for 4% of the time, Pallas kernels for 14%

profile of v1, /device:TPU:8, one launch (start us, length us, event | category | flops | bytes accessed | tf_op | source)
XLA Modules:
  0.0 77.6 jit_solution(4991715526477124117)
XLA Ops:
  0.6 0.1 collective-permute-start
  1.4 0.7 fusion.3
  2.0 1.1 %constant_dynamic-slice_fusion.1 = (bf16[4,1,256,128]{3,2,1,0:T(8,128)(2,1)S(1)}, bf16[4,1,256,128]{3,2,1,0:T(8,128)(2,1)S(1)}) fusion(bf16[4,2,256,128]{3,2,1,0:T(8,128)(2,1)} %bitcast.23, s32[]{:T(128)S(6)} %select_n.34, bf16[4,2,256,128]{3,2,1,0:T(8,128)(2,1)} %bitcast.24), kind=kLoop, calls=%fused_computation.12 | loop fusion | bytes 1048580 | tf_op jit(solution)/shard_map/jit(dynamic_index_in_dim)/dynamic_slice | solution.py:301
  3.1 0.0 collective-permute-done.far
  3.1 0.0 copy-start.13
  3.1 0.6 copy-done.13
  3.7 1.5 %gather.1 = bf16[8,160,128]{2,1,0:T(8,128)(2,1)} custom-call(bf16[128,128]{1,0:T(8,128)(2,1)} %bitcast.35, bf16[16,128]{1,0:T(8,128)(2,1)} %bitcast.38, bf16[16,128]{1,0:T(8,128)(2,1)} %copy-done.13), custom_call_target="tpu_custom_call" | custom-call | tf_op jit(solution)/shard_map/gather/pallas_call | solution.py:313
  5.3 8.5 %all-to-all-start = ((bf16[8,160,128]{2,1,0:T(8,128)(2,1)}), bf16[8,160,128]{2,1,0:T(8,128)(2,1)S(1)}, u32[]{:S(2)}, u32[]{:S(2)}) async-start(bf16[8,160,128]{2,1,0:T(8,128)(2,1)} %gather.1), calls=%async_computation | async-start | bytes 655360 | tf_op jit(solution)/shard_map/all_to_all | solution.py:320
  13.8 2.8 %collective-permute-start.3 = (bf16[2064,128]{1,0:T(8,128)(2,1)S(1)}, bf16[2064,128]{1,0:T(8,128)(2,1)S(1)}, u32[]{:S(2)}, u32[]{:S(2)}) collective-permute-start(bf16[2064,128]{1,0:T(8,128)(2,1)S(1)} %fusion.1), channel_id=1, source_target_pairs={{0,24},{8,0},{16,8},{24,16},{1,25},{9,1},{17,9},{25,17},{2,26},{10... | collective-permute-start | bytes 1585160 | tf_op jit(solution)/shard_map/ppermute | solution.py:31
  16.6 0.0 collective-permute-start.1
  16.6 11.1 %all-to-all-done.q3 = bf16[8,160,128]{2,1,0:T(8,128)(2,1)S(1)} async-done(((bf16[8,160,128]{2,1,0:T(8,128)(2,1)}), bf16[8,160,128]{2,1,0:T(8,128)(2,1)S(1)}, u32[]{:S(2)}, u32[]{:S(2)}) %all-to-all-start) | async-done | bytes 327712 | tf_op jit(solution)/shard_map/all_to_all | solution.py:320
  27.7 2.4 %collective-permute-start.8 = (bf16[256,128]{1,0:T(8,128)(2,1)S(1)}, bf16[256,128]{1,0:T(8,128)(2,1)S(1)}, u32[]{:S(2)}, u32[]{:S(2)}) collective-permute-start(bf16[256,128]{1,0:T(8,128)(2,1)S(1)} %bitcast.27), channel_id=1, source_target_pairs={{0,4},{2,6},{4,0},{6,2},{1,5},{3,7},{5,1},{7,3},{8,12},{10,14},{12... | collective-permute-start | bytes 196616 | tf_op jit(solution)/shard_map/ppermute | solution.py:31
  30.1 0.0 collective-permute-start.7
  30.1 0.0 collective-permute-done.3.bn
  30.1 0.0 copy-start
  30.1 0.0 copy-start.1
  30.1 0.0 copy-start.2
  30.1 2.8 %collective-permute-start.4 = (bf16[1040,128]{1,0:T(8,128)(2,1)S(1)}, bf16[1040,128]{1,0:T(8,128)(2,1)S(1)}, u32[]{:S(2)}, u32[]{:S(2)}) collective-permute-start(bf16[1040,128]{1,0:T(8,128)(2,1)S(1)} %slice.13), channel_id=1, source_target_pairs={{0,24},{8,0},{16,8},{24,16},{1,25},{9,1},{17,9},{25,17},{2,26},{10... | collective-permute-start | bytes 798728 | tf_op jit(solution)/shard_map/ppermute | solution.py:31
  33.0 0.0 collective-permute-done.1.an
  33.0 0.1 collective-permute-start.2
  33.1 0.1 collective-permute-start.11
  33.2 0.4 collective-permute-done.8.r3
  33.5 0.1 collective-permute-start.12
  33.7 1.1 %collective-permute-done.7.r1 = bf16[256,128]{1,0:T(8,128)(2,1)S(1)} collective-permute-done((bf16[256,128]{1,0:T(8,128)(2,1)S(1)}, bf16[256,128]{1,0:T(8,128)(2,1)S(1)}, u32[]{:S(2)}, u32[]{:S(2)}) %collective-permute-start.7) | collective-permute-done | bytes 65568 | tf_op jit(solution)/shard_map/ppermute | solution.py:31
  34.8 2.1 %collective-permute-start.9 = (bf16[256,128]{1,0:T(8,128)(2,1)S(1)}, bf16[256,128]{1,0:T(8,128)(2,1)S(1)}, u32[]{:S(2)}, u32[]{:S(2)}) collective-permute-start(bf16[256,128]{1,0:T(8,128)(2,1)S(1)} %bitcast.29), channel_id=1, source_target_pairs={{0,6},{2,0},{4,2},{6,4},{1,7},{3,1},{5,3},{7,5},{8,14},{10,8},{12,... | collective-permute-start | bytes 196616 | tf_op jit(solution)/shard_map/ppermute | solution.py:31
  36.9 2.2 %collective-permute-done.9.r2 = bf16[256,128]{1,0:T(8,128)(2,1)S(1)} collective-permute-done((bf16[256,128]{1,0:T(8,128)(2,1)S(1)}, bf16[256,128]{1,0:T(8,128)(2,1)S(1)}, u32[]{:S(2)}, u32[]{:S(2)}) %collective-permute-start.9) | collective-permute-done | bytes 65568 | tf_op jit(solution)/shard_map/ppermute | solution.py:31
  39.1 2.9 %collective-permute-done.2.ckn = bf16[1024,128]{1,0:T(8,128)(2,1)S(1)} collective-permute-done((bf16[1024,128]{1,0:T(8,128)(2,1)S(1)}, bf16[1024,128]{1,0:T(8,128)(2,1)S(1)}, u32[]{:S(2)}, u32[]{:S(2)}) %collective-permute-start.2) | collective-permute-done | bytes 262176 | tf_op jit(solution)/shard_map/ppermute | solution.py:31
  42.0 0.0 collective-permute-start.5
  42.0 0.0 collective-permute-done.4.cvn
  42.0 0.5 collective-permute-start.6
  42.5 0.8 %collective-permute-start.10 = (bf16[512,128]{1,0:T(8,128)(2,1)S(1)}, bf16[512,128]{1,0:T(8,128)(2,1)S(1)}, u32[]{:S(2)}, u32[]{:S(2)}) collective-permute-start(bf16[512,128]{1,0:T(8,128)(2,1)S(1)} %pad_maximum_fusion), channel_id=1, source_target_pairs={{0,0},{8,8},{16,16},{24,24},{40,32},{48,40},{56,48},{32,56},{80,64... | collective-permute-start | bytes 393224 | tf_op jit(solution)/shard_map/ppermute | solution.py:327
  43.4 7.3 %first.1 = (f32[1024,128]{1,0:T(8,128)S(1)}, f32[1024,128]{1,0:T(8,128)S(1)}, f32[1024,128]{1,0:T(8,128)S(1)}) custom-call(s32[1,4]{1,0:T(1,128)S(1)} %copy-done.2, s32[1]{0:T(128)} %copy.33.live, bf16[8,160,128]{2,1,0:T(8,128)(2,1)S(1)} %all-to-all-done.q3, bf16[2048,128]{1,0:T(8,128)(2,1)S(1)} %copy-done.1, bf16[2048,128]{1,0:T(8,128)(2,1)S(1)} %copy-done, ...), custom_call_target="tpu_custom_call" | custom-call | flops 1610612736 | bytes 1048576 | tf_op jit(solution)/shard_map/first/pallas_call | solution.py:333
  50.8 4.2 %second.1.refs_1_ = s16[8,144,128]{2,1,0:T(8,128)(2,1)} custom-call(bf16[8,160,128]{2,1,0:T(8,128)(2,1)S(1)} %all-to-all-done.q3, bf16[1024,128]{1,0:T(8,128)(2,1)S(1)} %collective-permute-done.2.ckn, bf16[1040,128]{1,0:T(8,128)(2,1)S(1)} %collective-permute-done.4.cvn, bf16[1024,128]{1,0:T(8,128)(2,1)S(1)} %collective-permute-done.5.ckf, ...), custom_call_target="tpu_custom_call" | custom-call | flops 536870912 | bytes 1048576 | tf_op jit(solution)/shard_map/second/pallas_call | solution.py:347
  54.9 4.9 %all-to-all-start.1 = ((s16[8,144,128]{2,1,0:T(8,128)(2,1)}), s16[8,144,128]{2,1,0:T(8,128)(2,1)S(1)}, u32[]{:S(2)}, u32[]{:S(2)}) async-start(s16[8,144,128]{2,1,0:T(8,128)(2,1)} %second.1.refs_1_), calls=%async_computation.1 | async-start | bytes 589824 | tf_op jit(solution)/shard_map/all_to_all | solution.py:379
  59.9 0.2 reshape.57
  60.2 0.2 copy.26
  60.4 0.7 copy.25.refs_0_
  61.1 2.3 %route.1 = (bf16[256,128]{1,0:T(8,128)(2,1)}, bf16[256,128]{1,0:T(8,128)(2,1)}, bf16[256,128]{1,0:T(8,128)(2,1)}, bf16[256,128]{1,0:T(8,128)(2,1)}) custom-call(bf16[256,128]{1,0:T(8,128)(2,1)} %bitcast.30, bf16[256,128]{1,0:T(8,128)(2,1)} %copy-done.6, bf16[256,128]{1,0:T(8,128)(2,1)} %copy-done.7, bf16[256,128]{1,0:T(8,128)(2,1)} %copy-done.5, ...), custom_call_target="tpu_custom_call" | custom-call | tf_op jit(solution)/shard_map/route/pallas_call | solution.py:369
  63.4 0.8 collective-permute-start.13
  64.2 2.5 %collective-permute-start.14 = (bf16[256,128]{1,0:T(8,128)(2,1)}, bf16[256,128]{1,0:T(8,128)(2,1)S(1)}, u32[]{:S(2)}, u32[]{:S(2)}) collective-permute-start(bf16[256,128]{1,0:T(8,128)(2,1)} %get-tuple-element.14), channel_id=1, source_target_pairs={{0,24},{8,0},{16,8},{24,16},{1,25},{9,1},{17,9},{25,17},{2,26},{10... | collective-permute-start | bytes 196616 | tf_op jit(solution)/shard_map/ppermute | solution.py:31
  66.7 2.4 %collective-permute-start.15 = (bf16[256,128]{1,0:T(8,128)(2,1)}, bf16[256,128]{1,0:T(8,128)(2,1)S(1)}, u32[]{:S(2)}, u32[]{:S(2)}) collective-permute-start(bf16[256,128]{1,0:T(8,128)(2,1)} %get-tuple-element.15), channel_id=1, source_target_pairs={{0,16},{8,24},{16,0},{24,8},{1,17},{9,25},{17,1},{25,9},{2,18},{10... | collective-permute-start | bytes 196616 | tf_op jit(solution)/shard_map/ppermute | solution.py:31
  69.1 0.1 collective-permute-done.13.n1
  69.1 0.7 collective-permute-done.14.n2
  69.8 2.9 %collective-permute-done.15.n3 = bf16[256,128]{1,0:T(8,128)(2,1)S(1)} collective-permute-done((bf16[256,128]{1,0:T(8,128)(2,1)}, bf16[256,128]{1,0:T(8,128)(2,1)S(1)}, u32[]{:S(2)}, u32[]{:S(2)}) %collective-permute-start.15) | collective-permute-done | bytes 65568 | tf_op jit(solution)/shard_map/ppermute | solution.py:31
  72.7 0.6 copy-done.10
  73.3 1.6 %place.1 = bf16[256,128]{1,0:T(8,128)(2,1)} custom-call(bf16[256,128]{1,0:T(8,128)(2,1)} %get-tuple-element.12.n0, bf16[256,128]{1,0:T(8,128)(2,1)} %copy-done.8, bf16[256,128]{1,0:T(8,128)(2,1)} %copy-done.9, bf16[256,128]{1,0:T(8,128)(2,1)} %copy-done.10), custom_call_target="tpu_custom_call" | custom-call | tf_op jit(solution)/shard_map/place/pallas_call | solution.py:387
  74.9 0.7 copy-done.3
  75.6 2.0 %merge.1 = bf16[128,128]{1,0:T(8,128)(2,1)} custom-call(s16[8,144,128]{2,1,0:T(8,128)(2,1)} %copy-done.3), custom_call_target="tpu_custom_call" | custom-call | tf_op jit(solution)/shard_map/merge/pallas_call | solution.py:380
  (40 shorter events, 0.3 us)
Async XLA Ops:
  0.6 2.5 %collective-permute-start = (bf16[16,128]{1,0:T(8,128)(2,1)}, bf16[16,128]{1,0:T(8,128)(2,1)S(1)}, u32[]{:S(2)}, u32[]{:S(2)}) collective-permute-start(bf16[16,128]{1,0:T(8,128)(2,1)} %bitcast.37), channel_id=1, source_target_pairs={{0,1},{1,0},{2,3},{3,2},{4,5},{5,4},{6,7},{7,6},{8,9},{9,8},{10,11... | collective-permute-start | bytes 12296 | tf_op jit(solution)/shard_map/ppermute | solution.py:36
  3.1 0.6 copy-start.13
  5.3 22.4 %all-to-all-start = ((bf16[8,160,128]{2,1,0:T(8,128)(2,1)}), bf16[8,160,128]{2,1,0:T(8,128)(2,1)S(1)}, u32[]{:S(2)}, u32[]{:S(2)}) async-start(bf16[8,160,128]{2,1,0:T(8,128)(2,1)} %gather.1), calls=%async_computation | async-start | bytes 655360 | tf_op jit(solution)/shard_map/all_to_all | solution.py:320
  13.8 16.3 %collective-permute-start.3 = (bf16[2064,128]{1,0:T(8,128)(2,1)S(1)}, bf16[2064,128]{1,0:T(8,128)(2,1)S(1)}, u32[]{:S(2)}, u32[]{:S(2)}) collective-permute-start(bf16[2064,128]{1,0:T(8,128)(2,1)S(1)} %fusion.1), channel_id=1, source_target_pairs={{0,24},{8,0},{16,8},{24,16},{1,25},{9,1},{17,9},{25,17},{2,26},{10... | collective-permute-start | bytes 1585160 | tf_op jit(solution)/shard_map/ppermute | solution.py:31
  16.6 16.4 %collective-permute-start.1 = (bf16[2064,128]{1,0:T(8,128)(2,1)S(1)}, bf16[2064,128]{1,0:T(8,128)(2,1)S(1)}, u32[]{:S(2)}, u32[]{:S(2)}) collective-permute-start(bf16[2064,128]{1,0:T(8,128)(2,1)S(1)} %fusion.1), channel_id=1, source_target_pairs={{0,8},{8,16},{16,24},{24,0},{1,9},{9,17},{17,25},{25,1},{2,10},{10... | collective-permute-start | bytes 1585160 | tf_op jit(solution)/shard_map/ppermute | solution.py:31
  27.7 9.2 %copy-start.4 = (bf16[8,32,128]{2,1,0:T(8,128)(2,1)}, bf16[8,32,128]{2,1,0:T(8,128)(2,1)S(1)}, u32[]{:S(2)}) copy-start(bf16[8,32,128]{2,1,0:T(8,128)(2,1)S(1)} %slice.14) | copy-start | bytes 196612
  27.7 5.9 %collective-permute-start.8 = (bf16[256,128]{1,0:T(8,128)(2,1)S(1)}, bf16[256,128]{1,0:T(8,128)(2,1)S(1)}, u32[]{:S(2)}, u32[]{:S(2)}) collective-permute-start(bf16[256,128]{1,0:T(8,128)(2,1)S(1)} %bitcast.27), channel_id=1, source_target_pairs={{0,4},{2,6},{4,0},{6,2},{1,5},{3,7},{5,1},{7,3},{8,12},{10,14},{12... | collective-permute-start | bytes 196616 | tf_op jit(solution)/shard_map/ppermute | solution.py:31
  30.1 4.8 %collective-permute-start.7 = (bf16[256,128]{1,0:T(8,128)(2,1)S(1)}, bf16[256,128]{1,0:T(8,128)(2,1)S(1)}, u32[]{:S(2)}, u32[]{:S(2)}) collective-permute-start(bf16[256,128]{1,0:T(8,128)(2,1)S(1)} %bitcast.28), channel_id=1, source_target_pairs={{0,2},{2,4},{4,6},{6,0},{1,3},{3,5},{5,7},{7,1},{8,10},{10,12},{12... | collective-permute-start | bytes 196616 | tf_op jit(solution)/shard_map/ppermute | solution.py:31
  30.1 13.3 %copy-start = (bf16[2048,128]{1,0:T(8,128)(2,1)S(1)}, bf16[2048,128]{1,0:T(8,128)(2,1)}, u32[]{:S(2)}) copy-start(bf16[2048,128]{1,0:T(8,128)(2,1)} %ov.1) | copy-start | bytes 1572868
  30.1 13.3 %copy-start.1 = (bf16[2048,128]{1,0:T(8,128)(2,1)S(1)}, bf16[2048,128]{1,0:T(8,128)(2,1)}, u32[]{:S(2)}) copy-start(bf16[2048,128]{1,0:T(8,128)(2,1)} %ok.1) | copy-start | bytes 1572868
  30.1 13.3 %copy-start.2 = (s32[1,4]{1,0:T(1,128)S(1)}, s32[1,4]{1,0:T(1,128)}, u32[]{:S(2)}) copy-start(s32[1,4]{1,0:T(1,128)} %table.1) | copy-start | bytes 52
  30.1 11.9 %collective-permute-start.4 = (bf16[1040,128]{1,0:T(8,128)(2,1)S(1)}, bf16[1040,128]{1,0:T(8,128)(2,1)S(1)}, u32[]{:S(2)}, u32[]{:S(2)}) collective-permute-start(bf16[1040,128]{1,0:T(8,128)(2,1)S(1)} %slice.13), channel_id=1, source_target_pairs={{0,24},{8,0},{16,8},{24,16},{1,25},{9,1},{17,9},{25,17},{2,26},{10... | collective-permute-start | bytes 798728 | tf_op jit(solution)/shard_map/ppermute | solution.py:31
  33.0 9.0 %collective-permute-start.2 = (bf16[1024,128]{1,0:T(8,128)(2,1)S(1)}, bf16[1024,128]{1,0:T(8,128)(2,1)S(1)}, u32[]{:S(2)}, u32[]{:S(2)}) collective-permute-start(bf16[1024,128]{1,0:T(8,128)(2,1)S(1)} %slice.12), channel_id=1, source_target_pairs={{0,8},{8,16},{16,24},{24,0},{1,9},{9,17},{17,25},{25,1},{2,10},{10... | collective-permute-start | bytes 786440 | tf_op jit(solution)/shard_map/ppermute | solution.py:31
  33.1 10.3 %collective-permute-start.11 = (bf16[2064,128]{1,0:T(8,128)(2,1)S(1)}, bf16[2064,128]{1,0:T(8,128)(2,1)S(1)}, u32[]{:S(2)}, u32[]{:S(2)}) collective-permute-start(bf16[2064,128]{1,0:T(8,128)(2,1)S(1)} %collective-permute-done.1.an), channel_id=1, source_target_pairs={{0,1},{1,0},{2,3},{3,2},{4,5},{5,4},{6,7},{7,6},{8,9},{9,8},{10,11... | collective-permute-start | bytes 1585160 | tf_op jit(solution)/shard_map/ppermute | solution.py:36
  33.5 17.2 %copy-start.5 = (bf16[256,128]{1,0:T(8,128)(2,1)}, bf16[256,128]{1,0:T(8,128)(2,1)S(1)}, u32[]{:S(2)}) copy-start(bf16[256,128]{1,0:T(8,128)(2,1)S(1)} %collective-permute-done.8.r3) | copy-start | bytes 196612
  33.5 9.8 %collective-permute-start.12 = (bf16[2064,128]{1,0:T(8,128)(2,1)S(1)}, bf16[2064,128]{1,0:T(8,128)(2,1)S(1)}, u32[]{:S(2)}, u32[]{:S(2)}) collective-permute-start(bf16[2064,128]{1,0:T(8,128)(2,1)S(1)} %collective-permute-done.3.bn), channel_id=1, source_target_pairs={{0,1},{1,0},{2,3},{3,2},{4,5},{5,4},{6,7},{7,6},{8,9},{9,8},{10,11... | collective-permute-start | bytes 1585160 | tf_op jit(solution)/shard_map/ppermute | solution.py:36
  34.8 15.9 %copy-start.6 = (bf16[256,128]{1,0:T(8,128)(2,1)}, bf16[256,128]{1,0:T(8,128)(2,1)S(1)}, u32[]{:S(2)}) copy-start(bf16[256,128]{1,0:T(8,128)(2,1)S(1)} %collective-permute-done.7.r1) | copy-start | bytes 196612
  34.8 4.3 %collective-permute-start.9 = (bf16[256,128]{1,0:T(8,128)(2,1)S(1)}, bf16[256,128]{1,0:T(8,128)(2,1)S(1)}, u32[]{:S(2)}, u32[]{:S(2)}) collective-permute-start(bf16[256,128]{1,0:T(8,128)(2,1)S(1)} %bitcast.29), channel_id=1, source_target_pairs={{0,6},{2,0},{4,2},{6,4},{1,7},{3,1},{5,3},{7,5},{8,14},{10,8},{12,... | collective-permute-start | bytes 196616 | tf_op jit(solution)/shard_map/ppermute | solution.py:31
  39.1 11.6 %copy-start.7 = (bf16[256,128]{1,0:T(8,128)(2,1)}, bf16[256,128]{1,0:T(8,128)(2,1)S(1)}, u32[]{:S(2)}) copy-start(bf16[256,128]{1,0:T(8,128)(2,1)S(1)} %collective-permute-done.9.r2) | copy-start | bytes 196612
  42.0 8.8 %collective-permute-start.5 = (bf16[1024,128]{1,0:T(8,128)(2,1)S(1)}, bf16[1024,128]{1,0:T(8,128)(2,1)S(1)}, u32[]{:S(2)}, u32[]{:S(2)}) collective-permute-start(bf16[1024,128]{1,0:T(8,128)(2,1)S(1)} %collective-permute-done.2.ckn), channel_id=1, source_target_pairs={{0,1},{1,0},{2,3},{3,2},{4,5},{5,4},{6,7},{7,6},{8,9},{9,8},{10,11... | collective-permute-start | bytes 786440 | tf_op jit(solution)/shard_map/ppermute | solution.py:36
  42.0 8.8 %collective-permute-start.6 = (bf16[1040,128]{1,0:T(8,128)(2,1)S(1)}, bf16[1040,128]{1,0:T(8,128)(2,1)S(1)}, u32[]{:S(2)}, u32[]{:S(2)}) collective-permute-start(bf16[1040,128]{1,0:T(8,128)(2,1)S(1)} %collective-permute-done.4.cvn), channel_id=1, source_target_pairs={{0,1},{1,0},{2,3},{3,2},{4,5},{5,4},{6,7},{7,6},{8,9},{9,8},{10,11... | collective-permute-start | bytes 798728 | tf_op jit(solution)/shard_map/ppermute | solution.py:36
  42.5 8.2 %collective-permute-start.10 = (bf16[512,128]{1,0:T(8,128)(2,1)S(1)}, bf16[512,128]{1,0:T(8,128)(2,1)S(1)}, u32[]{:S(2)}, u32[]{:S(2)}) collective-permute-start(bf16[512,128]{1,0:T(8,128)(2,1)S(1)} %pad_maximum_fusion), channel_id=1, source_target_pairs={{0,0},{8,8},{16,16},{24,24},{40,32},{48,40},{56,48},{32,56},{80,64... | collective-permute-start | bytes 393224 | tf_op jit(solution)/shard_map/ppermute | solution.py:327
  54.9 5.0 %copy-start.11 = (s32[2048]{0:T(1024)S(1)}, s32[2048]{0:T(1024)}, u32[]{:S(2)}) copy-start(s32[2048]{0:T(1024)} %param.15) | copy-start | bytes 24580
  54.9 5.0 %copy-start.12 = (s32[2048]{0:T(1024)S(1)}, s32[2048]{0:T(1024)}, u32[]{:S(2)}) copy-start(s32[2048]{0:T(1024)} %param.14) | copy-start | bytes 24580
  54.9 19.9 %all-to-all-start.1 = ((s16[8,144,128]{2,1,0:T(8,128)(2,1)}), s16[8,144,128]{2,1,0:T(8,128)(2,1)S(1)}, u32[]{:S(2)}, u32[]{:S(2)}) async-start(s16[8,144,128]{2,1,0:T(8,128)(2,1)} %second.1.refs_1_), calls=%async_computation.1 | async-start | bytes 589824 | tf_op jit(solution)/shard_map/all_to_all | solution.py:379
  63.4 5.7 %collective-permute-start.13 = (bf16[256,128]{1,0:T(8,128)(2,1)}, bf16[256,128]{1,0:T(8,128)(2,1)S(1)}, u32[]{:S(2)}, u32[]{:S(2)}) collective-permute-start(bf16[256,128]{1,0:T(8,128)(2,1)} %get-tuple-element.13), channel_id=1, source_target_pairs={{0,8},{8,16},{16,24},{24,0},{1,9},{9,17},{17,25},{25,1},{2,10},{10... | collective-permute-start | bytes 196616 | tf_op jit(solution)/shard_map/ppermute | solution.py:31
  64.2 5.6 %collective-permute-start.14 = (bf16[256,128]{1,0:T(8,128)(2,1)}, bf16[256,128]{1,0:T(8,128)(2,1)S(1)}, u32[]{:S(2)}, u32[]{:S(2)}) collective-permute-start(bf16[256,128]{1,0:T(8,128)(2,1)} %get-tuple-element.14), channel_id=1, source_target_pairs={{0,24},{8,0},{16,8},{24,16},{1,25},{9,1},{17,9},{25,17},{2,26},{10... | collective-permute-start | bytes 196616 | tf_op jit(solution)/shard_map/ppermute | solution.py:31
  66.7 6.0 %collective-permute-start.15 = (bf16[256,128]{1,0:T(8,128)(2,1)}, bf16[256,128]{1,0:T(8,128)(2,1)S(1)}, u32[]{:S(2)}, u32[]{:S(2)}) collective-permute-start(bf16[256,128]{1,0:T(8,128)(2,1)} %get-tuple-element.15), channel_id=1, source_target_pairs={{0,16},{8,24},{16,0},{24,8},{1,17},{9,25},{17,1},{25,9},{2,18},{10... | collective-permute-start | bytes 196616 | tf_op jit(solution)/shard_map/ppermute | solution.py:31
  69.1 3.5 %copy-start.8 = (bf16[256,128]{1,0:T(8,128)(2,1)}, bf16[256,128]{1,0:T(8,128)(2,1)S(1)}, u32[]{:S(2)}) copy-start(bf16[256,128]{1,0:T(8,128)(2,1)S(1)} %collective-permute-done.13.n1) | copy-start | bytes 196612
  69.8 2.9 %copy-start.9 = (bf16[256,128]{1,0:T(8,128)(2,1)}, bf16[256,128]{1,0:T(8,128)(2,1)S(1)}, u32[]{:S(2)}) copy-start(bf16[256,128]{1,0:T(8,128)(2,1)S(1)} %collective-permute-done.14.n2) | copy-start | bytes 196612
  72.7 0.6 copy-start.10
  74.9 0.7 copy-start.3

commit v2 on v1

--- a/solution.py
+++ b/solution.py
@@ -126,6 +126,25 @@
         out[b, 0:BLOCK, :] = queries[...]
         out[b, BLOCK : BLOCK + 16, :] = near[...]
         out[b, BLOCK + 16 : SENT, :] = far[...]
+
+
+def rows_kernel(q3, af, bf, out):
+    for b in range(8):
+        out[b * 32 : b * 32 + 32, :] = q3[b, BLOCK:SENT, :]
+
+
+def select_kernel(r0, r1, r2, r3, out):
+    z = lax.axis_index("z")
+
+    @pl.when(z < 4)
+    def _():
+        out[0:256, :] = r0[...]
+        out[256:512, :] = r3[...]
+
+    @pl.when(z >= 4)
+    def _():
+        out[0:256, :] = r1[...]
+        out[256:512, :] = r2[...]
 
 
 def first_kernel(
@@ -198,7 +217,8 @@
         total[rows, :] = total_in[rows, :] * factor
         acc[rows, :] = acc_in[rows, :] * factor
     weigh_pages(
-        scores, level, total, acc, 0, mask, lambda p: [page_parts(cvn, p), page_parts(cvf, p)]
+        scores, level, total, acc, 0, mask,
+        lambda p: [page_parts(cvn, p), page_parts(cvf, p)],
     )
     weigh(lambda rows: fresh[rows, :], values, level, total, acc, 256)
 
@@ -237,7 +257,7 @@
     out[...] = total.astype(BF16)
 
 
-def route_kernel(r0, r1, r2, r3, code, o0, o1, o2, o3):
+def route_kernel(r0, r1, r2, r3, code, payload, o0, o1, o2, o3):
     z, x, y, core = here()
     target = lax.broadcasted_iota(I32, (4 * 256, 256), 0)
     lane = lax.broadcasted_iota(I32, (4 * 256, 256), 1)
@@ -259,18 +279,7 @@
     out[...] = total.astype(BF16)
 
 
-def after(value, *others):
-    def kernel(*refs):
-        pass
-
-    return pl.pallas_call(
-        kernel,
-        out_shape=jax.ShapeDtypeStruct(value.shape, value.dtype),
-        in_specs=[pl.BlockSpec(memory_space=pl.ANY)] * (1 + len(others)),
-        out_specs=pl.BlockSpec(memory_space=pl.ANY),
-        input_output_aliases={0: 0},
-        name="after",
-    )(value, *others)
+SMALL = pltpu.CompilerParams(vmem_limit_bytes=8 * 1024 * 1024)
 
 
 def smem():
@@ -315,21 +324,22 @@
         out_shape=jax.ShapeDtypeStruct((8, SENT, HD), BF16),
         in_specs=[vmem()] * 3,
         out_specs=vmem(),
+        compiler_params=SMALL,
         name="gather",
     )(queries.reshape(BLOCK, HD), near, far)
     q3 = lax.all_to_all(sent, "z", 0, 0)
-    rows = q3[:, BLOCK:, :].reshape(256, HD)
+    rows = pl.pallas_call(
+        rows_kernel,
+        out_shape=jax.ShapeDtypeStruct((256, HD), BF16),
+        in_specs=[vmem()] * 3,
+        out_specs=vmem(),
+        compiler_params=SMALL,
+        name="rows",
+    )(q3, af, bf)
     rows = [rows, shifted(rows, "y", 1), shifted(rows, "y", -1), shifted(rows, "y", 2)]
-    lower = z < 4
-    new = jnp.concatenate(
-        [jnp.where(lower, rows[0], rows[1]), jnp.where(lower, rows[3], rows[2])], axis=0
-    )
-    new = lax.ppermute(
-        new, ("z", "x"), [(p * 4 + (i + p) % 4, p * 4 + i) for p in range(8) for i in range(4)]
-    )
 
     state = jax.ShapeDtypeStruct((QROWS, HD), F32)
-    params = pltpu.CompilerParams(vmem_limit_bytes=48 * 1024 * 1024)
+    params = pltpu.CompilerParams(vmem_limit_bytes=50 * 1024 * 1024)
     level, total, acc = pl.pallas_call(
         first_kernel,
         out_shape=(state,) * 3,
@@ -341,9 +351,20 @@
             pltpu.VMEM((QROWS, HD), F32),
         ],
         compiler_params=params,
-        cost_estimate=cost(6),
+        cost_estimate=cost(8),
         name="first",
     )(page_table, page_count, q3, cache_keys, cache_values, an, af, bn, bf)
+    new = pl.pallas_call(
+        select_kernel,
+        out_shape=jax.ShapeDtypeStruct((512, HD), BF16),
+        in_specs=[vmem()] * 4,
+        out_specs=vmem(),
+        compiler_params=SMALL,
+        name="select",
+    )(*rows)
+    new = lax.ppermute(
+        new, ("z", "x"), [(p * 4 + (i + p) % 4, p * 4 + i) for p in range(8) for i in range(4)]
+    )
     payload = pl.pallas_call(
         second_kernel,
         out_shape=jax.ShapeDtypeStruct((8, PAYLOAD, HD), jnp.int16),
@@ -356,7 +377,7 @@
         ]
         + [pltpu.VMEM((QROWS, HD), F32)] * 4,
         compiler_params=params,
-        cost_estimate=cost(2),
+        cost_estimate=cost(1),
         name="second",
     )(q3, ckn, cvn, ckf, cvf, new, level, total, acc)
 
@@ -364,15 +385,15 @@
     code = lax.dynamic_index_in_dim(code, x, 1, keepdims=False)
     code = jnp.where(core == 1, jnp.flip(code, 2), code)
     code = jnp.repeat(jnp.transpose(code, (1, 0, 2, 3)).reshape(4, 128), 2, axis=1)
-    code = after(code, payload)
     piece = jax.ShapeDtypeStruct((256, HD), BF16)
     t0, to_after, to_opposite, to_before = pl.pallas_call(
         route_kernel,
         out_shape=(piece,) * 4,
-        in_specs=[vmem()] * 5,
+        in_specs=[vmem()] * 5 + [pl.BlockSpec(memory_space=pl.ANY)],
         out_specs=(vmem(),) * 4,
+        compiler_params=SMALL,
         name="route",
-    )(*rows, code)
+    )(*rows, code, payload)
     t1 = shifted(to_after, "x", 1)
     t2 = shifted(to_before, "x", -1)
     t3 = shifted(to_opposite, "x", 2)
@@ -382,6 +403,7 @@
         out_shape=jax.ShapeDtypeStruct((BLOCK, HD), BF16),
         in_specs=[vmem()],
         out_specs=vmem(),
+        compiler_params=SMALL,
         name="merge",
     )(parts)
     appended = pl.pallas_call(
@@ -389,6 +411,7 @@
         out_shape=jax.ShapeDtypeStruct((256, HD), BF16),
         in_specs=[vmem()] * 4,
         out_specs=vmem(),
+        compiler_params=SMALL,
         name="place",
     )(t0, t1, t2, t3)
     return attended.reshape(queries.shape), appended.reshape(BLOCK, 2, HD)

time: 78.6 us -> 71.1 us (0.905)
  Pallas kernels: 18.9 us -> 14.5 us
  waiting for transfers between devices: 21.2 us -> 17.2 us
  local copies, waits for them, and re-layouts: 4.22 us -> 5.09 us
    all_to_all x1, waiting for transfers between devices: 11.1 us -> 6.46 us  [shards(): q3 = lax.all_to_all(sent, 'z', 0, 0)]
    slice x2, local copies, waits for them, and re-layouts: 0.04 us -> 2.67 us  [shards(): ckn, cvn = (shifted(an[:SIDE], 'x', 1), shifted(bn[SIDE:], 'x', -1))]
    ppermute x10, waiting for transfers between devices: 10.1 us -> 7.61 us  [shifted(): lax.ppermute(value, axis, [(i, (i + steps) % count) for i in range(count)])]
    all_to_all x1, waiting for transfers between devices: 0.01 us -> 1.97 us  [shards(): parts = lax.all_to_all(payload, 'z', 0, 0)]
    pallas_call x1, Pallas kernels: 2.33 us -> 0.76 us  [shards(): pl.pallas_call(route_kernel, out_shape=(piece,) * 4, in_specs=[vmem()] *...]
    ppermute x5, waiting for transfers between devices: 0.01 us -> 1.17 us  [swapped(): return lax.ppermute(value, axis, [(i, i ^ bit) for i in range(count)])]
    unnamed x28 -> x16, local copies, waits for them, and re-layouts: 1.98 us -> 0.82 us
    pallas_call x1, Pallas kernels: 1.95 us -> 0.99 us  [shards(): pl.pallas_call(merge_kernel, out_shape=jax.ShapeDtypeStruct((BLOCK, HD),...]
  transfers between devices with their start and end apart: 18 -> 18, of which waited for: 8 -> 9; matrix products, arithmetic and copies ran while one was open for 4% -> 5% of each run, Pallas kernels for 14% -> 13%
where the time goes in v2:
time: 71.1 us; the launch traced here: 69.9 us
  starting transfers between devices  30.9 us (43%)
  waiting for transfers between devices  17.2 us (24%)
  Pallas kernels  14.5 us (20%)
  local copies, waits for them, and re-layouts  5.09 us (7%)
  between operations  1.49 us (2%)
    ppermute x10, starting transfers between devices, shifted(): lax.ppermute(value, axis, [(i, (i + steps) % count) for i in range(count)])  15.5 us
    all_to_all x1, starting transfers between devices, shards(): q3 = lax.all_to_all(sent, 'z', 0, 0)  8.47 us
    ppermute x10, waiting for transfers between devices, shifted(): lax.ppermute(value, axis, [(i, (i + steps) % count) for i in range(count)])  7.61 us
    pallas_call x1, Pallas kernels, shards(): pl.pallas_call(first_kernel, out_shape=(state,) * 3, in_specs=[smem()] *...  7.14 us
    all_to_all x1, waiting for transfers between devices, shards(): q3 = lax.all_to_all(sent, 'z', 0, 0)  6.46 us
    all_to_all x1, starting transfers between devices, shards(): parts = lax.all_to_all(payload, 'z', 0, 0)  5.01 us
    pallas_call x1, Pallas kernels, shards(): pl.pallas_call(second_kernel, out_shape=jax.ShapeDtypeStruct((8, PAYLOAD,...  4.18 us
    slice x2, local copies, waits for them, and re-layouts, shards(): ckn, cvn = (shifted(an[:SIDE], 'x', 1), shifted(bn[SIDE:], 'x', -1))  2.67 us
  transfers between devices with their start and end apart: 18, of which 9 were waited for; matrix products, arithmetic and copies ran while one was open for 5% of the time, Pallas kernels for 13%

profile of v2, /device:TPU:8, one launch (start us, length us, event | category | flops | bytes accessed | tf_op | source)
XLA Modules:
  0.0 69.9 jit_solution(10341820918143384097)
XLA Ops:
  1.3 0.7 fusion.3
  1.9 1.1 %constant_dynamic-slice_fusion.1 = (bf16[4,1,256,128]{3,2,1,0:T(8,128)(2,1)S(1)}, bf16[4,1,256,128]{3,2,1,0:T(8,128)(2,1)S(1)}) fusion(bf16[4,2,256,128]{3,2,1,0:T(8,128)(2,1)} %bitcast.21, s32[]{:T(128)S(6)} %select_n.22, bf16[4,2,256,128]{3,2,1,0:T(8,128)(2,1)} %bitcast.22), kind=kLoop, calls=%fused_computation.9 | loop fusion | bytes 1048580 | tf_op jit(solution)/shard_map/jit(dynamic_index_in_dim)/dynamic_slice | solution.py:310
  3.0 0.0 copy-start.4
  3.0 0.0 copy-start.3
  3.1 1.6 %collective-permute-start.1 = (bf16[2064,128]{1,0:T(8,128)(2,1)S(1)}, bf16[2064,128]{1,0:T(8,128)(2,1)}, u32[]{:S(2)}, u32[]{:S(2)}) collective-permute-start(bf16[2064,128]{1,0:T(8,128)(2,1)S(1)} %fusion.1), channel_id=1, source_target_pairs={{0,8},{8,16},{16,24},{24,0},{1,9},{9,17},{17,25},{25,1},{2,10},{10... | collective-permute-start | bytes 1585160 | tf_op jit(solution)/shard_map/ppermute | solution.py:31
  4.6 1.7 %collective-permute-start.3 = (bf16[2064,128]{1,0:T(8,128)(2,1)S(1)}, bf16[2064,128]{1,0:T(8,128)(2,1)}, u32[]{:S(2)}, u32[]{:S(2)}) collective-permute-start(bf16[2064,128]{1,0:T(8,128)(2,1)S(1)} %fusion.1), channel_id=1, source_target_pairs={{0,24},{8,0},{16,8},{24,16},{1,25},{9,1},{17,9},{25,17},{2,26},{10... | collective-permute-start | bytes 1585160 | tf_op jit(solution)/shard_map/ppermute | solution.py:31
  6.4 0.0 collective-permute-start
  6.4 1.2 %collective-permute-done.far = bf16[16,128]{1,0:T(8,128)(2,1)S(1)} collective-permute-done((bf16[16,128]{1,0:T(8,128)(2,1)S(1)}, bf16[16,128]{1,0:T(8,128)(2,1)S(1)}, u32[]{:S(2)}, u32[]{:S(2)}) %collective-permute-start) | collective-permute-done | bytes 4128 | tf_op jit(solution)/shard_map/ppermute | solution.py:36
  7.6 0.8 %gather.1 = bf16[8,160,128]{2,1,0:T(8,128)(2,1)} custom-call(bf16[128,128]{1,0:T(8,128)(2,1)S(1)} %bitcast.23, bf16[16,128]{1,0:T(8,128)(2,1)S(1)} %bitcast.25, bf16[16,128]{1,0:T(8,128)(2,1)S(1)} %collective-permute-done.far), custom_call_target="tpu_custom_call" | custom-call | tf_op jit(solution)/shard_map/gather/pallas_call | solution.py:322
  8.3 8.5 %all-to-all-start = ((bf16[8,160,128]{2,1,0:T(8,128)(2,1)}), bf16[8,160,128]{2,1,0:T(8,128)(2,1)S(1)}, u32[]{:S(2)}, u32[]{:S(2)}) async-start(bf16[8,160,128]{2,1,0:T(8,128)(2,1)} %gather.1), calls=%async_computation | async-start | bytes 655360 | tf_op jit(solution)/shard_map/all_to_all | solution.py:330
  16.8 1.4 %collective-permute-done.1.an = bf16[2064,128]{1,0:T(8,128)(2,1)} collective-permute-done((bf16[2064,128]{1,0:T(8,128)(2,1)S(1)}, bf16[2064,128]{1,0:T(8,128)(2,1)}, u32[]{:S(2)}, u32[]{:S(2)}) %collective-permute-start.1) | collective-permute-done | bytes 528416 | tf_op jit(solution)/shard_map/ppermute | solution.py:31
  18.2 0.0 collective-permute-start.7
  18.2 0.0 collective-permute-done.3.bn
  18.2 0.5 collective-permute-start.8
  18.7 1.0 %slice.9 = bf16[1040,128]{1,0:T(8,128)(2,1)S(1)} slice(bf16[2064,128]{1,0:T(8,128)(2,1)} %collective-permute-done.3.bn), slice={[1024:2064], [0:128]} | slice | bytes 532480 | tf_op jit(solution)/shard_map/slice | solution.py:317
  19.7 2.5 %collective-permute-start.4 = (bf16[1040,128]{1,0:T(8,128)(2,1)S(1)}, bf16[1040,128]{1,0:T(8,128)(2,1)S(1)}, u32[]{:S(2)}, u32[]{:S(2)}) collective-permute-start(bf16[1040,128]{1,0:T(8,128)(2,1)S(1)} %slice.9), channel_id=1, source_target_pairs={{0,24},{8,0},{16,8},{24,16},{1,25},{9,1},{17,9},{25,17},{2,26},{10... | collective-permute-start | bytes 798728 | tf_op jit(solution)/shard_map/ppermute | solution.py:31
  22.2 1.7 %slice.8 = bf16[1024,128]{1,0:T(8,128)(2,1)} slice(bf16[2064,128]{1,0:T(8,128)(2,1)} %collective-permute-done.1.an), slice={[0:1024], [0:128]} | slice | bytes 524288 | tf_op jit(solution)/shard_map/slice | solution.py:317
  23.9 0.0 collective-permute-start.2
  24.0 6.5 %all-to-all-done.q3 = bf16[8,160,128]{2,1,0:T(8,128)(2,1)S(1)} async-done(((bf16[8,160,128]{2,1,0:T(8,128)(2,1)}), bf16[8,160,128]{2,1,0:T(8,128)(2,1)S(1)}, u32[]{:S(2)}, u32[]{:S(2)}) %all-to-all-start) | async-done | bytes 327712 | tf_op jit(solution)/shard_map/all_to_all | solution.py:330
  30.4 0.0 collective-permute-done.7.af
  30.4 0.0 collective-permute-done.8.bf
  30.4 0.8 %copy-done = bf16[2064,128]{1,0:T(8,128)(2,1)} copy-done((bf16[2064,128]{1,0:T(8,128)(2,1)}, bf16[2064,128]{1,0:T(8,128)(2,1)S(1)}, u32[]{:S(2)}) %copy-start) | copy-done | bytes 528408
  31.2 0.4 collective-permute-start.10
  31.7 2.6 %collective-permute-start.11 = (bf16[256,128]{1,0:T(8,128)(2,1)S(1)}, bf16[256,128]{1,0:T(8,128)(2,1)S(1)}, u32[]{:S(2)}, u32[]{:S(2)}) collective-permute-start(bf16[256,128]{1,0:T(8,128)(2,1)S(1)} %rows.1.r0), channel_id=1, source_target_pairs={{0,4},{2,6},{4,0},{6,2},{1,5},{3,7},{5,1},{7,3},{8,12},{10,14},{12... | collective-permute-start | bytes 196616 | tf_op jit(solution)/shard_map/ppermute | solution.py:31
  34.3 1.9 %collective-permute-start.9 = (bf16[256,128]{1,0:T(8,128)(2,1)S(1)}, bf16[256,128]{1,0:T(8,128)(2,1)S(1)}, u32[]{:S(2)}, u32[]{:S(2)}) collective-permute-start(bf16[256,128]{1,0:T(8,128)(2,1)S(1)} %rows.1.r0), channel_id=1, source_target_pairs={{0,2},{2,4},{4,6},{6,0},{1,3},{3,5},{5,7},{7,1},{8,10},{10,12},{12... | collective-permute-start | bytes 196616 | tf_op jit(solution)/shard_map/ppermute | solution.py:31
  36.2 0.0 collective-permute-done.2.ckn
  36.2 0.5 collective-permute-start.5
  36.7 0.9 %collective-permute-done.11.r3 = bf16[256,128]{1,0:T(8,128)(2,1)S(1)} collective-permute-done((bf16[256,128]{1,0:T(8,128)(2,1)S(1)}, bf16[256,128]{1,0:T(8,128)(2,1)S(1)}, u32[]{:S(2)}, u32[]{:S(2)}) %collective-permute-start.11) | collective-permute-done | bytes 65568 | tf_op jit(solution)/shard_map/ppermute | solution.py:31
  37.6 1.0 %collective-permute-done.9.r1 = bf16[256,128]{1,0:T(8,128)(2,1)S(1)} collective-permute-done((bf16[256,128]{1,0:T(8,128)(2,1)S(1)}, bf16[256,128]{1,0:T(8,128)(2,1)S(1)}, u32[]{:S(2)}, u32[]{:S(2)}) %collective-permute-start.9) | collective-permute-done | bytes 65568 | tf_op jit(solution)/shard_map/ppermute | solution.py:31
  38.6 0.8 %collective-permute-start.12 = (bf16[512,128]{1,0:T(8,128)(2,1)S(1)}, bf16[512,128]{1,0:T(8,128)(2,1)S(1)}, u32[]{:S(2)}, u32[]{:S(2)}) collective-permute-start(bf16[512,128]{1,0:T(8,128)(2,1)S(1)} %select.6), channel_id=1, source_target_pairs={{0,0},{8,8},{16,16},{24,24},{40,32},{48,40},{56,48},{32,56},{80,64... | collective-permute-start | bytes 393224 | tf_op jit(solution)/shard_map/ppermute | solution.py:365
  39.4 7.1 %first.1 = (f32[1024,128]{1,0:T(8,128)S(1)}, f32[1024,128]{1,0:T(8,128)S(1)}, f32[1024,128]{1,0:T(8,128)S(1)}) custom-call(s32[1,4]{1,0:T(1,128)S(1)} %copy-done.5, s32[1]{0:T(128)} %copy.31.live, bf16[8,160,128]{2,1,0:T(8,128)(2,1)S(1)} %all-to-all-done.q3, bf16[2048,128]{1,0:T(8,128)(2,1)S(1)} %copy-done.2, bf16[2048,128]{1,0:T(8,128)(2,1)S(1)} %copy-done.1, ...), custom_call_target="tpu_custom_call" | custom-call | flops 2147483648 | bytes 1048576 | tf_op jit(solution)/shard_map/first/pallas_call | solution.py:343
  46.6 0.0 collective-permute-done.6.cvf
  46.6 0.0 collective-permute-done.12.new
  46.6 4.2 %second.1.payload = s16[8,144,128]{2,1,0:T(8,128)(2,1)} custom-call(bf16[8,160,128]{2,1,0:T(8,128)(2,1)S(1)} %all-to-all-done.q3, bf16[1024,128]{1,0:T(8,128)(2,1)S(1)} %collective-permute-done.2.ckn, bf16[1040,128]{1,0:T(8,128)(2,1)S(1)} %collective-permute-done.4.cvn, bf16[1024,128]{1,0:T(8,128)(2,1)S(1)} %collective-permute-done.5.ckf, ...), custom_call_target="tpu_custom_call" | custom-call | flops 268435456 | bytes 1048576 | tf_op jit(solution)/shard_map/second/pallas_call | solution.py:368
  50.8 5.0 %all-to-all-start.1 = ((s16[8,144,128]{2,1,0:T(8,128)(2,1)}), s16[8,144,128]{2,1,0:T(8,128)(2,1)S(1)}, u32[]{:S(2)}, u32[]{:S(2)}) async-start(s16[8,144,128]{2,1,0:T(8,128)(2,1)} %second.1.payload), calls=%async_computation.1 | async-start | bytes 589824 | tf_op jit(solution)/shard_map/all_to_all | solution.py:400
  55.8 0.2 reshape.53
  56.1 0.2 copy.25
  56.3 0.1 copy.24.code
  56.4 0.8 %route.1 = (bf16[256,128]{1,0:T(8,128)(2,1)S(1)}, bf16[256,128]{1,0:T(8,128)(2,1)S(1)}, bf16[256,128]{1,0:T(8,128)(2,1)S(1)}, bf16[256,128]{1,0:T(8,128)(2,1)S(1)}) custom-call(bf16[256,128]{1,0:T(8,128)(2,1)S(1)} %rows.1.r0, bf16[256,128]{1,0:T(8,128)(2,1)S(1)} %collective-permute-done.9.r1, bf16[256,128]{1,0:T(8,128)(2,1)S(1)} %collective-permute-done.10.r2, ...), custom_call_target="tpu_custom_call" | custom-call | tf_op jit(solution)/shard_map/route/pallas_call | solution.py:389
  57.2 1.6 %collective-permute-start.13 = (bf16[256,128]{1,0:T(8,128)(2,1)S(1)}, bf16[256,128]{1,0:T(8,128)(2,1)S(1)}, u32[]{:S(2)}, u32[]{:S(2)}) collective-permute-start(bf16[256,128]{1,0:T(8,128)(2,1)S(1)} %get-tuple-element.13), channel_id=1, source_target_pairs={{0,8},{8,16},{16,24},{24,0},{1,9},{9,17},{17,25},{25,1},{2,10},{10... | collective-permute-start | bytes 196616 | tf_op jit(solution)/shard_map/ppermute | solution.py:31
  58.8 1.7 %collective-permute-start.14 = (bf16[256,128]{1,0:T(8,128)(2,1)S(1)}, bf16[256,128]{1,0:T(8,128)(2,1)S(1)}, u32[]{:S(2)}, u32[]{:S(2)}) collective-permute-start(bf16[256,128]{1,0:T(8,128)(2,1)S(1)} %get-tuple-element.14), channel_id=1, source_target_pairs={{0,24},{8,0},{16,8},{24,16},{1,25},{9,1},{17,9},{25,17},{2,26},{10... | collective-permute-start | bytes 196616 | tf_op jit(solution)/shard_map/ppermute | solution.py:31
  60.5 1.4 %collective-permute-start.15 = (bf16[256,128]{1,0:T(8,128)(2,1)S(1)}, bf16[256,128]{1,0:T(8,128)(2,1)S(1)}, u32[]{:S(2)}, u32[]{:S(2)}) collective-permute-start(bf16[256,128]{1,0:T(8,128)(2,1)S(1)} %get-tuple-element.15), channel_id=1, source_target_pairs={{0,16},{8,24},{16,0},{24,8},{1,17},{9,25},{17,1},{25,9},{2,18},{10... | collective-permute-start | bytes 196616 | tf_op jit(solution)/shard_map/ppermute | solution.py:31
  62.0 0.8 %collective-permute-done.13.n1 = bf16[256,128]{1,0:T(8,128)(2,1)S(1)} collective-permute-done((bf16[256,128]{1,0:T(8,128)(2,1)S(1)}, bf16[256,128]{1,0:T(8,128)(2,1)S(1)}, u32[]{:S(2)}, u32[]{:S(2)}) %collective-permute-start.13) | collective-permute-done | bytes 65568 | tf_op jit(solution)/shard_map/ppermute | solution.py:31
  62.7 0.5 collective-permute-done.14.n2
  63.3 3.0 %collective-permute-done.15.n3 = bf16[256,128]{1,0:T(8,128)(2,1)S(1)} collective-permute-done((bf16[256,128]{1,0:T(8,128)(2,1)S(1)}, bf16[256,128]{1,0:T(8,128)(2,1)S(1)}, u32[]{:S(2)}, u32[]{:S(2)}) %collective-permute-start.15) | collective-permute-done | bytes 65568 | tf_op jit(solution)/shard_map/ppermute | solution.py:31
  66.3 0.7 place.1
  66.9 2.0 %all-to-all-done.1.parts = s16[8,144,128]{2,1,0:T(8,128)(2,1)S(1)} async-done(((s16[8,144,128]{2,1,0:T(8,128)(2,1)}), s16[8,144,128]{2,1,0:T(8,128)(2,1)S(1)}, u32[]{:S(2)}, u32[]{:S(2)}) %all-to-all-start.1) | async-done | bytes 294944 | tf_op jit(solution)/shard_map/all_to_all | solution.py:400
  68.9 1.0 %merge.1 = bf16[128,128]{1,0:T(8,128)(2,1)} custom-call(s16[8,144,128]{2,1,0:T(8,128)(2,1)S(1)} %all-to-all-done.1.parts), custom_call_target="tpu_custom_call" | custom-call | tf_op jit(solution)/shard_map/merge/pallas_call | solution.py:401
  (25 shorter events, 0.2 us)
Async XLA Ops:
  3.0 3.4 %copy-start.4 = (bf16[8,2,128]{2,1,0:T(2,128)(2,1)S(1)}, bf16[8,2,128]{2,1,0:T(2,128)(2,1)}, u32[]{:S(2)}) copy-start(bf16[8,2,128]{2,1,0:T(2,128)(2,1)} %param.13) | copy-start | bytes 12292
  3.0 4.5 %copy-start.3 = (bf16[64,2,128]{2,1,0:T(2,128)(2,1)S(1)}, bf16[64,2,128]{2,1,0:T(2,128)(2,1)}, u32[]{:S(2)}) copy-start(bf16[64,2,128]{2,1,0:T(2,128)(2,1)} %param.8) | copy-start | bytes 98308
  3.1 15.1 %collective-permute-start.1 = (bf16[2064,128]{1,0:T(8,128)(2,1)S(1)}, bf16[2064,128]{1,0:T(8,128)(2,1)}, u32[]{:S(2)}, u32[]{:S(2)}) collective-permute-start(bf16[2064,128]{1,0:T(8,128)(2,1)S(1)} %fusion.1), channel_id=1, source_target_pairs={{0,8},{8,16},{16,24},{24,0},{1,9},{9,17},{17,25},{25,1},{2,10},{10... | collective-permute-start | bytes 1585160 | tf_op jit(solution)/shard_map/ppermute | solution.py:31
  4.6 13.6 %collective-permute-start.3 = (bf16[2064,128]{1,0:T(8,128)(2,1)S(1)}, bf16[2064,128]{1,0:T(8,128)(2,1)}, u32[]{:S(2)}, u32[]{:S(2)}) collective-permute-start(bf16[2064,128]{1,0:T(8,128)(2,1)S(1)} %fusion.1), channel_id=1, source_target_pairs={{0,24},{8,0},{16,8},{24,16},{1,25},{9,1},{17,9},{25,17},{2,26},{10... | collective-permute-start | bytes 1585160 | tf_op jit(solution)/shard_map/ppermute | solution.py:31
  6.4 1.2 %collective-permute-start = (bf16[16,128]{1,0:T(8,128)(2,1)S(1)}, bf16[16,128]{1,0:T(8,128)(2,1)S(1)}, u32[]{:S(2)}, u32[]{:S(2)}) collective-permute-start(bf16[16,128]{1,0:T(8,128)(2,1)S(1)} %bitcast.24), channel_id=1, source_target_pairs={{0,1},{1,0},{2,3},{3,2},{4,5},{5,4},{6,7},{7,6},{8,9},{9,8},{10,11... | collective-permute-start | bytes 12296 | tf_op jit(solution)/shard_map/ppermute | solution.py:36
  8.3 22.1 %all-to-all-start = ((bf16[8,160,128]{2,1,0:T(8,128)(2,1)}), bf16[8,160,128]{2,1,0:T(8,128)(2,1)S(1)}, u32[]{:S(2)}, u32[]{:S(2)}) async-start(bf16[8,160,128]{2,1,0:T(8,128)(2,1)} %gather.1), calls=%async_computation | async-start | bytes 655360 | tf_op jit(solution)/shard_map/all_to_all | solution.py:330
  18.2 12.2 %collective-permute-start.7 = (bf16[2064,128]{1,0:T(8,128)(2,1)}, bf16[2064,128]{1,0:T(8,128)(2,1)S(1)}, u32[]{:S(2)}, u32[]{:S(2)}) collective-permute-start(bf16[2064,128]{1,0:T(8,128)(2,1)} %collective-permute-done.1.an), channel_id=1, source_target_pairs={{0,1},{1,0},{2,3},{3,2},{4,5},{5,4},{6,7},{7,6},{8,9},{9,8},{10,11... | collective-permute-start | bytes 1585160 | tf_op jit(solution)/shard_map/ppermute | solution.py:36
  18.2 12.2 %collective-permute-start.8 = (bf16[2064,128]{1,0:T(8,128)(2,1)}, bf16[2064,128]{1,0:T(8,128)(2,1)S(1)}, u32[]{:S(2)}, u32[]{:S(2)}) collective-permute-start(bf16[2064,128]{1,0:T(8,128)(2,1)} %collective-permute-done.3.bn), channel_id=1, source_target_pairs={{0,1},{1,0},{2,3},{3,2},{4,5},{5,4},{6,7},{7,6},{8,9},{9,8},{10,11... | collective-permute-start | bytes 1585160 | tf_op jit(solution)/shard_map/ppermute | solution.py:36
  19.7 16.4 %collective-permute-start.4 = (bf16[1040,128]{1,0:T(8,128)(2,1)S(1)}, bf16[1040,128]{1,0:T(8,128)(2,1)S(1)}, u32[]{:S(2)}, u32[]{:S(2)}) collective-permute-start(bf16[1040,128]{1,0:T(8,128)(2,1)S(1)} %slice.9), channel_id=1, source_target_pairs={{0,24},{8,0},{16,8},{24,16},{1,25},{9,1},{17,9},{25,17},{2,26},{10... | collective-permute-start | bytes 798728 | tf_op jit(solution)/shard_map/ppermute | solution.py:31
  23.9 15.5 %copy-start.1 = (bf16[2048,128]{1,0:T(8,128)(2,1)S(1)}, bf16[2048,128]{1,0:T(8,128)(2,1)}, u32[]{:S(2)}) copy-start(bf16[2048,128]{1,0:T(8,128)(2,1)} %ov.1) | copy-start | bytes 1572868
  23.9 15.5 %copy-start.2 = (bf16[2048,128]{1,0:T(8,128)(2,1)S(1)}, bf16[2048,128]{1,0:T(8,128)(2,1)}, u32[]{:S(2)}) copy-start(bf16[2048,128]{1,0:T(8,128)(2,1)} %ok.1) | copy-start | bytes 1572868
  23.9 15.5 %copy-start.5 = (s32[1,4]{1,0:T(1,128)S(1)}, s32[1,4]{1,0:T(1,128)}, u32[]{:S(2)}) copy-start(s32[1,4]{1,0:T(1,128)} %table.1) | copy-start | bytes 52
  23.9 12.2 %collective-permute-start.2 = (bf16[1024,128]{1,0:T(8,128)(2,1)}, bf16[1024,128]{1,0:T(8,128)(2,1)S(1)}, u32[]{:S(2)}, u32[]{:S(2)}) collective-permute-start(bf16[1024,128]{1,0:T(8,128)(2,1)} %slice.8), channel_id=1, source_target_pairs={{0,8},{8,16},{16,24},{24,0},{1,9},{9,17},{17,25},{25,1},{2,10},{10... | collective-permute-start | bytes 786440 | tf_op jit(solution)/shard_map/ppermute | solution.py:31
  30.4 0.8 %copy-start = (bf16[2064,128]{1,0:T(8,128)(2,1)}, bf16[2064,128]{1,0:T(8,128)(2,1)S(1)}, u32[]{:S(2)}) copy-start(bf16[2064,128]{1,0:T(8,128)(2,1)S(1)} %collective-permute-done.8.bf) | copy-start | bytes 1585156
  31.2 5.4 %collective-permute-start.10 = (bf16[256,128]{1,0:T(8,128)(2,1)S(1)}, bf16[256,128]{1,0:T(8,128)(2,1)S(1)}, u32[]{:S(2)}, u32[]{:S(2)}) collective-permute-start(bf16[256,128]{1,0:T(8,128)(2,1)S(1)} %rows.1.r0), channel_id=1, source_target_pairs={{0,6},{2,0},{4,2},{6,4},{1,7},{3,1},{5,3},{7,5},{8,14},{10,8},{12,... | collective-permute-start | bytes 196616 | tf_op jit(solution)/shard_map/ppermute | solution.py:31
  31.7 5.9 %collective-permute-start.11 = (bf16[256,128]{1,0:T(8,128)(2,1)S(1)}, bf16[256,128]{1,0:T(8,128)(2,1)S(1)}, u32[]{:S(2)}, u32[]{:S(2)}) collective-permute-start(bf16[256,128]{1,0:T(8,128)(2,1)S(1)} %rows.1.r0), channel_id=1, source_target_pairs={{0,4},{2,6},{4,0},{6,2},{1,5},{3,7},{5,1},{7,3},{8,12},{10,14},{12... | collective-permute-start | bytes 196616 | tf_op jit(solution)/shard_map/ppermute | solution.py:31
  34.3 4.3 %collective-permute-start.9 = (bf16[256,128]{1,0:T(8,128)(2,1)S(1)}, bf16[256,128]{1,0:T(8,128)(2,1)S(1)}, u32[]{:S(2)}, u32[]{:S(2)}) collective-permute-start(bf16[256,128]{1,0:T(8,128)(2,1)S(1)} %rows.1.r0), channel_id=1, source_target_pairs={{0,2},{2,4},{4,6},{6,0},{1,3},{3,5},{5,7},{7,1},{8,10},{10,12},{12... | collective-permute-start | bytes 196616 | tf_op jit(solution)/shard_map/ppermute | solution.py:31
  36.2 10.4 %collective-permute-start.6 = (bf16[1040,128]{1,0:T(8,128)(2,1)S(1)}, bf16[1040,128]{1,0:T(8,128)(2,1)S(1)}, u32[]{:S(2)}, u32[]{:S(2)}) collective-permute-start(bf16[1040,128]{1,0:T(8,128)(2,1)S(1)} %collective-permute-done.4.cvn), channel_id=1, source_target_pairs={{0,1},{1,0},{2,3},{3,2},{4,5},{5,4},{6,7},{7,6},{8,9},{9,8},{10,11... | collective-permute-start | bytes 798728 | tf_op jit(solution)/shard_map/ppermute | solution.py:36
  36.2 10.4 %collective-permute-start.5 = (bf16[1024,128]{1,0:T(8,128)(2,1)S(1)}, bf16[1024,128]{1,0:T(8,128)(2,1)S(1)}, u32[]{:S(2)}, u32[]{:S(2)}) collective-permute-start(bf16[1024,128]{1,0:T(8,128)(2,1)S(1)} %collective-permute-done.2.ckn), channel_id=1, source_target_pairs={{0,1},{1,0},{2,3},{3,2},{4,5},{5,4},{6,7},{7,6},{8,9},{9,8},{10,11... | collective-permute-start | bytes 786440 | tf_op jit(solution)/shard_map/ppermute | solution.py:36
  38.6 8.1 %collective-permute-start.12 = (bf16[512,128]{1,0:T(8,128)(2,1)S(1)}, bf16[512,128]{1,0:T(8,128)(2,1)S(1)}, u32[]{:S(2)}, u32[]{:S(2)}) collective-permute-start(bf16[512,128]{1,0:T(8,128)(2,1)S(1)} %select.6), channel_id=1, source_target_pairs={{0,0},{8,8},{16,16},{24,24},{40,32},{48,40},{56,48},{32,56},{80,64... | collective-permute-start | bytes 393224 | tf_op jit(solution)/shard_map/ppermute | solution.py:365
  50.8 5.0 %copy-start.6 = (s32[2048]{0:T(1024)S(1)}, s32[2048]{0:T(1024)}, u32[]{:S(2)}) copy-start(s32[2048]{0:T(1024)} %param.15) | copy-start | bytes 24580
  50.8 5.0 %copy-start.7 = (s32[2048]{0:T(1024)S(1)}, s32[2048]{0:T(1024)}, u32[]{:S(2)}) copy-start(s32[2048]{0:T(1024)} %param.14) | copy-start | bytes 24580
  50.8 18.1 %all-to-all-start.1 = ((s16[8,144,128]{2,1,0:T(8,128)(2,1)}), s16[8,144,128]{2,1,0:T(8,128)(2,1)S(1)}, u32[]{:S(2)}, u32[]{:S(2)}) async-start(s16[8,144,128]{2,1,0:T(8,128)(2,1)} %second.1.payload), calls=%async_computation.1 | async-start | bytes 589824 | tf_op jit(solution)/shard_map/all_to_all | solution.py:400
  57.2 5.6 %collective-permute-start.13 = (bf16[256,128]{1,0:T(8,128)(2,1)S(1)}, bf16[256,128]{1,0:T(8,128)(2,1)S(1)}, u32[]{:S(2)}, u32[]{:S(2)}) collective-permute-start(bf16[256,128]{1,0:T(8,128)(2,1)S(1)} %get-tuple-element.13), channel_id=1, source_target_pairs={{0,8},{8,16},{16,24},{24,0},{1,9},{9,17},{17,25},{25,1},{2,10},{10... | collective-permute-start | bytes 196616 | tf_op jit(solution)/shard_map/ppermute | solution.py:31
  58.8 4.5 %collective-permute-start.14 = (bf16[256,128]{1,0:T(8,128)(2,1)S(1)}, bf16[256,128]{1,0:T(8,128)(2,1)S(1)}, u32[]{:S(2)}, u32[]{:S(2)}) collective-permute-start(bf16[256,128]{1,0:T(8,128)(2,1)S(1)} %get-tuple-element.14), channel_id=1, source_target_pairs={{0,24},{8,0},{16,8},{24,16},{1,25},{9,1},{17,9},{25,17},{2,26},{10... | collective-permute-start | bytes 196616 | tf_op jit(solution)/shard_map/ppermute | solution.py:31
  60.5 5.8 %collective-permute-start.15 = (bf16[256,128]{1,0:T(8,128)(2,1)S(1)}, bf16[256,128]{1,0:T(8,128)(2,1)S(1)}, u32[]{:S(2)}, u32[]{:S(2)}) collective-permute-start(bf16[256,128]{1,0:T(8,128)(2,1)S(1)} %get-tuple-element.15), channel_id=1, source_target_pairs={{0,16},{8,24},{16,0},{24,8},{1,17},{9,25},{17,1},{25,9},{2,18},{10... | collective-permute-start | bytes 196616 | tf_op jit(solution)/shard_map/ppermute | solution.py:31

commit v3 on v2

--- a/solution.py
+++ b/solution.py
@@ -17,7 +17,7 @@
 KEYS = 2 * HALF
 SIDE = PAGES * HALF
 QROWS = 1024
-TILE = 256
+TILE = 512
 BLOCK = 128
 NEG = -1e30
 SCALE = 1.4426950408889634 / math.sqrt(HD)
@@ -53,59 +53,52 @@
     return ref[pl.ds(pl.multiple_of(start + p * stride, HALF), HALF), :]
 
 
-def score_pages(q, scores, top, slot, mask, keys_at):
+def take(q, keys, values, top, total, acc, visible=None):
+    def scores(t):
+        found = []
+        for i, part in enumerate(keys):
+            s = lax.dot_general(
+                q[pl.ds(t * TILE, TILE), :],
+                part,
+                (((1,), (1,)), ((), ())),
+                preferred_element_type=F32,
+            )
+            if visible is not None:
+                s = jnp.where(visible(t), s, NEG)
+            found += [s[:, :HD], s[:, HD:]]
+        return found
+
+    def add(t, parts):
+        rows = pl.ds(t * TILE, TILE)
+        best = jnp.max(functools.reduce(jnp.maximum, parts), axis=1, keepdims=True)
+        old = top[rows, :]
+        now = jnp.maximum(old, jnp.broadcast_to(best, (TILE, HD)))
+        factor = jnp.exp2((old - now) * SCALE)
+        parts = [jnp.exp2((s - now) * SCALE) for s in parts]
+        total[rows, :] = total[rows, :] * factor + functools.reduce(jnp.add, parts)
+        weight = jnp.concatenate([e.astype(BF16) for e in parts], axis=1)
+        acc[rows, :] = acc[rows, :] * factor + jnp.dot(
+            weight, values, preferred_element_type=F32
+        )
+        top[rows, :] = now
+
+    following = scores(0)
+    for t in range(QROWS // TILE):
+        current = following
+        if t + 1 < QROWS // TILE:
+            following = scores(t + 1)
+        add(t, current)
+
+
+def take_pages(q, mask, keys_at, values_at, top, total, acc):
     def page(p, carry):
         @pl.when(((mask >> p) & 1) != 0)
         def _():
-            for i, keys in enumerate(keys_at(p)):
-                for t in range(QROWS // TILE):
-                    rows = pl.ds(t * TILE, TILE)
-                    s = lax.dot_general(
-                        q[rows, :], keys, (((1,), (1,)), ((), ())), preferred_element_type=F32
-                    )
-                    scores[slot + p, rows, i * HALF : (i + 1) * HALF] = s
-                    top[rows, :] = jnp.maximum(
-                        top[rows, :], jnp.maximum(s[:, :HD], s[:, HD:])
-                    )
+            take(q, keys_at(p), jnp.concatenate(values_at(p), axis=0), top, total, acc)
 
         return carry
 
     lax.fori_loop(0, PAGES, page, 0)
-
-
-def weigh(scores_at, values, level, total, acc, width):
-    for t in range(QROWS // TILE):
-        rows = pl.ds(t * TILE, TILE)
-        now = level[rows, :]
-        s = scores_at(rows)
-        parts = [
-            jnp.exp2((s[:, j * HD : (j + 1) * HD] - now) * SCALE) for j in range(width // HD)
-        ]
-        total[rows, :] = total[rows, :] + functools.reduce(jnp.add, parts)
-        weight = jnp.concatenate([e.astype(BF16) for e in parts], axis=1)
-        acc[rows, :] = acc[rows, :] + jnp.dot(weight, values, preferred_element_type=F32)
-
-
-def weigh_pages(scores, level, total, acc, slot, mask, values_at):
-    def page(p, carry):
-        @pl.when(((mask >> p) & 1) != 0)
-        def _():
-            values = jnp.concatenate(values_at(p), axis=0)
-            weigh(lambda rows: scores[slot + p, rows, :], values, level, total, acc, KEYS)
-
-        return carry
-
-    lax.fori_loop(0, PAGES, page, 0)
-
-
-def settle(top, level):
-    found = []
-    for b in range(QROWS // BLOCK):
-        rows = pl.ds(b * BLOCK, BLOCK)
-        row = jnp.max(jnp.transpose(top[rows, :], (1, 0)), axis=0, keepdims=True)
-        level[rows, :] = across(row)
-        found.append(row)
-    return found
 
 
 def mask_of(ref, start=2 * SIDE):
@@ -128,6 +121,13 @@
         out[b, BLOCK + 16 : SENT, :] = far[...]
 
 
+def own_mask(table, live):
+    mask = 0
+    for k in range(PAGES):
+        mask = mask + jnp.where(k < live[0], jnp.left_shift(1, table[0, k]), 0)
+    return mask
+
+
 def rows_kernel(q3, af, bf, out):
     for b in range(8):
         out[b * 32 : b * 32 + 32, :] = q3[b, BLOCK:SENT, :]
@@ -147,47 +147,43 @@
         out[256:512, :] = r2[...]
 
 
-def first_kernel(
-    table, live, q3, ok, ov, an, af, bn, bf, level, total, acc, q, scores, top
-):
+def first_kernel(table, live, q3, ok, ov, an, af, bn, bf, top, total, acc, q):
     load_queries(q, q3)
     top[...] = jnp.full(top.shape, NEG, F32)
     total[...] = jnp.zeros(total.shape, F32)
     acc[...] = jnp.zeros(acc.shape, F32)
-    own = 0
-    for k in range(PAGES):
-        own = own + jnp.where(k < live[0], jnp.left_shift(1, table[0, k]), 0)
-    stores = [
-        (
-            own,
-            lambda p: [page_parts(ok, p, 0, KEYS), page_parts(ok, p, HALF, KEYS)],
-            lambda p: [page_parts(ov, p, 0, KEYS), page_parts(ov, p, HALF, KEYS)],
+    take_pages(
+        q,
+        own_mask(table, live),
+        lambda p: [page_parts(ok, p, 0, KEYS), page_parts(ok, p, HALF, KEYS)],
+        lambda p: [page_parts(ov, p, 0, KEYS), page_parts(ov, p, HALF, KEYS)],
+        top, total, acc,
+    )
+    for near, far in ((an, af), (bn, bf)):
+        take_pages(
+            q,
+            mask_of(near),
+            lambda p, near=near, far=far: [page_parts(near, p), page_parts(far, p)],
+            lambda p, near=near, far=far: [page_parts(near, p, SIDE), page_parts(far, p, SIDE)],
+            top, total, acc,
         )
-    ]
-    for near, far in ((an, af), (bn, bf)):
-        stores.append(
-            (
-                mask_of(near),
-                lambda p, near=near, far=far: [page_parts(near, p), page_parts(far, p)],
-                lambda p, near=near, far=far: [page_parts(near, p, SIDE), page_parts(far, p, SIDE)],
-            )
-        )
-    for i, (mask, keys_at, _) in enumerate(stores):
-        score_pages(q, scores, top, i * PAGES, mask, keys_at)
-    settle(top, level)
-    for i, (mask, _, values_at) in enumerate(stores):
-        weigh_pages(scores, level, total, acc, i * PAGES, mask, values_at)
 
 
 def second_kernel(
-    q3, ckn, cvn, ckf, cvf, new, level_in, total_in, acc_in, out,
-    q, scores, fresh, top, level, total, acc,
+    q3, ckn, cvn, ckf, cvf, new, top_in, total_in, acc_in, out, q, top, total, acc
 ):
     z, x, y, core = here()
     load_queries(q, q3)
-    top[...] = level_in[...]
-    mask = mask_of(cvn, SIDE)
-    score_pages(q, scores, top, 0, mask, lambda p: [page_parts(ckn, p), page_parts(ckf, p)])
+    top[...] = top_in[...]
+    total[...] = total_in[...]
+    acc[...] = acc_in[...]
+    take_pages(
+        q,
+        mask_of(cvn, SIDE),
+        lambda p: [page_parts(ckn, p), page_parts(ckf, p)],
+        lambda p: [page_parts(cvn, p), page_parts(cvf, p)],
+        top, total, acc,
+    )
 
     at = lax.broadcasted_iota(I32, (BLOCK, BLOCK), 0)
     place = lax.broadcasted_iota(I32, (BLOCK, BLOCK), 1) == (at % 64) * 2 + at // 64
@@ -203,34 +199,22 @@
     head = ((y + side) & 3) * 2 + (core ^ ((slot // 8) & 1))
     token = ((slot // 16) % 8 * 4 + ((x + z) & 3)) * 64 + head * 8 + slot % 8
     row = lax.broadcasted_iota(I32, (TILE, 256), 0)
-    for t in range(QROWS // TILE):
-        rows = pl.ds(t * TILE, TILE)
-        s = lax.dot_general(q[rows, :], keys, (((1,), (1,)), ((), ())), preferred_element_type=F32)
-        position = ((2 * t + row // BLOCK) * 4 + x) * 64 + (row % BLOCK) // 2
-        s = jnp.where(token <= position, s, NEG)
-        fresh[rows, :] = s
-        top[rows, :] = jnp.maximum(top[rows, :], jnp.maximum(s[:, :HD], s[:, HD:]))
-    peaks = settle(top, level)
-    for t in range(QROWS // TILE):
-        rows = pl.ds(t * TILE, TILE)
-        factor = jnp.exp2((level_in[rows, :] - level[rows, :]) * SCALE)
-        total[rows, :] = total_in[rows, :] * factor
-        acc[rows, :] = acc_in[rows, :] * factor
-    weigh_pages(
-        scores, level, total, acc, 0, mask,
-        lambda p: [page_parts(cvn, p), page_parts(cvf, p)],
-    )
-    weigh(lambda rows: fresh[rows, :], values, level, total, acc, 256)
+
+    def visible(t):
+        position = ((TILE // BLOCK * t + row // BLOCK) * 4 + x) * 64 + (row % BLOCK) // 2
+        return token <= position
+
+    take(q, [keys], values, top, total, acc, visible)
 
     for j in range(8):
         rows = pl.ds(j * BLOCK, BLOCK)
         full = acc[rows, :]
         size = jnp.max(jnp.transpose(jnp.abs(full), (1, 0)), axis=0, keepdims=True)
-        size = jnp.maximum(size, 1e-30)
+        size = jnp.maximum(size, 1.2e-34)
         number = jnp.round(full * across(32767.0 / size)).astype(I32).astype(jnp.int16)
         weight = jnp.sum(jnp.transpose(total[rows, :], (1, 0)), axis=0, keepdims=True)
         stats = (
-            split_fixed(peaks[j] * SCALE)
+            split_fixed(jnp.transpose(top[rows, :], (1, 0))[0:1, :] * SCALE)
             + split_fixed(jnp.log2(weight))
             + split_fixed(jnp.log2(size))
         )
@@ -238,7 +222,7 @@
         out[j] = jnp.concatenate([number, stats.astype(jnp.int16)], axis=0)
 
 
-def merge_kernel(parts, out):
+def merge_kernel(parts, n0, n1, n2, n3, out, appended):
     stats = [parts[s, BLOCK:PAYLOAD, :].astype(I32) for s in range(8)]
 
     def rows(at):
@@ -255,6 +239,9 @@
     for s in range(8):
         total = total + parts[s, 0:BLOCK, :].astype(F32) * columns[:, s : s + 1]
     out[...] = total.astype(BF16)
+    rows = n0[...].astype(F32) + n1[...].astype(F32)
+    rows = rows + n2[...].astype(F32) + n3[...].astype(F32)
+    appended[...] = rows.astype(BF16)
 
 
 def route_kernel(r0, r1, r2, r3, code, payload, o0, o1, o2, o3):
@@ -271,12 +258,6 @@
     total = total.astype(BF16)
     for d, o in enumerate((o0, o1, o2, o3)):
         o[...] = total[d * 256 : (d + 1) * 256, :]
-
-
-def place_kernel(n0, n1, n2, n3, out):
-    total = n0[...].astype(F32) + n1[...].astype(F32)
-    total = total + n2[...].astype(F32) + n3[...].astype(F32)
-    out[...] = total.astype(BF16)
 
 
 SMALL = pltpu.CompilerParams(vmem_limit_bytes=8 * 1024 * 1024)
@@ -336,20 +317,17 @@
         compiler_params=SMALL,
         name="rows",
     )(q3, af, bf)
-    rows = [rows, shifted(rows, "y", 1), shifted(rows, "y", -1), shifted(rows, "y", 2)]
+    opposite = shifted(rows, "y", 2)
+    rows = [rows, shifted(rows, "y", 1), shifted(rows, "y", -1), opposite]
 
     state = jax.ShapeDtypeStruct((QROWS, HD), F32)
-    params = pltpu.CompilerParams(vmem_limit_bytes=50 * 1024 * 1024)
+    params = pltpu.CompilerParams(vmem_limit_bytes=24 * 1024 * 1024)
     level, total, acc = pl.pallas_call(
         first_kernel,
         out_shape=(state,) * 3,
         in_specs=[smem()] * 2 + [vmem()] * 7,
         out_specs=(vmem(),) * 3,
-        scratch_shapes=[
-            pltpu.VMEM((QROWS, HD), BF16),
-            pltpu.VMEM((3 * PAGES, QROWS, KEYS), F32),
-            pltpu.VMEM((QROWS, HD), F32),
-        ],
+        scratch_shapes=[pltpu.VMEM((QROWS, HD), BF16)],
         compiler_params=params,
         cost_estimate=cost(8),
         name="first",
@@ -370,12 +348,7 @@
         out_shape=jax.ShapeDtypeStruct((8, PAYLOAD, HD), jnp.int16),
         in_specs=[vmem()] * 9,
         out_specs=vmem(),
-        scratch_shapes=[
-            pltpu.VMEM((QROWS, HD), BF16),
-            pltpu.VMEM((PAGES, QROWS, KEYS), F32),
-            pltpu.VMEM((QROWS, 256), F32),
-        ]
-        + [pltpu.VMEM((QROWS, HD), F32)] * 4,
+        scratch_shapes=[pltpu.VMEM((QROWS, HD), BF16)] + [pltpu.VMEM((QROWS, HD), F32)] * 3,
         compiler_params=params,
         cost_estimate=cost(1),
         name="second",
@@ -394,26 +367,21 @@
         compiler_params=SMALL,
         name="route",
     )(*rows, code, payload)
+    t3 = shifted(to_opposite, "x", 2)
     t1 = shifted(to_after, "x", 1)
     t2 = shifted(to_before, "x", -1)
-    t3 = shifted(to_opposite, "x", 2)
     parts = lax.all_to_all(payload, "z", 0, 0)
-    attended = pl.pallas_call(
+    attended, appended = pl.pallas_call(
         merge_kernel,
-        out_shape=jax.ShapeDtypeStruct((BLOCK, HD), BF16),
-        in_specs=[vmem()],
-        out_specs=vmem(),
+        out_shape=(
+            jax.ShapeDtypeStruct((BLOCK, HD), BF16),
+            jax.ShapeDtypeStruct((256, HD), BF16),
+        ),
+        in_specs=[vmem()] * 5,
+        out_specs=(vmem(),) * 2,
         compiler_params=SMALL,
         name="merge",
-    )(parts)
-    appended = pl.pallas_call(
-        place_kernel,
-        out_shape=jax.ShapeDtypeStruct((256, HD), BF16),
-        in_specs=[vmem()] * 4,
-        out_specs=vmem(),
-        compiler_params=SMALL,
-        name="place",
-    )(t0, t1, t2, t3)
+    )(parts, t0, t1, t2, t3)
     return attended.reshape(queries.shape), appended.reshape(BLOCK, 2, HD)
 
 

time: 71.1 us -> 69.9 us (0.983)
  waiting for transfers between devices: 17.2 us -> 19.3 us
  Pallas kernels: 14.5 us -> 12.8 us
  starting transfers between devices: 30.9 us -> 30 us
  local copies, waits for them, and re-layouts: 5.09 us -> 4.37 us
    all_to_all x1, waiting for transfers between devices: 6.46 us -> 7.55 us  [shards(): q3 = lax.all_to_all(sent, 'z', 0, 0)]
    pallas_call x1, Pallas kernels: 4.18 us -> 3.21 us  [shards(): pl.pallas_call(second_kernel, out_shape=jax.ShapeDtypeStruct((8, PAYLOAD,...]
    slice x2, local copies, waits for them, and re-layouts: 2.67 us -> 1.71 us  [shards(): ckn, cvn = (shifted(an[:SIDE], 'x', 1), shifted(bn[SIDE:], 'x', -1))]
    pallas_call x2 -> x1, Pallas kernels: 1.65 us -> 1 us  [shards(): pl.pallas_call(merge_kernel, out_shape=(jax.ShapeDtypeStruct((BLOCK, HD),...]
  transfers between devices with their start and end apart: 18 -> 18, of which waited for: 9 -> 9; matrix products, arithmetic and copies ran while one was open for 5% -> 3% of each run, Pallas kernels for 13% -> 13%
where the time goes in v3:
time: 69.9 us; the launch traced here: 68.7 us
  starting transfers between devices  30 us (43%)
  waiting for transfers between devices  19.3 us (28%)
  Pallas kernels  12.8 us (18%)
  local copies, waits for them, and re-layouts  4.37 us (6%)
  between operations  1.48 us (2%)
  other arithmetic  0.71 us (1%)
    ppermute x10, starting transfers between devices, shifted(): lax.ppermute(value, axis, [(i, (i + steps) % count) for i in range(count)])  14.9 us
    all_to_all x1, starting transfers between devices, shards(): q3 = lax.all_to_all(sent, 'z', 0, 0)  8.47 us
    ppermute x10, waiting for transfers between devices, shifted(): lax.ppermute(value, axis, [(i, (i + steps) % count) for i in range(count)])  8.15 us
    all_to_all x1, waiting for transfers between devices, shards(): q3 = lax.all_to_all(sent, 'z', 0, 0)  7.55 us
    pallas_call x1, Pallas kernels, shards(): pl.pallas_call(first_kernel, out_shape=(state,) * 3, in_specs=[smem()] *...  7.07 us
    all_to_all x1, starting transfers between devices, shards(): parts = lax.all_to_all(payload, 'z', 0, 0)  4.76 us
    pallas_call x1, Pallas kernels, shards(): pl.pallas_call(second_kernel, out_shape=jax.ShapeDtypeStruct((8, PAYLOAD,...  3.21 us
    all_to_all x1, waiting for transfers between devices, shards(): parts = lax.all_to_all(payload, 'z', 0, 0)  2.42 us
  transfers between devices with their start and end apart: 18, of which 9 were waited for; matrix products, arithmetic and copies ran while one was open for 3% of the time, Pallas kernels for 13%

profile of v3, /device:TPU:8, one launch (start us, length us, event | category | flops | bytes accessed | tf_op | source)
XLA Modules:
  0.0 68.7 jit_solution(10063751469541250809)
XLA Ops:
  1.3 0.7 fusion.3
  1.9 1.1 %constant_dynamic-slice_fusion.1 = (bf16[4,1,256,128]{3,2,1,0:T(8,128)(2,1)S(1)}, bf16[4,1,256,128]{3,2,1,0:T(8,128)(2,1)S(1)}) fusion(bf16[4,2,256,128]{3,2,1,0:T(8,128)(2,1)} %bitcast.21, s32[]{:T(128)S(6)} %select_n.22, bf16[4,2,256,128]{3,2,1,0:T(8,128)(2,1)} %bitcast.22), kind=kLoop, calls=%fused_computation.9 | loop fusion | bytes 1048580 | tf_op jit(solution)/shard_map/jit(dynamic_index_in_dim)/dynamic_slice | solution.py:291
  3.0 0.0 copy-start.3
  3.0 0.0 copy-start.2
  3.1 1.6 %collective-permute-start.1 = (bf16[2064,128]{1,0:T(8,128)(2,1)S(1)}, bf16[2064,128]{1,0:T(8,128)(2,1)}, u32[]{:S(2)}, u32[]{:S(2)}) collective-permute-start(bf16[2064,128]{1,0:T(8,128)(2,1)S(1)} %fusion.1), channel_id=1, source_target_pairs={{0,8},{8,16},{16,24},{24,0},{1,9},{9,17},{17,25},{25,1},{2,10},{10... | collective-permute-start | bytes 1585160 | tf_op jit(solution)/shard_map/ppermute | solution.py:31
  4.6 1.7 %collective-permute-start.3 = (bf16[2064,128]{1,0:T(8,128)(2,1)S(1)}, bf16[2064,128]{1,0:T(8,128)(2,1)S(1)}, u32[]{:S(2)}, u32[]{:S(2)}) collective-permute-start(bf16[2064,128]{1,0:T(8,128)(2,1)S(1)} %fusion.1), channel_id=1, source_target_pairs={{0,24},{8,0},{16,8},{24,16},{1,25},{9,1},{17,9},{25,17},{2,26},{10... | collective-permute-start | bytes 1585160 | tf_op jit(solution)/shard_map/ppermute | solution.py:31
  6.4 0.0 collective-permute-start
  6.4 1.2 %collective-permute-done.far = bf16[16,128]{1,0:T(8,128)(2,1)S(1)} collective-permute-done((bf16[16,128]{1,0:T(8,128)(2,1)S(1)}, bf16[16,128]{1,0:T(8,128)(2,1)S(1)}, u32[]{:S(2)}, u32[]{:S(2)}) %collective-permute-start) | collective-permute-done | bytes 4128 | tf_op jit(solution)/shard_map/ppermute | solution.py:36
  7.6 0.8 %gather.1 = bf16[8,160,128]{2,1,0:T(8,128)(2,1)} custom-call(bf16[128,128]{1,0:T(8,128)(2,1)S(1)} %bitcast.23, bf16[16,128]{1,0:T(8,128)(2,1)S(1)} %bitcast.25, bf16[16,128]{1,0:T(8,128)(2,1)S(1)} %collective-permute-done.far), custom_call_target="tpu_custom_call" | custom-call | tf_op jit(solution)/shard_map/gather/pallas_call | solution.py:303
  8.3 8.5 %all-to-all-start = ((bf16[8,160,128]{2,1,0:T(8,128)(2,1)}), bf16[8,160,128]{2,1,0:T(8,128)(2,1)S(1)}, u32[]{:S(2)}, u32[]{:S(2)}) async-start(bf16[8,160,128]{2,1,0:T(8,128)(2,1)} %gather.1), calls=%async_computation | async-start | bytes 655360 | tf_op jit(solution)/shard_map/all_to_all | solution.py:311
  16.8 1.4 %collective-permute-done.1.an = bf16[2064,128]{1,0:T(8,128)(2,1)} collective-permute-done((bf16[2064,128]{1,0:T(8,128)(2,1)S(1)}, bf16[2064,128]{1,0:T(8,128)(2,1)}, u32[]{:S(2)}, u32[]{:S(2)}) %collective-permute-start.1) | collective-permute-done | bytes 528416 | tf_op jit(solution)/shard_map/ppermute | solution.py:31
  18.2 0.0 collective-permute-start.7
  18.2 0.0 collective-permute-done.3.bn
  18.2 0.5 collective-permute-start.8
  18.8 2.4 %collective-permute-start.4 = (bf16[1040,128]{1,0:T(8,128)(2,1)S(1)}, bf16[1040,128]{1,0:T(8,128)(2,1)S(1)}, u32[]{:S(2)}, u32[]{:S(2)}) collective-permute-start(bf16[1040,128]{1,0:T(8,128)(2,1)S(1)} %slice.9), channel_id=1, source_target_pairs={{0,24},{8,0},{16,8},{24,16},{1,25},{9,1},{17,9},{25,17},{2,26},{10... | collective-permute-start | bytes 798728 | tf_op jit(solution)/shard_map/ppermute | solution.py:31
  21.2 1.7 %slice.8 = bf16[1024,128]{1,0:T(8,128)(2,1)} slice(bf16[2064,128]{1,0:T(8,128)(2,1)} %collective-permute-done.1.an), slice={[0:1024], [0:128]} | slice | bytes 524288 | tf_op jit(solution)/shard_map/slice | solution.py:298
  22.9 0.0 collective-permute-start.2
  22.9 7.6 %all-to-all-done.q3 = bf16[8,160,128]{2,1,0:T(8,128)(2,1)S(1)} async-done(((bf16[8,160,128]{2,1,0:T(8,128)(2,1)}), bf16[8,160,128]{2,1,0:T(8,128)(2,1)S(1)}, u32[]{:S(2)}, u32[]{:S(2)}) %all-to-all-start) | async-done | bytes 327712 | tf_op jit(solution)/shard_map/all_to_all | solution.py:311
  30.4 0.0 collective-permute-done.7.af
  30.4 0.0 collective-permute-done.8.bf
  30.4 0.5 collective-permute-start.10
  31.0 2.6 %collective-permute-start.11 = (bf16[256,128]{1,0:T(8,128)(2,1)S(1)}, bf16[256,128]{1,0:T(8,128)(2,1)S(1)}, u32[]{:S(2)}, u32[]{:S(2)}) collective-permute-start(bf16[256,128]{1,0:T(8,128)(2,1)S(1)} %rows.1.r0), channel_id=1, source_target_pairs={{0,4},{2,6},{4,0},{6,2},{1,5},{3,7},{5,1},{7,3},{8,12},{10,14},{12... | collective-permute-start | bytes 196616 | tf_op jit(solution)/shard_map/ppermute | solution.py:31
  33.6 1.9 %collective-permute-start.9 = (bf16[256,128]{1,0:T(8,128)(2,1)S(1)}, bf16[256,128]{1,0:T(8,128)(2,1)S(1)}, u32[]{:S(2)}, u32[]{:S(2)}) collective-permute-start(bf16[256,128]{1,0:T(8,128)(2,1)S(1)} %rows.1.r0), channel_id=1, source_target_pairs={{0,2},{2,4},{4,6},{6,0},{1,3},{3,5},{5,7},{7,1},{8,10},{10,12},{12... | collective-permute-start | bytes 196616 | tf_op jit(solution)/shard_map/ppermute | solution.py:31
  35.5 0.0 collective-permute-done.4.cvn
  35.5 0.5 collective-permute-start.5
  36.0 0.0 collective-permute-done.10.r2
  36.0 0.9 %collective-permute-done.11.r3 = bf16[256,128]{1,0:T(8,128)(2,1)S(1)} collective-permute-done((bf16[256,128]{1,0:T(8,128)(2,1)S(1)}, bf16[256,128]{1,0:T(8,128)(2,1)S(1)}, u32[]{:S(2)}, u32[]{:S(2)}) %collective-permute-start.11) | collective-permute-done | bytes 65568 | tf_op jit(solution)/shard_map/ppermute | solution.py:31
  36.9 1.0 %collective-permute-done.9.r1 = bf16[256,128]{1,0:T(8,128)(2,1)S(1)} collective-permute-done((bf16[256,128]{1,0:T(8,128)(2,1)S(1)}, bf16[256,128]{1,0:T(8,128)(2,1)S(1)}, u32[]{:S(2)}, u32[]{:S(2)}) %collective-permute-start.9) | collective-permute-done | bytes 65568 | tf_op jit(solution)/shard_map/ppermute | solution.py:31
  37.8 0.8 %collective-permute-start.12 = (bf16[512,128]{1,0:T(8,128)(2,1)S(1)}, bf16[512,128]{1,0:T(8,128)(2,1)S(1)}, u32[]{:S(2)}, u32[]{:S(2)}) collective-permute-start(bf16[512,128]{1,0:T(8,128)(2,1)S(1)} %select.6), channel_id=1, source_target_pairs={{0,0},{8,8},{16,16},{24,24},{40,32},{48,40},{56,48},{32,56},{80,64... | collective-permute-start | bytes 393224 | tf_op jit(solution)/shard_map/ppermute | solution.py:343
  38.7 0.0 copy-start.1
  38.7 1.0 %copy-done.1 = bf16[2048,128]{1,0:T(8,128)(2,1)S(1)} copy-done((bf16[2048,128]{1,0:T(8,128)(2,1)S(1)}, bf16[2048,128]{1,0:T(8,128)(2,1)}, u32[]{:S(2)}) %copy-start.1) | copy-done | bytes 524312
  39.8 7.1 %first.1 = (f32[1024,128]{1,0:T(8,128)S(1)}, f32[1024,128]{1,0:T(8,128)S(1)}, f32[1024,128]{1,0:T(8,128)S(1)}) custom-call(s32[1,4]{1,0:T(1,128)S(1)} %copy-done.4, s32[1]{0:T(128)} %copy.31.live, bf16[8,160,128]{2,1,0:T(8,128)(2,1)S(1)} %all-to-all-done.q3, bf16[2048,128]{1,0:T(8,128)(2,1)S(1)} %copy-done.1, bf16[2048,128]{1,0:T(8,128)(2,1)S(1)} %copy-done, ...), custom_call_target="tpu_custom_call" | custom-call | flops 2147483648 | bytes 1048576 | tf_op jit(solution)/shard_map/first/pallas_call | solution.py:325
  46.9 0.0 collective-permute-done.5.ckf
  46.9 0.0 collective-permute-done.6.cvf
  46.9 3.2 %second.1.payload = s16[8,144,128]{2,1,0:T(8,128)(2,1)} custom-call(bf16[8,160,128]{2,1,0:T(8,128)(2,1)S(1)} %all-to-all-done.q3, bf16[1024,128]{1,0:T(8,128)(2,1)S(1)} %collective-permute-done.2.ckn, bf16[1040,128]{1,0:T(8,128)(2,1)S(1)} %collective-permute-done.4.cvn, bf16[1024,128]{1,0:T(8,128)(2,1)S(1)} %collective-permute-done.5.ckf, ...), custom_call_target="tpu_custom_call" | custom-call | flops 268435456 | bytes 1048576 | tf_op jit(solution)/shard_map/second/pallas_call | solution.py:346
  50.1 4.8 %all-to-all-start.1 = ((s16[8,144,128]{2,1,0:T(8,128)(2,1)}), s16[8,144,128]{2,1,0:T(8,128)(2,1)S(1)}, u32[]{:S(2)}, u32[]{:S(2)}) async-start(s16[8,144,128]{2,1,0:T(8,128)(2,1)} %second.1.payload), calls=%async_computation.1 | async-start | bytes 589824 | tf_op jit(solution)/shard_map/all_to_all | solution.py:373
  54.9 0.2 reshape.52
  55.2 0.2 copy.25
  55.4 0.1 copy.24.code
  55.5 0.8 %route.1 = (bf16[256,128]{1,0:T(8,128)(2,1)S(1)}, bf16[256,128]{1,0:T(8,128)(2,1)S(1)}, bf16[256,128]{1,0:T(8,128)(2,1)S(1)}, bf16[256,128]{1,0:T(8,128)(2,1)S(1)}) custom-call(bf16[256,128]{1,0:T(8,128)(2,1)S(1)} %rows.1.r0, bf16[256,128]{1,0:T(8,128)(2,1)S(1)} %collective-permute-done.9.r1, bf16[256,128]{1,0:T(8,128)(2,1)S(1)} %collective-permute-done.10.r2, ...), custom_call_target="tpu_custom_call" | custom-call | tf_op jit(solution)/shard_map/route/pallas_call | solution.py:362
  56.2 0.8 %collective-permute-start.13 = (bf16[256,128]{1,0:T(8,128)(2,1)S(1)}, bf16[256,128]{1,0:T(8,128)(2,1)S(1)}, u32[]{:S(2)}, u32[]{:S(2)}) collective-permute-start(bf16[256,128]{1,0:T(8,128)(2,1)S(1)} %get-tuple-element.15), channel_id=1, source_target_pairs={{0,8},{8,16},{16,24},{24,0},{1,9},{9,17},{17,25},{25,1},{2,10},{10... | collective-permute-start | bytes 196616 | tf_op jit(solution)/shard_map/ppermute | solution.py:31
  57.0 2.5 %collective-permute-start.14 = (bf16[256,128]{1,0:T(8,128)(2,1)S(1)}, bf16[256,128]{1,0:T(8,128)(2,1)S(1)}, u32[]{:S(2)}, u32[]{:S(2)}) collective-permute-start(bf16[256,128]{1,0:T(8,128)(2,1)S(1)} %get-tuple-element.16), channel_id=1, source_target_pairs={{0,24},{8,0},{16,8},{24,16},{1,25},{9,1},{17,9},{25,17},{2,26},{10... | collective-permute-start | bytes 196616 | tf_op jit(solution)/shard_map/ppermute | solution.py:31
  59.6 0.9 %collective-permute-start.15 = (bf16[256,128]{1,0:T(8,128)(2,1)S(1)}, bf16[256,128]{1,0:T(8,128)(2,1)S(1)}, u32[]{:S(2)}, u32[]{:S(2)}) collective-permute-start(bf16[256,128]{1,0:T(8,128)(2,1)S(1)} %get-tuple-element.17), channel_id=1, source_target_pairs={{0,16},{8,24},{16,0},{24,8},{1,17},{9,25},{17,1},{25,9},{2,18},{10... | collective-permute-start | bytes 196616 | tf_op jit(solution)/shard_map/ppermute | solution.py:31
  60.4 1.3 %collective-permute-done.13.n1 = bf16[256,128]{1,0:T(8,128)(2,1)S(1)} collective-permute-done((bf16[256,128]{1,0:T(8,128)(2,1)S(1)}, bf16[256,128]{1,0:T(8,128)(2,1)S(1)}, u32[]{:S(2)}, u32[]{:S(2)}) %collective-permute-start.13) | collective-permute-done | bytes 65568 | tf_op jit(solution)/shard_map/ppermute | solution.py:31
  61.8 0.3 collective-permute-done.14.n2
  62.1 3.3 %collective-permute-done.15.n3 = bf16[256,128]{1,0:T(8,128)(2,1)S(1)} collective-permute-done((bf16[256,128]{1,0:T(8,128)(2,1)S(1)}, bf16[256,128]{1,0:T(8,128)(2,1)S(1)}, u32[]{:S(2)}, u32[]{:S(2)}) %collective-permute-start.15) | collective-permute-done | bytes 65568 | tf_op jit(solution)/shard_map/ppermute | solution.py:31
  65.3 2.4 %all-to-all-done.1.parts = s16[8,144,128]{2,1,0:T(8,128)(2,1)S(1)} async-done(((s16[8,144,128]{2,1,0:T(8,128)(2,1)}), s16[8,144,128]{2,1,0:T(8,128)(2,1)S(1)}, u32[]{:S(2)}, u32[]{:S(2)}) %all-to-all-start.1) | async-done | bytes 294944 | tf_op jit(solution)/shard_map/all_to_all | solution.py:373
  67.7 1.0 %merge.1 = (bf16[128,128]{1,0:T(8,128)(2,1)}, bf16[256,128]{1,0:T(8,128)(2,1)}) custom-call(s16[8,144,128]{2,1,0:T(8,128)(2,1)S(1)} %all-to-all-done.1.parts, bf16[256,128]{1,0:T(8,128)(2,1)S(1)} %get-tuple-element.14.n0, bf16[256,128]{1,0:T(8,128)(2,1)S(1)} %collective-permute-done.13.n1, bf16[256,128]{1,0:T(8,128)(2,1)S(1)} %collective-permute-done.14.n2, ...), custom_call_target="tpu_custom_call" | custom-call | tf_op jit(solution)/shard_map/merge/pallas_call | solution.py:374
  (22 shorter events, 0.2 us)
Async XLA Ops:
  3.0 3.4 %copy-start.3 = (bf16[8,2,128]{2,1,0:T(2,128)(2,1)S(1)}, bf16[8,2,128]{2,1,0:T(2,128)(2,1)}, u32[]{:S(2)}) copy-start(bf16[8,2,128]{2,1,0:T(2,128)(2,1)} %param.13) | copy-start | bytes 12292
  3.0 4.5 %copy-start.2 = (bf16[64,2,128]{2,1,0:T(2,128)(2,1)S(1)}, bf16[64,2,128]{2,1,0:T(2,128)(2,1)}, u32[]{:S(2)}) copy-start(bf16[64,2,128]{2,1,0:T(2,128)(2,1)} %param.8) | copy-start | bytes 98308
  3.1 15.1 %collective-permute-start.1 = (bf16[2064,128]{1,0:T(8,128)(2,1)S(1)}, bf16[2064,128]{1,0:T(8,128)(2,1)}, u32[]{:S(2)}, u32[]{:S(2)}) collective-permute-start(bf16[2064,128]{1,0:T(8,128)(2,1)S(1)} %fusion.1), channel_id=1, source_target_pairs={{0,8},{8,16},{16,24},{24,0},{1,9},{9,17},{17,25},{25,1},{2,10},{10... | collective-permute-start | bytes 1585160 | tf_op jit(solution)/shard_map/ppermute | solution.py:31
  4.6 13.6 %collective-permute-start.3 = (bf16[2064,128]{1,0:T(8,128)(2,1)S(1)}, bf16[2064,128]{1,0:T(8,128)(2,1)S(1)}, u32[]{:S(2)}, u32[]{:S(2)}) collective-permute-start(bf16[2064,128]{1,0:T(8,128)(2,1)S(1)} %fusion.1), channel_id=1, source_target_pairs={{0,24},{8,0},{16,8},{24,16},{1,25},{9,1},{17,9},{25,17},{2,26},{10... | collective-permute-start | bytes 1585160 | tf_op jit(solution)/shard_map/ppermute | solution.py:31
  6.4 1.2 %collective-permute-start = (bf16[16,128]{1,0:T(8,128)(2,1)S(1)}, bf16[16,128]{1,0:T(8,128)(2,1)S(1)}, u32[]{:S(2)}, u32[]{:S(2)}) collective-permute-start(bf16[16,128]{1,0:T(8,128)(2,1)S(1)} %bitcast.24), channel_id=1, source_target_pairs={{0,1},{1,0},{2,3},{3,2},{4,5},{5,4},{6,7},{7,6},{8,9},{9,8},{10,11... | collective-permute-start | bytes 12296 | tf_op jit(solution)/shard_map/ppermute | solution.py:36
  8.3 22.1 %all-to-all-start = ((bf16[8,160,128]{2,1,0:T(8,128)(2,1)}), bf16[8,160,128]{2,1,0:T(8,128)(2,1)S(1)}, u32[]{:S(2)}, u32[]{:S(2)}) async-start(bf16[8,160,128]{2,1,0:T(8,128)(2,1)} %gather.1), calls=%async_computation | async-start | bytes 655360 | tf_op jit(solution)/shard_map/all_to_all | solution.py:311
  18.2 12.2 %collective-permute-start.7 = (bf16[2064,128]{1,0:T(8,128)(2,1)}, bf16[2064,128]{1,0:T(8,128)(2,1)S(1)}, u32[]{:S(2)}, u32[]{:S(2)}) collective-permute-start(bf16[2064,128]{1,0:T(8,128)(2,1)} %collective-permute-done.1.an), channel_id=1, source_target_pairs={{0,1},{1,0},{2,3},{3,2},{4,5},{5,4},{6,7},{7,6},{8,9},{9,8},{10,11... | collective-permute-start | bytes 1585160 | tf_op jit(solution)/shard_map/ppermute | solution.py:36
  18.2 12.2 %collective-permute-start.8 = (bf16[2064,128]{1,0:T(8,128)(2,1)S(1)}, bf16[2064,128]{1,0:T(8,128)(2,1)S(1)}, u32[]{:S(2)}, u32[]{:S(2)}) collective-permute-start(bf16[2064,128]{1,0:T(8,128)(2,1)S(1)} %collective-permute-done.3.bn), channel_id=1, source_target_pairs={{0,1},{1,0},{2,3},{3,2},{4,5},{5,4},{6,7},{7,6},{8,9},{9,8},{10,11... | collective-permute-start | bytes 1585160 | tf_op jit(solution)/shard_map/ppermute | solution.py:36
  18.8 16.7 %collective-permute-start.4 = (bf16[1040,128]{1,0:T(8,128)(2,1)S(1)}, bf16[1040,128]{1,0:T(8,128)(2,1)S(1)}, u32[]{:S(2)}, u32[]{:S(2)}) collective-permute-start(bf16[1040,128]{1,0:T(8,128)(2,1)S(1)} %slice.9), channel_id=1, source_target_pairs={{0,24},{8,0},{16,8},{24,16},{1,25},{9,1},{17,9},{25,17},{2,26},{10... | collective-permute-start | bytes 798728 | tf_op jit(solution)/shard_map/ppermute | solution.py:31
  22.9 15.8 %copy-start = (bf16[2048,128]{1,0:T(8,128)(2,1)S(1)}, bf16[2048,128]{1,0:T(8,128)(2,1)}, u32[]{:S(2)}) copy-start(bf16[2048,128]{1,0:T(8,128)(2,1)} %ov.1) | copy-start | bytes 1572868
  22.9 15.8 %copy-start.4 = (s32[1,4]{1,0:T(1,128)S(1)}, s32[1,4]{1,0:T(1,128)}, u32[]{:S(2)}) copy-start(s32[1,4]{1,0:T(1,128)} %table.1) | copy-start | bytes 52
  22.9 12.6 %collective-permute-start.2 = (bf16[1024,128]{1,0:T(8,128)(2,1)}, bf16[1024,128]{1,0:T(8,128)(2,1)S(1)}, u32[]{:S(2)}, u32[]{:S(2)}) collective-permute-start(bf16[1024,128]{1,0:T(8,128)(2,1)} %slice.8), channel_id=1, source_target_pairs={{0,8},{8,16},{16,24},{24,0},{1,9},{9,17},{17,25},{25,1},{2,10},{10... | collective-permute-start | bytes 786440 | tf_op jit(solution)/shard_map/ppermute | solution.py:31
  30.4 5.5 %collective-permute-start.10 = (bf16[256,128]{1,0:T(8,128)(2,1)S(1)}, bf16[256,128]{1,0:T(8,128)(2,1)S(1)}, u32[]{:S(2)}, u32[]{:S(2)}) collective-permute-start(bf16[256,128]{1,0:T(8,128)(2,1)S(1)} %rows.1.r0), channel_id=1, source_target_pairs={{0,6},{2,0},{4,2},{6,4},{1,7},{3,1},{5,3},{7,5},{8,14},{10,8},{12,... | collective-permute-start | bytes 196616 | tf_op jit(solution)/shard_map/ppermute | solution.py:31
  31.0 5.9 %collective-permute-start.11 = (bf16[256,128]{1,0:T(8,128)(2,1)S(1)}, bf16[256,128]{1,0:T(8,128)(2,1)S(1)}, u32[]{:S(2)}, u32[]{:S(2)}) collective-permute-start(bf16[256,128]{1,0:T(8,128)(2,1)S(1)} %rows.1.r0), channel_id=1, source_target_pairs={{0,4},{2,6},{4,0},{6,2},{1,5},{3,7},{5,1},{7,3},{8,12},{10,14},{12... | collective-permute-start | bytes 196616 | tf_op jit(solution)/shard_map/ppermute | solution.py:31
  33.6 4.3 %collective-permute-start.9 = (bf16[256,128]{1,0:T(8,128)(2,1)S(1)}, bf16[256,128]{1,0:T(8,128)(2,1)S(1)}, u32[]{:S(2)}, u32[]{:S(2)}) collective-permute-start(bf16[256,128]{1,0:T(8,128)(2,1)S(1)} %rows.1.r0), channel_id=1, source_target_pairs={{0,2},{2,4},{4,6},{6,0},{1,3},{3,5},{5,7},{7,1},{8,10},{10,12},{12... | collective-permute-start | bytes 196616 | tf_op jit(solution)/shard_map/ppermute | solution.py:31
  35.5 11.4 %collective-permute-start.6 = (bf16[1040,128]{1,0:T(8,128)(2,1)S(1)}, bf16[1040,128]{1,0:T(8,128)(2,1)S(1)}, u32[]{:S(2)}, u32[]{:S(2)}) collective-permute-start(bf16[1040,128]{1,0:T(8,128)(2,1)S(1)} %collective-permute-done.4.cvn), channel_id=1, source_target_pairs={{0,1},{1,0},{2,3},{3,2},{4,5},{5,4},{6,7},{7,6},{8,9},{9,8},{10,11... | collective-permute-start | bytes 798728 | tf_op jit(solution)/shard_map/ppermute | solution.py:36
  35.5 11.4 %collective-permute-start.5 = (bf16[1024,128]{1,0:T(8,128)(2,1)S(1)}, bf16[1024,128]{1,0:T(8,128)(2,1)S(1)}, u32[]{:S(2)}, u32[]{:S(2)}) collective-permute-start(bf16[1024,128]{1,0:T(8,128)(2,1)S(1)} %collective-permute-done.2.ckn), channel_id=1, source_target_pairs={{0,1},{1,0},{2,3},{3,2},{4,5},{5,4},{6,7},{7,6},{8,9},{9,8},{10,11... | collective-permute-start | bytes 786440 | tf_op jit(solution)/shard_map/ppermute | solution.py:36
  37.8 9.0 %collective-permute-start.12 = (bf16[512,128]{1,0:T(8,128)(2,1)S(1)}, bf16[512,128]{1,0:T(8,128)(2,1)S(1)}, u32[]{:S(2)}, u32[]{:S(2)}) collective-permute-start(bf16[512,128]{1,0:T(8,128)(2,1)S(1)} %select.6), channel_id=1, source_target_pairs={{0,0},{8,8},{16,16},{24,24},{40,32},{48,40},{56,48},{32,56},{80,64... | collective-permute-start | bytes 393224 | tf_op jit(solution)/shard_map/ppermute | solution.py:343
  38.7 1.0 %copy-start.1 = (bf16[2048,128]{1,0:T(8,128)(2,1)S(1)}, bf16[2048,128]{1,0:T(8,128)(2,1)}, u32[]{:S(2)}) copy-start(bf16[2048,128]{1,0:T(8,128)(2,1)} %ok.1) | copy-start | bytes 1572868
  50.1 4.8 %copy-start.5 = (s32[2048]{0:T(1024)S(1)}, s32[2048]{0:T(1024)}, u32[]{:S(2)}) copy-start(s32[2048]{0:T(1024)} %param.15) | copy-start | bytes 24580
  50.1 4.8 %copy-start.6 = (s32[2048]{0:T(1024)S(1)}, s32[2048]{0:T(1024)}, u32[]{:S(2)}) copy-start(s32[2048]{0:T(1024)} %param.14) | copy-start | bytes 24580
  50.1 17.6 %all-to-all-start.1 = ((s16[8,144,128]{2,1,0:T(8,128)(2,1)}), s16[8,144,128]{2,1,0:T(8,128)(2,1)S(1)}, u32[]{:S(2)}, u32[]{:S(2)}) async-start(s16[8,144,128]{2,1,0:T(8,128)(2,1)} %second.1.payload), calls=%async_computation.1 | async-start | bytes 589824 | tf_op jit(solution)/shard_map/all_to_all | solution.py:373
  56.2 5.6 %collective-permute-start.13 = (bf16[256,128]{1,0:T(8,128)(2,1)S(1)}, bf16[256,128]{1,0:T(8,128)(2,1)S(1)}, u32[]{:S(2)}, u32[]{:S(2)}) collective-permute-start(bf16[256,128]{1,0:T(8,128)(2,1)S(1)} %get-tuple-element.15), channel_id=1, source_target_pairs={{0,8},{8,16},{16,24},{24,0},{1,9},{9,17},{17,25},{25,1},{2,10},{10... | collective-permute-start | bytes 196616 | tf_op jit(solution)/shard_map/ppermute | solution.py:31
  57.0 5.1 %collective-permute-start.14 = (bf16[256,128]{1,0:T(8,128)(2,1)S(1)}, bf16[256,128]{1,0:T(8,128)(2,1)S(1)}, u32[]{:S(2)}, u32[]{:S(2)}) collective-permute-start(bf16[256,128]{1,0:T(8,128)(2,1)S(1)} %get-tuple-element.16), channel_id=1, source_target_pairs={{0,24},{8,0},{16,8},{24,16},{1,25},{9,1},{17,9},{25,17},{2,26},{10... | collective-permute-start | bytes 196616 | tf_op jit(solution)/shard_map/ppermute | solution.py:31
  59.6 5.8 %collective-permute-start.15 = (bf16[256,128]{1,0:T(8,128)(2,1)S(1)}, bf16[256,128]{1,0:T(8,128)(2,1)S(1)}, u32[]{:S(2)}, u32[]{:S(2)}) collective-permute-start(bf16[256,128]{1,0:T(8,128)(2,1)S(1)} %get-tuple-element.17), channel_id=1, source_target_pairs={{0,16},{8,24},{16,0},{24,8},{1,17},{9,25},{17,1},{25,9},{2,18},{10... | collective-permute-start | bytes 196616 | tf_op jit(solution)/shard_map/ppermute | solution.py:31

commit v4 on v3

--- a/solution.py
+++ b/solution.py
@@ -34,10 +34,6 @@
 def swapped(value, axis, bit):
     count = lax.axis_size(axis)
     return lax.ppermute(value, axis, [(i, i ^ bit) for i in range(count)])
-
-
-def across(row):
-    return jnp.transpose(jnp.broadcast_to(row, (BLOCK, BLOCK)), (1, 0))
 
 
 def split_fixed(value):
@@ -206,17 +202,19 @@
 
     take(q, [keys], values, top, total, acc, visible)
 
+    lane = lax.broadcasted_iota(I32, (BLOCK, BLOCK), 1)
     for j in range(8):
         rows = pl.ds(j * BLOCK, BLOCK)
         full = acc[rows, :]
-        size = jnp.max(jnp.transpose(jnp.abs(full), (1, 0)), axis=0, keepdims=True)
-        size = jnp.maximum(size, 1.2e-34)
-        number = jnp.round(full * across(32767.0 / size)).astype(I32).astype(jnp.int16)
-        weight = jnp.sum(jnp.transpose(total[rows, :], (1, 0)), axis=0, keepdims=True)
+        size = jnp.maximum(jnp.max(jnp.abs(full), axis=1, keepdims=True), 1.2e-34)
+        number = jnp.round(full * (32767.0 / size)).astype(I32).astype(jnp.int16)
+        weight = jnp.sum(total[rows, :], axis=1, keepdims=True)
+        turned = jnp.where(lane == 0, top[rows, :], jnp.where(lane == 1, weight, size))
+        turned = jnp.transpose(turned, (1, 0))
         stats = (
-            split_fixed(jnp.transpose(top[rows, :], (1, 0))[0:1, :] * SCALE)
-            + split_fixed(jnp.log2(weight))
-            + split_fixed(jnp.log2(size))
+            split_fixed(turned[0:1, :] * SCALE)
+            + split_fixed(jnp.log2(turned[1:2, :]))
+            + split_fixed(jnp.log2(turned[2:3, :]))
         )
         stats = jnp.concatenate(stats + [jnp.zeros((10, BLOCK), I32)], axis=0)
         out[j] = jnp.concatenate([number, stats.astype(jnp.int16)], axis=0)
@@ -381,7 +379,7 @@
         out_specs=(vmem(),) * 2,
         compiler_params=SMALL,
         name="merge",
-    )(parts, t0, t1, t2, t3)
+    )(parts, t3, t2, t1, t0)
     return attended.reshape(queries.shape), appended.reshape(BLOCK, 2, HD)
 
 

time: 69.9 us -> 70.6 us (1.010); the launches traced: 68.7 us -> 70.8 us
  starting transfers between devices: 30 us -> 35.1 us
  Pallas kernels: 12.8 us -> 10.8 us
  waiting for transfers between devices: 19.3 us -> 18.3 us
    all_to_all x1, starting transfers between devices: 4.76 us -> 9.33 us  [shards(): parts = lax.all_to_all(payload, 'z', 0, 0)]
    pallas_call x1, Pallas kernels: 7.07 us -> 5.23 us  [shards(): pl.pallas_call(first_kernel, out_shape=(state,) * 3, in_specs=[smem()] *...]
  transfers between devices with their start and end apart: 18 -> 18, of which waited for: 9 -> 9; matrix products, arithmetic and copies ran while one was open for 3% -> 3% of each run, Pallas kernels for 13% -> 10%
where the time goes in v4:
time: 70.6 us; the launch traced here: 70.8 us
  starting transfers between devices  35.1 us (50%)
  waiting for transfers between devices  18.3 us (26%)
  Pallas kernels  10.8 us (15%)
  local copies, waits for them, and re-layouts  4.37 us (6%)
  between operations  1.48 us (2%)
  other arithmetic  0.71 us (1%)
    ppermute x10, starting transfers between devices, shifted(): lax.ppermute(value, axis, [(i, (i + steps) % count) for i in range(count)])  15.4 us
    all_to_all x1, starting transfers between devices, shards(): parts = lax.all_to_all(payload, 'z', 0, 0)  9.33 us
    all_to_all x1, starting transfers between devices, shards(): q3 = lax.all_to_all(sent, 'z', 0, 0)  8.47 us
    ppermute x10, waiting for transfers between devices, shifted(): lax.ppermute(value, axis, [(i, (i + steps) % count) for i in range(count)])  7.57 us
    all_to_all x1, waiting for transfers between devices, shards(): q3 = lax.all_to_all(sent, 'z', 0, 0)  7.55 us
    pallas_call x1, Pallas kernels, shards(): pl.pallas_call(first_kernel, out_shape=(state,) * 3, in_specs=[smem()] *...  5.23 us
    pallas_call x1, Pallas kernels, shards(): pl.pallas_call(second_kernel, out_shape=jax.ShapeDtypeStruct((8, PAYLOAD,...  3.05 us
    all_to_all x1, waiting for transfers between devices, shards(): parts = lax.all_to_all(payload, 'z', 0, 0)  2.02 us
  transfers between devices with their start and end apart: 18, of which 9 were waited for; matrix products, arithmetic and copies ran while one was open for 3% of the time, Pallas kernels for 10%

profile of v4, /device:TPU:8, one launch (start us, length us, event | category | flops | bytes accessed | tf_op | source)
XLA Modules:
  0.0 70.8 jit_solution(11956886492612408742)
XLA Ops:
  1.3 0.7 fusion.3
  1.9 1.1 %constant_dynamic-slice_fusion.1 = (bf16[4,1,256,128]{3,2,1,0:T(8,128)(2,1)S(1)}, bf16[4,1,256,128]{3,2,1,0:T(8,128)(2,1)S(1)}) fusion(bf16[4,2,256,128]{3,2,1,0:T(8,128)(2,1)} %bitcast.21, s32[]{:T(128)S(6)} %select_n.22, bf16[4,2,256,128]{3,2,1,0:T(8,128)(2,1)} %bitcast.22), kind=kLoop, calls=%fused_computation.9 | loop fusion | bytes 1048580 | tf_op jit(solution)/shard_map/jit(dynamic_index_in_dim)/dynamic_slice | solution.py:289
  3.0 0.0 copy-start.3
  3.0 0.0 copy-start.2
  3.1 1.6 %collective-permute-start.1 = (bf16[2064,128]{1,0:T(8,128)(2,1)S(1)}, bf16[2064,128]{1,0:T(8,128)(2,1)}, u32[]{:S(2)}, u32[]{:S(2)}) collective-permute-start(bf16[2064,128]{1,0:T(8,128)(2,1)S(1)} %fusion.1), channel_id=1, source_target_pairs={{0,8},{8,16},{16,24},{24,0},{1,9},{9,17},{17,25},{25,1},{2,10},{10... | collective-permute-start | bytes 1585160 | tf_op jit(solution)/shard_map/ppermute | solution.py:31
  4.6 1.7 %collective-permute-start.3 = (bf16[2064,128]{1,0:T(8,128)(2,1)S(1)}, bf16[2064,128]{1,0:T(8,128)(2,1)S(1)}, u32[]{:S(2)}, u32[]{:S(2)}) collective-permute-start(bf16[2064,128]{1,0:T(8,128)(2,1)S(1)} %fusion.1), channel_id=1, source_target_pairs={{0,24},{8,0},{16,8},{24,16},{1,25},{9,1},{17,9},{25,17},{2,26},{10... | collective-permute-start | bytes 1585160 | tf_op jit(solution)/shard_map/ppermute | solution.py:31
  6.4 0.0 collective-permute-start
  6.4 1.2 %collective-permute-done.far = bf16[16,128]{1,0:T(8,128)(2,1)S(1)} collective-permute-done((bf16[16,128]{1,0:T(8,128)(2,1)S(1)}, bf16[16,128]{1,0:T(8,128)(2,1)S(1)}, u32[]{:S(2)}, u32[]{:S(2)}) %collective-permute-start) | collective-permute-done | bytes 4128 | tf_op jit(solution)/shard_map/ppermute | solution.py:36
  7.6 0.8 %gather.1 = bf16[8,160,128]{2,1,0:T(8,128)(2,1)} custom-call(bf16[128,128]{1,0:T(8,128)(2,1)S(1)} %bitcast.23, bf16[16,128]{1,0:T(8,128)(2,1)S(1)} %bitcast.25, bf16[16,128]{1,0:T(8,128)(2,1)S(1)} %collective-permute-done.far), custom_call_target="tpu_custom_call" | custom-call | tf_op jit(solution)/shard_map/gather/pallas_call | solution.py:301
  8.3 8.5 %all-to-all-start = ((bf16[8,160,128]{2,1,0:T(8,128)(2,1)}), bf16[8,160,128]{2,1,0:T(8,128)(2,1)S(1)}, u32[]{:S(2)}, u32[]{:S(2)}) async-start(bf16[8,160,128]{2,1,0:T(8,128)(2,1)} %gather.1), calls=%async_computation | async-start | bytes 655360 | tf_op jit(solution)/shard_map/all_to_all | solution.py:309
  16.8 1.4 %collective-permute-done.1.an = bf16[2064,128]{1,0:T(8,128)(2,1)} collective-permute-done((bf16[2064,128]{1,0:T(8,128)(2,1)S(1)}, bf16[2064,128]{1,0:T(8,128)(2,1)}, u32[]{:S(2)}, u32[]{:S(2)}) %collective-permute-start.1) | collective-permute-done | bytes 528416 | tf_op jit(solution)/shard_map/ppermute | solution.py:31
  18.2 0.0 collective-permute-start.7
  18.2 0.0 collective-permute-done.3.bn
  18.2 0.5 collective-permute-start.8
  18.8 2.4 %collective-permute-start.4 = (bf16[1040,128]{1,0:T(8,128)(2,1)S(1)}, bf16[1040,128]{1,0:T(8,128)(2,1)S(1)}, u32[]{:S(2)}, u32[]{:S(2)}) collective-permute-start(bf16[1040,128]{1,0:T(8,128)(2,1)S(1)} %slice.9), channel_id=1, source_target_pairs={{0,24},{8,0},{16,8},{24,16},{1,25},{9,1},{17,9},{25,17},{2,26},{10... | collective-permute-start | bytes 798728 | tf_op jit(solution)/shard_map/ppermute | solution.py:31
  21.2 1.7 %slice.8 = bf16[1024,128]{1,0:T(8,128)(2,1)} slice(bf16[2064,128]{1,0:T(8,128)(2,1)} %collective-permute-done.1.an), slice={[0:1024], [0:128]} | slice | bytes 524288 | tf_op jit(solution)/shard_map/slice | solution.py:296
  22.9 0.0 collective-permute-start.2
  22.9 7.6 %all-to-all-done.q3 = bf16[8,160,128]{2,1,0:T(8,128)(2,1)S(1)} async-done(((bf16[8,160,128]{2,1,0:T(8,128)(2,1)}), bf16[8,160,128]{2,1,0:T(8,128)(2,1)S(1)}, u32[]{:S(2)}, u32[]{:S(2)}) %all-to-all-start) | async-done | bytes 327712 | tf_op jit(solution)/shard_map/all_to_all | solution.py:309
  30.4 0.0 collective-permute-done.7.af
  30.4 0.0 collective-permute-done.8.bf
  30.4 0.5 collective-permute-start.10
  31.0 2.6 %collective-permute-start.11 = (bf16[256,128]{1,0:T(8,128)(2,1)S(1)}, bf16[256,128]{1,0:T(8,128)(2,1)S(1)}, u32[]{:S(2)}, u32[]{:S(2)}) collective-permute-start(bf16[256,128]{1,0:T(8,128)(2,1)S(1)} %rows.1.r0), channel_id=1, source_target_pairs={{0,4},{2,6},{4,0},{6,2},{1,5},{3,7},{5,1},{7,3},{8,12},{10,14},{12... | collective-permute-start | bytes 196616 | tf_op jit(solution)/shard_map/ppermute | solution.py:31
  33.6 1.9 %collective-permute-start.9 = (bf16[256,128]{1,0:T(8,128)(2,1)S(1)}, bf16[256,128]{1,0:T(8,128)(2,1)S(1)}, u32[]{:S(2)}, u32[]{:S(2)}) collective-permute-start(bf16[256,128]{1,0:T(8,128)(2,1)S(1)} %rows.1.r0), channel_id=1, source_target_pairs={{0,2},{2,4},{4,6},{6,0},{1,3},{3,5},{5,7},{7,1},{8,10},{10,12},{12... | collective-permute-start | bytes 196616 | tf_op jit(solution)/shard_map/ppermute | solution.py:31
  35.5 0.0 collective-permute-done.4.cvn
  35.5 0.5 collective-permute-start.5
  36.0 0.0 collective-permute-done.10.r2
  36.0 0.9 %collective-permute-done.11.r3 = bf16[256,128]{1,0:T(8,128)(2,1)S(1)} collective-permute-done((bf16[256,128]{1,0:T(8,128)(2,1)S(1)}, bf16[256,128]{1,0:T(8,128)(2,1)S(1)}, u32[]{:S(2)}, u32[]{:S(2)}) %collective-permute-start.11) | collective-permute-done | bytes 65568 | tf_op jit(solution)/shard_map/ppermute | solution.py:31
  36.9 1.0 %collective-permute-done.9.r1 = bf16[256,128]{1,0:T(8,128)(2,1)S(1)} collective-permute-done((bf16[256,128]{1,0:T(8,128)(2,1)S(1)}, bf16[256,128]{1,0:T(8,128)(2,1)S(1)}, u32[]{:S(2)}, u32[]{:S(2)}) %collective-permute-start.9) | collective-permute-done | bytes 65568 | tf_op jit(solution)/shard_map/ppermute | solution.py:31
  37.8 0.8 %collective-permute-start.12 = (bf16[512,128]{1,0:T(8,128)(2,1)S(1)}, bf16[512,128]{1,0:T(8,128)(2,1)S(1)}, u32[]{:S(2)}, u32[]{:S(2)}) collective-permute-start(bf16[512,128]{1,0:T(8,128)(2,1)S(1)} %select.6), channel_id=1, source_target_pairs={{0,0},{8,8},{16,16},{24,24},{40,32},{48,40},{56,48},{32,56},{80,64... | collective-permute-start | bytes 393224 | tf_op jit(solution)/shard_map/ppermute | solution.py:341
  38.7 0.0 copy-start.1
  38.7 1.0 %copy-done.1 = bf16[2048,128]{1,0:T(8,128)(2,1)S(1)} copy-done((bf16[2048,128]{1,0:T(8,128)(2,1)S(1)}, bf16[2048,128]{1,0:T(8,128)(2,1)}, u32[]{:S(2)}) %copy-start.1) | copy-done | bytes 524312
  39.8 5.2 %first.1 = (f32[1024,128]{1,0:T(8,128)S(1)}, f32[1024,128]{1,0:T(8,128)S(1)}, f32[1024,128]{1,0:T(8,128)S(1)}) custom-call(s32[1,4]{1,0:T(1,128)S(1)} %copy-done.4, s32[1]{0:T(128)} %copy.31.live, bf16[8,160,128]{2,1,0:T(8,128)(2,1)S(1)} %all-to-all-done.q3, bf16[2048,128]{1,0:T(8,128)(2,1)S(1)} %copy-done.1, bf16[2048,128]{1,0:T(8,128)(2,1)S(1)} %copy-done, ...), custom_call_target="tpu_custom_call" | custom-call | flops 2147483648 | bytes 1048576 | tf_op jit(solution)/shard_map/first/pallas_call | solution.py:323
  45.0 0.0 collective-permute-done.5.ckf
  45.0 0.0 collective-permute-done.12.new
  45.0 3.1 %second.1.payload = s16[8,144,128]{2,1,0:T(8,128)(2,1)} custom-call(bf16[8,160,128]{2,1,0:T(8,128)(2,1)S(1)} %all-to-all-done.q3, bf16[1024,128]{1,0:T(8,128)(2,1)S(1)} %collective-permute-done.2.ckn, bf16[1040,128]{1,0:T(8,128)(2,1)S(1)} %collective-permute-done.4.cvn, bf16[1024,128]{1,0:T(8,128)(2,1)S(1)} %collective-permute-done.5.ckf, ...), custom_call_target="tpu_custom_call" | custom-call | flops 268435456 | bytes 1048576 | tf_op jit(solution)/shard_map/second/pallas_call | solution.py:344
  48.1 9.3 %all-to-all-start.1 = ((s16[8,144,128]{2,1,0:T(8,128)(2,1)}), s16[8,144,128]{2,1,0:T(8,128)(2,1)S(1)}, u32[]{:S(2)}, u32[]{:S(2)}) async-start(s16[8,144,128]{2,1,0:T(8,128)(2,1)} %second.1.payload), calls=%async_computation.1 | async-start | bytes 589824 | tf_op jit(solution)/shard_map/all_to_all | solution.py:371
  57.5 0.2 reshape.52
  57.7 0.2 copy.25
  58.0 0.1 copy.24.code
  58.0 0.8 %route.1 = (bf16[256,128]{1,0:T(8,128)(2,1)S(1)}, bf16[256,128]{1,0:T(8,128)(2,1)S(1)}, bf16[256,128]{1,0:T(8,128)(2,1)S(1)}, bf16[256,128]{1,0:T(8,128)(2,1)S(1)}) custom-call(bf16[256,128]{1,0:T(8,128)(2,1)S(1)} %rows.1.r0, bf16[256,128]{1,0:T(8,128)(2,1)S(1)} %collective-permute-done.9.r1, bf16[256,128]{1,0:T(8,128)(2,1)S(1)} %collective-permute-done.10.r2, ...), custom_call_target="tpu_custom_call" | custom-call | tf_op jit(solution)/shard_map/route/pallas_call | solution.py:360
  58.8 2.6 %collective-permute-start.13 = (bf16[256,128]{1,0:T(8,128)(2,1)S(1)}, bf16[256,128]{1,0:T(8,128)(2,1)S(1)}, u32[]{:S(2)}, u32[]{:S(2)}) collective-permute-start(bf16[256,128]{1,0:T(8,128)(2,1)S(1)} %get-tuple-element.14), channel_id=1, source_target_pairs={{0,16},{8,24},{16,0},{24,8},{1,17},{9,25},{17,1},{25,9},{2,18},{10... | collective-permute-start | bytes 196616 | tf_op jit(solution)/shard_map/ppermute | solution.py:31
  61.4 0.8 %collective-permute-start.14 = (bf16[256,128]{1,0:T(8,128)(2,1)S(1)}, bf16[256,128]{1,0:T(8,128)(2,1)S(1)}, u32[]{:S(2)}, u32[]{:S(2)}) collective-permute-start(bf16[256,128]{1,0:T(8,128)(2,1)S(1)} %get-tuple-element.15), channel_id=1, source_target_pairs={{0,24},{8,0},{16,8},{24,16},{1,25},{9,1},{17,9},{25,17},{2,26},{10... | collective-permute-start | bytes 196616 | tf_op jit(solution)/shard_map/ppermute | solution.py:31
  62.3 1.2 %collective-permute-start.15 = (bf16[256,128]{1,0:T(8,128)(2,1)S(1)}, bf16[256,128]{1,0:T(8,128)(2,1)S(1)}, u32[]{:S(2)}, u32[]{:S(2)}) collective-permute-start(bf16[256,128]{1,0:T(8,128)(2,1)S(1)} %get-tuple-element.16), channel_id=1, source_target_pairs={{0,8},{8,16},{16,24},{24,0},{1,9},{9,17},{17,25},{25,1},{2,10},{10... | collective-permute-start | bytes 196616 | tf_op jit(solution)/shard_map/ppermute | solution.py:31
  63.5 1.8 %collective-permute-done.13.n0 = bf16[256,128]{1,0:T(8,128)(2,1)S(1)} collective-permute-done((bf16[256,128]{1,0:T(8,128)(2,1)S(1)}, bf16[256,128]{1,0:T(8,128)(2,1)S(1)}, u32[]{:S(2)}, u32[]{:S(2)}) %collective-permute-start.13) | collective-permute-done | bytes 65568 | tf_op jit(solution)/shard_map/ppermute | solution.py:31
  65.3 0.4 collective-permute-done.14.n1
  65.7 2.1 %collective-permute-done.15.n2 = bf16[256,128]{1,0:T(8,128)(2,1)S(1)} collective-permute-done((bf16[256,128]{1,0:T(8,128)(2,1)S(1)}, bf16[256,128]{1,0:T(8,128)(2,1)S(1)}, u32[]{:S(2)}, u32[]{:S(2)}) %collective-permute-start.15) | collective-permute-done | bytes 65568 | tf_op jit(solution)/shard_map/ppermute | solution.py:31
  67.8 2.0 %all-to-all-done.1.parts = s16[8,144,128]{2,1,0:T(8,128)(2,1)S(1)} async-done(((s16[8,144,128]{2,1,0:T(8,128)(2,1)}), s16[8,144,128]{2,1,0:T(8,128)(2,1)S(1)}, u32[]{:S(2)}, u32[]{:S(2)}) %all-to-all-start.1) | async-done | bytes 294944 | tf_op jit(solution)/shard_map/all_to_all | solution.py:371
  69.8 1.0 %merge.1 = (bf16[128,128]{1,0:T(8,128)(2,1)}, bf16[256,128]{1,0:T(8,128)(2,1)}) custom-call(s16[8,144,128]{2,1,0:T(8,128)(2,1)S(1)} %all-to-all-done.1.parts, bf16[256,128]{1,0:T(8,128)(2,1)S(1)} %collective-permute-done.13.n0, bf16[256,128]{1,0:T(8,128)(2,1)S(1)} %collective-permute-done.14.n1, bf16[256,128]{1,0:T(8,128)(2,1)S(1)} %collective-permute-done.15.n2, ...), custom_call_target="tpu_custom_call" | custom-call | tf_op jit(solution)/shard_map/merge/pallas_call | solution.py:372
  (22 shorter events, 0.2 us)
Async XLA Ops:
  3.0 3.4 %copy-start.3 = (bf16[8,2,128]{2,1,0:T(2,128)(2,1)S(1)}, bf16[8,2,128]{2,1,0:T(2,128)(2,1)}, u32[]{:S(2)}) copy-start(bf16[8,2,128]{2,1,0:T(2,128)(2,1)} %param.13) | copy-start | bytes 12292
  3.0 4.5 %copy-start.2 = (bf16[64,2,128]{2,1,0:T(2,128)(2,1)S(1)}, bf16[64,2,128]{2,1,0:T(2,128)(2,1)}, u32[]{:S(2)}) copy-start(bf16[64,2,128]{2,1,0:T(2,128)(2,1)} %param.8) | copy-start | bytes 98308
  3.1 15.1 %collective-permute-start.1 = (bf16[2064,128]{1,0:T(8,128)(2,1)S(1)}, bf16[2064,128]{1,0:T(8,128)(2,1)}, u32[]{:S(2)}, u32[]{:S(2)}) collective-permute-start(bf16[2064,128]{1,0:T(8,128)(2,1)S(1)} %fusion.1), channel_id=1, source_target_pairs={{0,8},{8,16},{16,24},{24,0},{1,9},{9,17},{17,25},{25,1},{2,10},{10... | collective-permute-start | bytes 1585160 | tf_op jit(solution)/shard_map/ppermute | solution.py:31
  4.6 13.6 %collective-permute-start.3 = (bf16[2064,128]{1,0:T(8,128)(2,1)S(1)}, bf16[2064,128]{1,0:T(8,128)(2,1)S(1)}, u32[]{:S(2)}, u32[]{:S(2)}) collective-permute-start(bf16[2064,128]{1,0:T(8,128)(2,1)S(1)} %fusion.1), channel_id=1, source_target_pairs={{0,24},{8,0},{16,8},{24,16},{1,25},{9,1},{17,9},{25,17},{2,26},{10... | collective-permute-start | bytes 1585160 | tf_op jit(solution)/shard_map/ppermute | solution.py:31
  6.4 1.2 %collective-permute-start = (bf16[16,128]{1,0:T(8,128)(2,1)S(1)}, bf16[16,128]{1,0:T(8,128)(2,1)S(1)}, u32[]{:S(2)}, u32[]{:S(2)}) collective-permute-start(bf16[16,128]{1,0:T(8,128)(2,1)S(1)} %bitcast.24), channel_id=1, source_target_pairs={{0,1},{1,0},{2,3},{3,2},{4,5},{5,4},{6,7},{7,6},{8,9},{9,8},{10,11... | collective-permute-start | bytes 12296 | tf_op jit(solution)/shard_map/ppermute | solution.py:36
  8.3 22.1 %all-to-all-start = ((bf16[8,160,128]{2,1,0:T(8,128)(2,1)}), bf16[8,160,128]{2,1,0:T(8,128)(2,1)S(1)}, u32[]{:S(2)}, u32[]{:S(2)}) async-start(bf16[8,160,128]{2,1,0:T(8,128)(2,1)} %gather.1), calls=%async_computation | async-start | bytes 655360 | tf_op jit(solution)/shard_map/all_to_all | solution.py:309
  18.2 12.2 %collective-permute-start.7 = (bf16[2064,128]{1,0:T(8,128)(2,1)}, bf16[2064,128]{1,0:T(8,128)(2,1)S(1)}, u32[]{:S(2)}, u32[]{:S(2)}) collective-permute-start(bf16[2064,128]{1,0:T(8,128)(2,1)} %collective-permute-done.1.an), channel_id=1, source_target_pairs={{0,1},{1,0},{2,3},{3,2},{4,5},{5,4},{6,7},{7,6},{8,9},{9,8},{10,11... | collective-permute-start | bytes 1585160 | tf_op jit(solution)/shard_map/ppermute | solution.py:36
  18.2 12.2 %collective-permute-start.8 = (bf16[2064,128]{1,0:T(8,128)(2,1)S(1)}, bf16[2064,128]{1,0:T(8,128)(2,1)S(1)}, u32[]{:S(2)}, u32[]{:S(2)}) collective-permute-start(bf16[2064,128]{1,0:T(8,128)(2,1)S(1)} %collective-permute-done.3.bn), channel_id=1, source_target_pairs={{0,1},{1,0},{2,3},{3,2},{4,5},{5,4},{6,7},{7,6},{8,9},{9,8},{10,11... | collective-permute-start | bytes 1585160 | tf_op jit(solution)/shard_map/ppermute | solution.py:36
  18.8 16.7 %collective-permute-start.4 = (bf16[1040,128]{1,0:T(8,128)(2,1)S(1)}, bf16[1040,128]{1,0:T(8,128)(2,1)S(1)}, u32[]{:S(2)}, u32[]{:S(2)}) collective-permute-start(bf16[1040,128]{1,0:T(8,128)(2,1)S(1)} %slice.9), channel_id=1, source_target_pairs={{0,24},{8,0},{16,8},{24,16},{1,25},{9,1},{17,9},{25,17},{2,26},{10... | collective-permute-start | bytes 798728 | tf_op jit(solution)/shard_map/ppermute | solution.py:31
  22.9 15.8 %copy-start = (bf16[2048,128]{1,0:T(8,128)(2,1)S(1)}, bf16[2048,128]{1,0:T(8,128)(2,1)}, u32[]{:S(2)}) copy-start(bf16[2048,128]{1,0:T(8,128)(2,1)} %ov.1) | copy-start | bytes 1572868
  22.9 15.8 %copy-start.4 = (s32[1,4]{1,0:T(1,128)S(1)}, s32[1,4]{1,0:T(1,128)}, u32[]{:S(2)}) copy-start(s32[1,4]{1,0:T(1,128)} %table.1) | copy-start | bytes 52
  22.9 12.6 %collective-permute-start.2 = (bf16[1024,128]{1,0:T(8,128)(2,1)}, bf16[1024,128]{1,0:T(8,128)(2,1)S(1)}, u32[]{:S(2)}, u32[]{:S(2)}) collective-permute-start(bf16[1024,128]{1,0:T(8,128)(2,1)} %slice.8), channel_id=1, source_target_pairs={{0,8},{8,16},{16,24},{24,0},{1,9},{9,17},{17,25},{25,1},{2,10},{10... | collective-permute-start | bytes 786440 | tf_op jit(solution)/shard_map/ppermute | solution.py:31
  30.4 5.5 %collective-permute-start.10 = (bf16[256,128]{1,0:T(8,128)(2,1)S(1)}, bf16[256,128]{1,0:T(8,128)(2,1)S(1)}, u32[]{:S(2)}, u32[]{:S(2)}) collective-permute-start(bf16[256,128]{1,0:T(8,128)(2,1)S(1)} %rows.1.r0), channel_id=1, source_target_pairs={{0,6},{2,0},{4,2},{6,4},{1,7},{3,1},{5,3},{7,5},{8,14},{10,8},{12,... | collective-permute-start | bytes 196616 | tf_op jit(solution)/shard_map/ppermute | solution.py:31
  31.0 5.9 %collective-permute-start.11 = (bf16[256,128]{1,0:T(8,128)(2,1)S(1)}, bf16[256,128]{1,0:T(8,128)(2,1)S(1)}, u32[]{:S(2)}, u32[]{:S(2)}) collective-permute-start(bf16[256,128]{1,0:T(8,128)(2,1)S(1)} %rows.1.r0), channel_id=1, source_target_pairs={{0,4},{2,6},{4,0},{6,2},{1,5},{3,7},{5,1},{7,3},{8,12},{10,14},{12... | collective-permute-start | bytes 196616 | tf_op jit(solution)/shard_map/ppermute | solution.py:31
  33.6 4.3 %collective-permute-start.9 = (bf16[256,128]{1,0:T(8,128)(2,1)S(1)}, bf16[256,128]{1,0:T(8,128)(2,1)S(1)}, u32[]{:S(2)}, u32[]{:S(2)}) collective-permute-start(bf16[256,128]{1,0:T(8,128)(2,1)S(1)} %rows.1.r0), channel_id=1, source_target_pairs={{0,2},{2,4},{4,6},{6,0},{1,3},{3,5},{5,7},{7,1},{8,10},{10,12},{12... | collective-permute-start | bytes 196616 | tf_op jit(solution)/shard_map/ppermute | solution.py:31
  35.5 9.6 %collective-permute-start.6 = (bf16[1040,128]{1,0:T(8,128)(2,1)S(1)}, bf16[1040,128]{1,0:T(8,128)(2,1)S(1)}, u32[]{:S(2)}, u32[]{:S(2)}) collective-permute-start(bf16[1040,128]{1,0:T(8,128)(2,1)S(1)} %collective-permute-done.4.cvn), channel_id=1, source_target_pairs={{0,1},{1,0},{2,3},{3,2},{4,5},{5,4},{6,7},{7,6},{8,9},{9,8},{10,11... | collective-permute-start | bytes 798728 | tf_op jit(solution)/shard_map/ppermute | solution.py:36
  35.5 9.5 %collective-permute-start.5 = (bf16[1024,128]{1,0:T(8,128)(2,1)S(1)}, bf16[1024,128]{1,0:T(8,128)(2,1)S(1)}, u32[]{:S(2)}, u32[]{:S(2)}) collective-permute-start(bf16[1024,128]{1,0:T(8,128)(2,1)S(1)} %collective-permute-done.2.ckn), channel_id=1, source_target_pairs={{0,1},{1,0},{2,3},{3,2},{4,5},{5,4},{6,7},{7,6},{8,9},{9,8},{10,11... | collective-permute-start | bytes 786440 | tf_op jit(solution)/shard_map/ppermute | solution.py:36
  37.8 7.2 %collective-permute-start.12 = (bf16[512,128]{1,0:T(8,128)(2,1)S(1)}, bf16[512,128]{1,0:T(8,128)(2,1)S(1)}, u32[]{:S(2)}, u32[]{:S(2)}) collective-permute-start(bf16[512,128]{1,0:T(8,128)(2,1)S(1)} %select.6), channel_id=1, source_target_pairs={{0,0},{8,8},{16,16},{24,24},{40,32},{48,40},{56,48},{32,56},{80,64... | collective-permute-start | bytes 393224 | tf_op jit(solution)/shard_map/ppermute | solution.py:341
  38.7 1.0 %copy-start.1 = (bf16[2048,128]{1,0:T(8,128)(2,1)S(1)}, bf16[2048,128]{1,0:T(8,128)(2,1)}, u32[]{:S(2)}) copy-start(bf16[2048,128]{1,0:T(8,128)(2,1)} %ok.1) | copy-start | bytes 1572868
  48.1 9.3 %copy-start.5 = (s32[2048]{0:T(1024)S(1)}, s32[2048]{0:T(1024)}, u32[]{:S(2)}) copy-start(s32[2048]{0:T(1024)} %param.15) | copy-start | bytes 24580
  48.1 9.3 %copy-start.6 = (s32[2048]{0:T(1024)S(1)}, s32[2048]{0:T(1024)}, u32[]{:S(2)}) copy-start(s32[2048]{0:T(1024)} %param.14) | copy-start | bytes 24580
  48.1 21.7 %all-to-all-start.1 = ((s16[8,144,128]{2,1,0:T(8,128)(2,1)}), s16[8,144,128]{2,1,0:T(8,128)(2,1)S(1)}, u32[]{:S(2)}, u32[]{:S(2)}) async-start(s16[8,144,128]{2,1,0:T(8,128)(2,1)} %second.1.payload), calls=%async_computation.1 | async-start | bytes 589824 | tf_op jit(solution)/shard_map/all_to_all | solution.py:371
  58.8 6.5 %collective-permute-start.13 = (bf16[256,128]{1,0:T(8,128)(2,1)S(1)}, bf16[256,128]{1,0:T(8,128)(2,1)S(1)}, u32[]{:S(2)}, u32[]{:S(2)}) collective-permute-start(bf16[256,128]{1,0:T(8,128)(2,1)S(1)} %get-tuple-element.14), channel_id=1, source_target_pairs={{0,16},{8,24},{16,0},{24,8},{1,17},{9,25},{17,1},{25,9},{2,18},{10... | collective-permute-start | bytes 196616 | tf_op jit(solution)/shard_map/ppermute | solution.py:31
  61.4 4.3 %collective-permute-start.14 = (bf16[256,128]{1,0:T(8,128)(2,1)S(1)}, bf16[256,128]{1,0:T(8,128)(2,1)S(1)}, u32[]{:S(2)}, u32[]{:S(2)}) collective-permute-start(bf16[256,128]{1,0:T(8,128)(2,1)S(1)} %get-tuple-element.15), channel_id=1, source_target_pairs={{0,24},{8,0},{16,8},{24,16},{1,25},{9,1},{17,9},{25,17},{2,26},{10... | collective-permute-start | bytes 196616 | tf_op jit(solution)/shard_map/ppermute | solution.py:31
  62.3 5.5 %collective-permute-start.15 = (bf16[256,128]{1,0:T(8,128)(2,1)S(1)}, bf16[256,128]{1,0:T(8,128)(2,1)S(1)}, u32[]{:S(2)}, u32[]{:S(2)}) collective-permute-start(bf16[256,128]{1,0:T(8,128)(2,1)S(1)} %get-tuple-element.16), channel_id=1, source_target_pairs={{0,8},{8,16},{16,24},{24,0},{1,9},{9,17},{17,25},{25,1},{2,10},{10... | collective-permute-start | bytes 196616 | tf_op jit(solution)/shard_map/ppermute | solution.py:31

commit v5 on v3

--- a/solution.py
+++ b/solution.py
@@ -128,7 +128,7 @@
     return mask
 
 
-def rows_kernel(q3, af, bf, out):
+def rows_kernel(q3, af, bf, ok, ov, out):
     for b in range(8):
         out[b * 32 : b * 32 + 32, :] = q3[b, BLOCK:SENT, :]
 
@@ -312,11 +312,11 @@
     rows = pl.pallas_call(
         rows_kernel,
         out_shape=jax.ShapeDtypeStruct((256, HD), BF16),
-        in_specs=[vmem()] * 3,
+        in_specs=[vmem()] * 5,
         out_specs=vmem(),
         compiler_params=SMALL,
         name="rows",
-    )(q3, af, bf)
+    )(q3, af, bf, cache_keys, cache_values)
     opposite = shifted(rows, "y", 2)
     rows = [rows, shifted(rows, "y", 1), shifted(rows, "y", -1), opposite]
 

time: 69.9 us -> 69.3 us (level)
  waiting for transfers between devices: 19.3 us -> 18 us
  Pallas kernels: 12.8 us -> 13.7 us
  starting transfers between devices: 30 us -> 29.3 us
    pallas_call x1, Pallas kernels: 3.21 us -> 4.07 us  [shards(): pl.pallas_call(second_kernel, out_shape=jax.ShapeDtypeStruct((8, PAYLOAD,...]
    all_to_all x1, waiting for transfers between devices: 2.42 us -> 1.71 us  [shards(): parts = lax.all_to_all(payload, 'z', 0, 0)]
  transfers between devices with their start and end apart: 18 -> 18, of which waited for: 9 -> 9; matrix products, arithmetic and copies ran while one was open for 3% -> 4% of each run, Pallas kernels for 13% -> 13%
where the time goes in v5:
time: 69.3 us; the launch traced here: 67.9 us
  starting transfers between devices  29.3 us (42%)
  waiting for transfers between devices  18 us (26%)
  Pallas kernels  13.7 us (20%)
  local copies, waits for them, and re-layouts  4.67 us (7%)
  between operations  1.5 us (2%)
  other arithmetic  0.71 us (1%)
    ppermute x10, starting transfers between devices, shifted(): lax.ppermute(value, axis, [(i, (i + steps) % count) for i in range(count)])  14.8 us
    all_to_all x1, starting transfers between devices, shards(): q3 = lax.all_to_all(sent, 'z', 0, 0)  8.47 us
    ppermute x10, waiting for transfers between devices, shifted(): lax.ppermute(value, axis, [(i, (i + steps) % count) for i in range(count)])  8.26 us
    pallas_call x1, Pallas kernels, shards(): pl.pallas_call(first_kernel, out_shape=(state,) * 3, in_specs=[smem()] *...  7.07 us
    all_to_all x1, waiting for transfers between devices, shards(): q3 = lax.all_to_all(sent, 'z', 0, 0)  6.89 us
    all_to_all x1, starting transfers between devices, shards(): parts = lax.all_to_all(payload, 'z', 0, 0)  4.18 us
    pallas_call x1, Pallas kernels, shards(): pl.pallas_call(second_kernel, out_shape=jax.ShapeDtypeStruct((8, PAYLOAD,...  4.07 us
    slice x2, local copies, waits for them, and re-layouts, shards(): ckn, cvn = (shifted(an[:SIDE], 'x', 1), shifted(bn[SIDE:], 'x', -1))  2.38 us
  transfers between devices with their start and end apart: 18, of which 9 were waited for; matrix products, arithmetic and copies ran while one was open for 4% of the time, Pallas kernels for 13%

profile of v5, /device:TPU:8, one launch (start us, length us, event | category | flops | bytes accessed | tf_op | source)
XLA Modules:
  0.0 67.9 jit_solution(15090771274733563646)
XLA Ops:
  1.3 0.7 fusion.3
  1.9 1.1 %constant_dynamic-slice_fusion.1 = (bf16[4,1,256,128]{3,2,1,0:T(8,128)(2,1)S(1)}, bf16[4,1,256,128]{3,2,1,0:T(8,128)(2,1)S(1)}) fusion(bf16[4,2,256,128]{3,2,1,0:T(8,128)(2,1)} %bitcast.21, s32[]{:T(128)S(6)} %select_n.22, bf16[4,2,256,128]{3,2,1,0:T(8,128)(2,1)} %bitcast.22), kind=kLoop, calls=%fused_computation.9 | loop fusion | bytes 1048580 | tf_op jit(solution)/shard_map/jit(dynamic_index_in_dim)/dynamic_slice | solution.py:291
  3.0 0.0 copy-start.5
  3.0 0.0 copy-start.4
  3.1 1.6 %collective-permute-start.1 = (bf16[2064,128]{1,0:T(8,128)(2,1)S(1)}, bf16[2064,128]{1,0:T(8,128)(2,1)}, u32[]{:S(2)}, u32[]{:S(2)}) collective-permute-start(bf16[2064,128]{1,0:T(8,128)(2,1)S(1)} %fusion.1), channel_id=1, source_target_pairs={{0,8},{8,16},{16,24},{24,0},{1,9},{9,17},{17,25},{25,1},{2,10},{10... | collective-permute-start | bytes 1585160 | tf_op jit(solution)/shard_map/ppermute | solution.py:31
  4.6 1.7 %collective-permute-start.3 = (bf16[2064,128]{1,0:T(8,128)(2,1)S(1)}, bf16[2064,128]{1,0:T(8,128)(2,1)S(1)}, u32[]{:S(2)}, u32[]{:S(2)}) collective-permute-start(bf16[2064,128]{1,0:T(8,128)(2,1)S(1)} %fusion.1), channel_id=1, source_target_pairs={{0,24},{8,0},{16,8},{24,16},{1,25},{9,1},{17,9},{25,17},{2,26},{10... | collective-permute-start | bytes 1585160 | tf_op jit(solution)/shard_map/ppermute | solution.py:31
  6.4 1.2 %collective-permute-done.far = bf16[16,128]{1,0:T(8,128)(2,1)S(1)} collective-permute-done((bf16[16,128]{1,0:T(8,128)(2,1)S(1)}, bf16[16,128]{1,0:T(8,128)(2,1)S(1)}, u32[]{:S(2)}, u32[]{:S(2)}) %collective-permute-start) | collective-permute-done | bytes 4128 | tf_op jit(solution)/shard_map/ppermute | solution.py:36
  7.6 0.8 %gather.1 = bf16[8,160,128]{2,1,0:T(8,128)(2,1)} custom-call(bf16[128,128]{1,0:T(8,128)(2,1)S(1)} %bitcast.23, bf16[16,128]{1,0:T(8,128)(2,1)S(1)} %bitcast.25, bf16[16,128]{1,0:T(8,128)(2,1)S(1)} %collective-permute-done.far), custom_call_target="tpu_custom_call" | custom-call | tf_op jit(solution)/shard_map/gather/pallas_call | solution.py:303
  8.3 8.5 %all-to-all-start = ((bf16[8,160,128]{2,1,0:T(8,128)(2,1)}), bf16[8,160,128]{2,1,0:T(8,128)(2,1)S(1)}, u32[]{:S(2)}, u32[]{:S(2)}) async-start(bf16[8,160,128]{2,1,0:T(8,128)(2,1)} %gather.1), calls=%async_computation | async-start | bytes 655360 | tf_op jit(solution)/shard_map/all_to_all | solution.py:311
  16.8 0.0 copy-start.1
  16.8 1.4 %collective-permute-done.1.an = bf16[2064,128]{1,0:T(8,128)(2,1)} collective-permute-done((bf16[2064,128]{1,0:T(8,128)(2,1)S(1)}, bf16[2064,128]{1,0:T(8,128)(2,1)}, u32[]{:S(2)}, u32[]{:S(2)}) %collective-permute-start.1) | collective-permute-done | bytes 528416 | tf_op jit(solution)/shard_map/ppermute | solution.py:31
  18.2 0.0 collective-permute-start.7
  18.2 0.0 collective-permute-done.3.bn
  18.2 0.5 collective-permute-start.8
  18.7 0.7 %slice.9 = bf16[1040,128]{1,0:T(8,128)(2,1)} slice(bf16[2064,128]{1,0:T(8,128)(2,1)S(1)} %collective-permute-done.3.bn), slice={[1024:2064], [0:128]} | slice | bytes 532480 | tf_op jit(solution)/shard_map/slice | solution.py:298
  19.5 2.4 %collective-permute-start.4 = (bf16[1040,128]{1,0:T(8,128)(2,1)}, bf16[1040,128]{1,0:T(8,128)(2,1)S(1)}, u32[]{:S(2)}, u32[]{:S(2)}) collective-permute-start(bf16[1040,128]{1,0:T(8,128)(2,1)} %slice.9), channel_id=1, source_target_pairs={{0,24},{8,0},{16,8},{24,16},{1,25},{9,1},{17,9},{25,17},{2,26},{10... | collective-permute-start | bytes 798728 | tf_op jit(solution)/shard_map/ppermute | solution.py:31
  21.9 1.7 %slice.8 = bf16[1024,128]{1,0:T(8,128)(2,1)} slice(bf16[2064,128]{1,0:T(8,128)(2,1)} %collective-permute-done.1.an), slice={[0:1024], [0:128]} | slice | bytes 524288 | tf_op jit(solution)/shard_map/slice | solution.py:298
  23.5 0.0 collective-permute-start.2
  23.5 6.9 %all-to-all-done.q3 = bf16[8,160,128]{2,1,0:T(8,128)(2,1)S(1)} async-done(((bf16[8,160,128]{2,1,0:T(8,128)(2,1)}), bf16[8,160,128]{2,1,0:T(8,128)(2,1)S(1)}, u32[]{:S(2)}, u32[]{:S(2)}) %all-to-all-start) | async-done | bytes 327712 | tf_op jit(solution)/shard_map/all_to_all | solution.py:311
  30.4 0.0 collective-permute-done.8.bf
  30.5 0.5 collective-permute-start.10
  31.0 2.6 %collective-permute-start.11 = (bf16[256,128]{1,0:T(8,128)(2,1)S(1)}, bf16[256,128]{1,0:T(8,128)(2,1)S(1)}, u32[]{:S(2)}, u32[]{:S(2)}) collective-permute-start(bf16[256,128]{1,0:T(8,128)(2,1)S(1)} %rows.1.r0), channel_id=1, source_target_pairs={{0,4},{2,6},{4,0},{6,2},{1,5},{3,7},{5,1},{7,3},{8,12},{10,14},{12... | collective-permute-start | bytes 196616 | tf_op jit(solution)/shard_map/ppermute | solution.py:31
  33.6 1.9 %collective-permute-start.9 = (bf16[256,128]{1,0:T(8,128)(2,1)S(1)}, bf16[256,128]{1,0:T(8,128)(2,1)S(1)}, u32[]{:S(2)}, u32[]{:S(2)}) collective-permute-start(bf16[256,128]{1,0:T(8,128)(2,1)S(1)} %rows.1.r0), channel_id=1, source_target_pairs={{0,2},{2,4},{4,6},{6,0},{1,3},{3,5},{5,7},{7,1},{8,10},{10,12},{12... | collective-permute-start | bytes 196616 | tf_op jit(solution)/shard_map/ppermute | solution.py:31
  35.5 0.0 collective-permute-done.4.cvn
  35.5 0.5 collective-permute-start.5
  36.0 0.0 collective-permute-done.10.r2
  36.0 0.9 %collective-permute-done.11.r3 = bf16[256,128]{1,0:T(8,128)(2,1)S(1)} collective-permute-done((bf16[256,128]{1,0:T(8,128)(2,1)S(1)}, bf16[256,128]{1,0:T(8,128)(2,1)S(1)}, u32[]{:S(2)}, u32[]{:S(2)}) %collective-permute-start.11) | collective-permute-done | bytes 65568 | tf_op jit(solution)/shard_map/ppermute | solution.py:31
  36.9 1.0 %collective-permute-done.9.r1 = bf16[256,128]{1,0:T(8,128)(2,1)S(1)} collective-permute-done((bf16[256,128]{1,0:T(8,128)(2,1)S(1)}, bf16[256,128]{1,0:T(8,128)(2,1)S(1)}, u32[]{:S(2)}, u32[]{:S(2)}) %collective-permute-start.9) | collective-permute-done | bytes 65568 | tf_op jit(solution)/shard_map/ppermute | solution.py:31
  37.9 0.8 %collective-permute-start.12 = (bf16[512,128]{1,0:T(8,128)(2,1)S(1)}, bf16[512,128]{1,0:T(8,128)(2,1)S(1)}, u32[]{:S(2)}, u32[]{:S(2)}) collective-permute-start(bf16[512,128]{1,0:T(8,128)(2,1)S(1)} %select.6), channel_id=1, source_target_pairs={{0,0},{8,8},{16,16},{24,24},{40,32},{48,40},{56,48},{32,56},{80,64... | collective-permute-start | bytes 393224 | tf_op jit(solution)/shard_map/ppermute | solution.py:343
  38.7 0.0 copy-start.6
  38.7 0.6 copy-done.6
  39.4 7.1 %first.1 = (f32[1024,128]{1,0:T(8,128)S(1)}, f32[1024,128]{1,0:T(8,128)S(1)}, f32[1024,128]{1,0:T(8,128)S(1)}) custom-call(s32[1,4]{1,0:T(1,128)S(1)} %copy-done.6, s32[1]{0:T(128)} %copy.31.live, bf16[8,160,128]{2,1,0:T(8,128)(2,1)S(1)} %all-to-all-done.q3, bf16[2048,128]{1,0:T(8,128)(2,1)S(1)} %copy-done.1, bf16[2048,128]{1,0:T(8,128)(2,1)S(1)} %copy-done, ...), custom_call_target="tpu_custom_call" | custom-call | flops 2147483648 | bytes 1048576 | tf_op jit(solution)/shard_map/first/pallas_call | solution.py:325
  46.5 0.0 collective-permute-done.6.cvf
  46.5 0.0 collective-permute-done.12.new
  46.5 4.1 %second.1.payload = s16[8,144,128]{2,1,0:T(8,128)(2,1)} custom-call(bf16[8,160,128]{2,1,0:T(8,128)(2,1)S(1)} %all-to-all-done.q3, bf16[1024,128]{1,0:T(8,128)(2,1)S(1)} %collective-permute-done.2.ckn, bf16[1040,128]{1,0:T(8,128)(2,1)S(1)} %collective-permute-done.4.cvn, bf16[1024,128]{1,0:T(8,128)(2,1)S(1)} %collective-permute-done.5.ckf, ...), custom_call_target="tpu_custom_call" | custom-call | flops 268435456 | bytes 1048576 | tf_op jit(solution)/shard_map/second/pallas_call | solution.py:346
  50.6 4.2 %all-to-all-start.1 = ((s16[8,144,128]{2,1,0:T(8,128)(2,1)}), s16[8,144,128]{2,1,0:T(8,128)(2,1)S(1)}, u32[]{:S(2)}, u32[]{:S(2)}) async-start(s16[8,144,128]{2,1,0:T(8,128)(2,1)} %second.1.payload), calls=%async_computation.1 | async-start | bytes 589824 | tf_op jit(solution)/shard_map/all_to_all | solution.py:373
  54.8 0.2 reshape.52
  55.1 0.2 copy.25
  55.3 0.1 copy.24.code
  55.4 0.8 %route.1 = (bf16[256,128]{1,0:T(8,128)(2,1)S(1)}, bf16[256,128]{1,0:T(8,128)(2,1)S(1)}, bf16[256,128]{1,0:T(8,128)(2,1)S(1)}, bf16[256,128]{1,0:T(8,128)(2,1)S(1)}) custom-call(bf16[256,128]{1,0:T(8,128)(2,1)S(1)} %rows.1.r0, bf16[256,128]{1,0:T(8,128)(2,1)S(1)} %collective-permute-done.9.r1, bf16[256,128]{1,0:T(8,128)(2,1)S(1)} %collective-permute-done.10.r2, ...), custom_call_target="tpu_custom_call" | custom-call | tf_op jit(solution)/shard_map/route/pallas_call | solution.py:362
  56.1 1.1 %collective-permute-start.13 = (bf16[256,128]{1,0:T(8,128)(2,1)S(1)}, bf16[256,128]{1,0:T(8,128)(2,1)S(1)}, u32[]{:S(2)}, u32[]{:S(2)}) collective-permute-start(bf16[256,128]{1,0:T(8,128)(2,1)S(1)} %get-tuple-element.15), channel_id=1, source_target_pairs={{0,8},{8,16},{16,24},{24,0},{1,9},{9,17},{17,25},{25,1},{2,10},{10... | collective-permute-start | bytes 196616 | tf_op jit(solution)/shard_map/ppermute | solution.py:31
  57.2 2.2 %collective-permute-start.14 = (bf16[256,128]{1,0:T(8,128)(2,1)S(1)}, bf16[256,128]{1,0:T(8,128)(2,1)S(1)}, u32[]{:S(2)}, u32[]{:S(2)}) collective-permute-start(bf16[256,128]{1,0:T(8,128)(2,1)S(1)} %get-tuple-element.16), channel_id=1, source_target_pairs={{0,24},{8,0},{16,8},{24,16},{1,25},{9,1},{17,9},{25,17},{2,26},{10... | collective-permute-start | bytes 196616 | tf_op jit(solution)/shard_map/ppermute | solution.py:31
  59.4 0.8 %collective-permute-start.15 = (bf16[256,128]{1,0:T(8,128)(2,1)S(1)}, bf16[256,128]{1,0:T(8,128)(2,1)S(1)}, u32[]{:S(2)}, u32[]{:S(2)}) collective-permute-start(bf16[256,128]{1,0:T(8,128)(2,1)S(1)} %get-tuple-element.17), channel_id=1, source_target_pairs={{0,16},{8,24},{16,0},{24,8},{1,17},{9,25},{17,1},{25,9},{2,18},{10... | collective-permute-start | bytes 196616 | tf_op jit(solution)/shard_map/ppermute | solution.py:31
  60.2 1.4 %collective-permute-done.13.n1 = bf16[256,128]{1,0:T(8,128)(2,1)S(1)} collective-permute-done((bf16[256,128]{1,0:T(8,128)(2,1)S(1)}, bf16[256,128]{1,0:T(8,128)(2,1)S(1)}, u32[]{:S(2)}, u32[]{:S(2)}) %collective-permute-start.13) | collective-permute-done | bytes 65568 | tf_op jit(solution)/shard_map/ppermute | solution.py:31
  61.7 0.3 collective-permute-done.14.n2
  62.0 3.3 %collective-permute-done.15.n3 = bf16[256,128]{1,0:T(8,128)(2,1)S(1)} collective-permute-done((bf16[256,128]{1,0:T(8,128)(2,1)S(1)}, bf16[256,128]{1,0:T(8,128)(2,1)S(1)}, u32[]{:S(2)}, u32[]{:S(2)}) %collective-permute-start.15) | collective-permute-done | bytes 65568 | tf_op jit(solution)/shard_map/ppermute | solution.py:31
  65.2 1.7 %all-to-all-done.1.parts = s16[8,144,128]{2,1,0:T(8,128)(2,1)S(1)} async-done(((s16[8,144,128]{2,1,0:T(8,128)(2,1)}), s16[8,144,128]{2,1,0:T(8,128)(2,1)S(1)}, u32[]{:S(2)}, u32[]{:S(2)}) %all-to-all-start.1) | async-done | bytes 294944 | tf_op jit(solution)/shard_map/all_to_all | solution.py:373
  66.9 1.0 %merge.1 = (bf16[128,128]{1,0:T(8,128)(2,1)}, bf16[256,128]{1,0:T(8,128)(2,1)}) custom-call(s16[8,144,128]{2,1,0:T(8,128)(2,1)S(1)} %all-to-all-done.1.parts, bf16[256,128]{1,0:T(8,128)(2,1)S(1)} %get-tuple-element.14.n0, bf16[256,128]{1,0:T(8,128)(2,1)S(1)} %collective-permute-done.13.n1, bf16[256,128]{1,0:T(8,128)(2,1)S(1)} %collective-permute-done.14.n2, ...), custom_call_target="tpu_custom_call" | custom-call | tf_op jit(solution)/shard_map/merge/pallas_call | solution.py:374
  (26 shorter events, 0.2 us)
Async XLA Ops:
  3.0 3.4 %copy-start.5 = (bf16[8,2,128]{2,1,0:T(2,128)(2,1)S(1)}, bf16[8,2,128]{2,1,0:T(2,128)(2,1)}, u32[]{:S(2)}) copy-start(bf16[8,2,128]{2,1,0:T(2,128)(2,1)} %param.13) | copy-start | bytes 12292
  3.0 4.5 %copy-start.4 = (bf16[64,2,128]{2,1,0:T(2,128)(2,1)S(1)}, bf16[64,2,128]{2,1,0:T(2,128)(2,1)}, u32[]{:S(2)}) copy-start(bf16[64,2,128]{2,1,0:T(2,128)(2,1)} %param.8) | copy-start | bytes 98308
  3.1 15.1 %collective-permute-start.1 = (bf16[2064,128]{1,0:T(8,128)(2,1)S(1)}, bf16[2064,128]{1,0:T(8,128)(2,1)}, u32[]{:S(2)}, u32[]{:S(2)}) collective-permute-start(bf16[2064,128]{1,0:T(8,128)(2,1)S(1)} %fusion.1), channel_id=1, source_target_pairs={{0,8},{8,16},{16,24},{24,0},{1,9},{9,17},{17,25},{25,1},{2,10},{10... | collective-permute-start | bytes 1585160 | tf_op jit(solution)/shard_map/ppermute | solution.py:31
  4.6 13.6 %collective-permute-start.3 = (bf16[2064,128]{1,0:T(8,128)(2,1)S(1)}, bf16[2064,128]{1,0:T(8,128)(2,1)S(1)}, u32[]{:S(2)}, u32[]{:S(2)}) collective-permute-start(bf16[2064,128]{1,0:T(8,128)(2,1)S(1)} %fusion.1), channel_id=1, source_target_pairs={{0,24},{8,0},{16,8},{24,16},{1,25},{9,1},{17,9},{25,17},{2,26},{10... | collective-permute-start | bytes 1585160 | tf_op jit(solution)/shard_map/ppermute | solution.py:31
  6.4 1.2 %collective-permute-start = (bf16[16,128]{1,0:T(8,128)(2,1)S(1)}, bf16[16,128]{1,0:T(8,128)(2,1)S(1)}, u32[]{:S(2)}, u32[]{:S(2)}) collective-permute-start(bf16[16,128]{1,0:T(8,128)(2,1)S(1)} %bitcast.24), channel_id=1, source_target_pairs={{0,1},{1,0},{2,3},{3,2},{4,5},{5,4},{6,7},{7,6},{8,9},{9,8},{10,11... | collective-permute-start | bytes 12296 | tf_op jit(solution)/shard_map/ppermute | solution.py:36
  8.3 22.1 %all-to-all-start = ((bf16[8,160,128]{2,1,0:T(8,128)(2,1)}), bf16[8,160,128]{2,1,0:T(8,128)(2,1)S(1)}, u32[]{:S(2)}, u32[]{:S(2)}) async-start(bf16[8,160,128]{2,1,0:T(8,128)(2,1)} %gather.1), calls=%async_computation | async-start | bytes 655360 | tf_op jit(solution)/shard_map/all_to_all | solution.py:311
  16.8 13.6 %copy-start = (bf16[2048,128]{1,0:T(8,128)(2,1)S(1)}, bf16[2048,128]{1,0:T(8,128)(2,1)}, u32[]{:S(2)}) copy-start(bf16[2048,128]{1,0:T(8,128)(2,1)} %ov.3) | copy-start | bytes 1572868
  16.8 13.6 %copy-start.1 = (bf16[2048,128]{1,0:T(8,128)(2,1)S(1)}, bf16[2048,128]{1,0:T(8,128)(2,1)}, u32[]{:S(2)}) copy-start(bf16[2048,128]{1,0:T(8,128)(2,1)} %ok.3) | copy-start | bytes 1572868
  18.2 12.2 %collective-permute-start.7 = (bf16[2064,128]{1,0:T(8,128)(2,1)}, bf16[2064,128]{1,0:T(8,128)(2,1)S(1)}, u32[]{:S(2)}, u32[]{:S(2)}) collective-permute-start(bf16[2064,128]{1,0:T(8,128)(2,1)} %collective-permute-done.1.an), channel_id=1, source_target_pairs={{0,1},{1,0},{2,3},{3,2},{4,5},{5,4},{6,7},{7,6},{8,9},{9,8},{10,11... | collective-permute-start | bytes 1585160 | tf_op jit(solution)/shard_map/ppermute | solution.py:36
  18.2 5.3 %copy-start.2 = (bf16[2064,128]{1,0:T(8,128)(2,1)}, bf16[2064,128]{1,0:T(8,128)(2,1)S(1)}, u32[]{:S(2)}) copy-start(bf16[2064,128]{1,0:T(8,128)(2,1)S(1)} %collective-permute-done.3.bn) | copy-start | bytes 1585156
  18.2 12.2 %collective-permute-start.8 = (bf16[2064,128]{1,0:T(8,128)(2,1)S(1)}, bf16[2064,128]{1,0:T(8,128)(2,1)S(1)}, u32[]{:S(2)}, u32[]{:S(2)}) collective-permute-start(bf16[2064,128]{1,0:T(8,128)(2,1)S(1)} %collective-permute-done.3.bn), channel_id=1, source_target_pairs={{0,1},{1,0},{2,3},{3,2},{4,5},{5,4},{6,7},{7,6},{8,9},{9,8},{10,11... | collective-permute-start | bytes 1585160 | tf_op jit(solution)/shard_map/ppermute | solution.py:36
  19.5 16.0 %collective-permute-start.4 = (bf16[1040,128]{1,0:T(8,128)(2,1)}, bf16[1040,128]{1,0:T(8,128)(2,1)S(1)}, u32[]{:S(2)}, u32[]{:S(2)}) collective-permute-start(bf16[1040,128]{1,0:T(8,128)(2,1)} %slice.9), channel_id=1, source_target_pairs={{0,24},{8,0},{16,8},{24,16},{1,25},{9,1},{17,9},{25,17},{2,26},{10... | collective-permute-start | bytes 798728 | tf_op jit(solution)/shard_map/ppermute | solution.py:31
  23.5 12.0 %collective-permute-start.2 = (bf16[1024,128]{1,0:T(8,128)(2,1)}, bf16[1024,128]{1,0:T(8,128)(2,1)S(1)}, u32[]{:S(2)}, u32[]{:S(2)}) collective-permute-start(bf16[1024,128]{1,0:T(8,128)(2,1)} %slice.8), channel_id=1, source_target_pairs={{0,8},{8,16},{16,24},{24,0},{1,9},{9,17},{17,25},{25,1},{2,10},{10... | collective-permute-start | bytes 786440 | tf_op jit(solution)/shard_map/ppermute | solution.py:31
  30.4 8.3 %copy-start.3 = (bf16[2064,128]{1,0:T(8,128)(2,1)S(1)}, bf16[2064,128]{1,0:T(8,128)(2,1)}, u32[]{:S(2)}) copy-start(bf16[2064,128]{1,0:T(8,128)(2,1)} %copy-done.2) | copy-start | bytes 1585156
  30.5 5.5 %collective-permute-start.10 = (bf16[256,128]{1,0:T(8,128)(2,1)S(1)}, bf16[256,128]{1,0:T(8,128)(2,1)S(1)}, u32[]{:S(2)}, u32[]{:S(2)}) collective-permute-start(bf16[256,128]{1,0:T(8,128)(2,1)S(1)} %rows.1.r0), channel_id=1, source_target_pairs={{0,6},{2,0},{4,2},{6,4},{1,7},{3,1},{5,3},{7,5},{8,14},{10,8},{12,... | collective-permute-start | bytes 196616 | tf_op jit(solution)/shard_map/ppermute | solution.py:31
  31.0 5.9 %collective-permute-start.11 = (bf16[256,128]{1,0:T(8,128)(2,1)S(1)}, bf16[256,128]{1,0:T(8,128)(2,1)S(1)}, u32[]{:S(2)}, u32[]{:S(2)}) collective-permute-start(bf16[256,128]{1,0:T(8,128)(2,1)S(1)} %rows.1.r0), channel_id=1, source_target_pairs={{0,4},{2,6},{4,0},{6,2},{1,5},{3,7},{5,1},{7,3},{8,12},{10,14},{12... | collective-permute-start | bytes 196616 | tf_op jit(solution)/shard_map/ppermute | solution.py:31
  33.6 4.3 %collective-permute-start.9 = (bf16[256,128]{1,0:T(8,128)(2,1)S(1)}, bf16[256,128]{1,0:T(8,128)(2,1)S(1)}, u32[]{:S(2)}, u32[]{:S(2)}) collective-permute-start(bf16[256,128]{1,0:T(8,128)(2,1)S(1)} %rows.1.r0), channel_id=1, source_target_pairs={{0,2},{2,4},{4,6},{6,0},{1,3},{3,5},{5,7},{7,1},{8,10},{10,12},{12... | collective-permute-start | bytes 196616 | tf_op jit(solution)/shard_map/ppermute | solution.py:31
  35.5 11.0 %collective-permute-start.6 = (bf16[1040,128]{1,0:T(8,128)(2,1)S(1)}, bf16[1040,128]{1,0:T(8,128)(2,1)S(1)}, u32[]{:S(2)}, u32[]{:S(2)}) collective-permute-start(bf16[1040,128]{1,0:T(8,128)(2,1)S(1)} %collective-permute-done.4.cvn), channel_id=1, source_target_pairs={{0,1},{1,0},{2,3},{3,2},{4,5},{5,4},{6,7},{7,6},{8,9},{9,8},{10,11... | collective-permute-start | bytes 798728 | tf_op jit(solution)/shard_map/ppermute | solution.py:36
  35.5 11.0 %collective-permute-start.5 = (bf16[1024,128]{1,0:T(8,128)(2,1)S(1)}, bf16[1024,128]{1,0:T(8,128)(2,1)S(1)}, u32[]{:S(2)}, u32[]{:S(2)}) collective-permute-start(bf16[1024,128]{1,0:T(8,128)(2,1)S(1)} %collective-permute-done.2.ckn), channel_id=1, source_target_pairs={{0,1},{1,0},{2,3},{3,2},{4,5},{5,4},{6,7},{7,6},{8,9},{9,8},{10,11... | collective-permute-start | bytes 786440 | tf_op jit(solution)/shard_map/ppermute | solution.py:36
  37.9 8.6 %collective-permute-start.12 = (bf16[512,128]{1,0:T(8,128)(2,1)S(1)}, bf16[512,128]{1,0:T(8,128)(2,1)S(1)}, u32[]{:S(2)}, u32[]{:S(2)}) collective-permute-start(bf16[512,128]{1,0:T(8,128)(2,1)S(1)} %select.6), channel_id=1, source_target_pairs={{0,0},{8,8},{16,16},{24,24},{40,32},{48,40},{56,48},{32,56},{80,64... | collective-permute-start | bytes 393224 | tf_op jit(solution)/shard_map/ppermute | solution.py:343
  38.7 0.7 copy-start.6
  50.6 4.2 %copy-start.7 = (s32[2048]{0:T(1024)S(1)}, s32[2048]{0:T(1024)}, u32[]{:S(2)}) copy-start(s32[2048]{0:T(1024)} %param.15) | copy-start | bytes 24580
  50.6 4.2 %copy-start.8 = (s32[2048]{0:T(1024)S(1)}, s32[2048]{0:T(1024)}, u32[]{:S(2)}) copy-start(s32[2048]{0:T(1024)} %param.14) | copy-start | bytes 24580
  50.6 16.4 %all-to-all-start.1 = ((s16[8,144,128]{2,1,0:T(8,128)(2,1)}), s16[8,144,128]{2,1,0:T(8,128)(2,1)S(1)}, u32[]{:S(2)}, u32[]{:S(2)}) async-start(s16[8,144,128]{2,1,0:T(8,128)(2,1)} %second.1.payload), calls=%async_computation.1 | async-start | bytes 589824 | tf_op jit(solution)/shard_map/all_to_all | solution.py:373
  56.1 5.6 %collective-permute-start.13 = (bf16[256,128]{1,0:T(8,128)(2,1)S(1)}, bf16[256,128]{1,0:T(8,128)(2,1)S(1)}, u32[]{:S(2)}, u32[]{:S(2)}) collective-permute-start(bf16[256,128]{1,0:T(8,128)(2,1)S(1)} %get-tuple-element.15), channel_id=1, source_target_pairs={{0,8},{8,16},{16,24},{24,0},{1,9},{9,17},{17,25},{25,1},{2,10},{10... | collective-permute-start | bytes 196616 | tf_op jit(solution)/shard_map/ppermute | solution.py:31
  57.2 4.7 %collective-permute-start.14 = (bf16[256,128]{1,0:T(8,128)(2,1)S(1)}, bf16[256,128]{1,0:T(8,128)(2,1)S(1)}, u32[]{:S(2)}, u32[]{:S(2)}) collective-permute-start(bf16[256,128]{1,0:T(8,128)(2,1)S(1)} %get-tuple-element.16), channel_id=1, source_target_pairs={{0,24},{8,0},{16,8},{24,16},{1,25},{9,1},{17,9},{25,17},{2,26},{10... | collective-permute-start | bytes 196616 | tf_op jit(solution)/shard_map/ppermute | solution.py:31
  59.4 5.8 %collective-permute-start.15 = (bf16[256,128]{1,0:T(8,128)(2,1)S(1)}, bf16[256,128]{1,0:T(8,128)(2,1)S(1)}, u32[]{:S(2)}, u32[]{:S(2)}) collective-permute-start(bf16[256,128]{1,0:T(8,128)(2,1)S(1)} %get-tuple-element.17), channel_id=1, source_target_pairs={{0,16},{8,24},{16,0},{24,8},{1,17},{9,25},{17,1},{25,9},{2,18},{10... | collective-permute-start | bytes 196616 | tf_op jit(solution)/shard_map/ppermute | solution.py:31
